TPU v7x, 512 devices: a whole 4x8x8 slice. The times are simulated.
512 devices in a mesh: seq: 128 (over z, y, core), tp: 4 (over x).
Axes of the slice: x: 4, y: 8, z: 8, core: 2. Of those that a mesh axis runs over, the one named last changes fastest.
Arguments:
- query_in: bfloat16 [16384, 1024], P('seq', 'tp'), may hold values from -6 to 6
- key_in: bfloat16 [16384, 1024], P('seq', 'tp'), may hold values from -6 to 6
- value_in: bfloat16 [16384, 1024], P('seq', 'tp'), may hold values from -6 to 6
- short_weight: float32 [3, 7, 1024], P(None, None, 'tp'), may hold values from -2 to 2
- residue: float32 [16, 1024], P(None, 'tp'), may hold values from -1.5 to 1.5
- rate: float32 [16, 1024], P(None, 'tp'), may hold values from 1e-05 to 0.05
- skip: float32 [1024], P('tp'), may hold values from -4 to 4
- out_weight: bfloat16 [1024, 4096], P('tp'), may hold values from -0.1875 to 0.1875
Outputs:
- mixed: bfloat16 [16384, 4096], P('seq', 'tp')
All inputs are finite; a program needn't handle non-finite values.
Results may differ from a plain program's by a relative error of at most 0.0049.
Values may be sent and summed in bfloat16 or wider, within the bound.
No kernel may reach another device: no remote copies, remote signals or barrier semaphores. Data moves between devices by JAX's collectives and lax.ppermute only.
A program may use at most 64 MiB of HBM per device.

v0:
```python
import math

import jax
import jax.numpy as jnp
from jax import lax
from jax.sharding import PartitionSpec as P


def passed_along(block, axis, distance):
    devices = range(lax.axis_size(axis))
    route = [(i - distance, i) for i in devices if i - distance in devices]
    return lax.ppermute(block, axis, route)


def short_conv(signal, border, weights):
    taps = weights.shape[0]
    rows_here = signal.shape[0]
    padded = jnp.concatenate([border.astype(jnp.float32), signal.astype(jnp.float32)], axis=0)
    total = jnp.zeros((rows_here, signal.shape[1]), jnp.float32)
    for offset in range(taps):
        total = total + weights[offset] * padded[taps - 1 - offset : taps - 1 - offset + rows_here]
    return total


def modal_spectrum(angles, parity, rate_rows, residue_rows, length):
    half_sine = 2.0 * jnp.sin(0.5 * angles) ** 2
    full_sine = jnp.sin(angles)
    shape_out = (angles + parity + rate_rows[0]).shape
    spec_real = jnp.zeros(shape_out, jnp.float32)
    spec_imag = jnp.zeros(shape_out, jnp.float32)
    for order_index in range(rate_rows.shape[0]):
        decay = rate_rows[order_index]
        retain = jnp.exp(-decay)
        amplitude = residue_rows[order_index] * jnp.sqrt(-jnp.expm1(-2.0 * decay))
        leftover = jnp.exp(-decay * length)
        numerator = amplitude * (1.0 - leftover * parity)
        below_real = -jnp.expm1(-decay) + retain * half_sine
        below_imag = retain * full_sine
        below_norm = below_real * below_real + below_imag * below_imag
        spec_real = spec_real + numerator * below_real / below_norm
        spec_imag = spec_imag - numerator * below_imag / below_norm
    return (spec_real, spec_imag)


def local(query_in, key_in, value_in, short_weight, residue, rate, skip, out_weight):
    rows_dev, channels = query_in.shape
    shards = lax.axis_size("seq")
    own_index = lax.axis_index("seq")
    cols_dev = rows_dev // shards
    length = shards * rows_dev
    period = 2 * length
    precise = lax.Precision.HIGHEST
    taps = short_weight.shape[1]
    rims = passed_along(
        (
            query_in[rows_dev - taps + 1 :],
            key_in[rows_dev - taps + 1 :],
            value_in[rows_dev - taps + 1 :],
        ),
        "seq",
        1,
    )
    queries = short_conv(query_in, rims[0], short_weight[0])
    keys = short_conv(key_in, rims[1], short_weight[1])
    values = short_conv(value_in, rims[2], short_weight[2])
    gated = keys * values
    indices = jnp.arange(rows_dev, dtype=jnp.int32)
    inner_phase = (
        2.0
        * math.pi
        / rows_dev
        * (indices[:, None] * indices[None, :] % rows_dev).astype(jnp.float32)
    )
    dft_cos = jnp.cos(inner_phase)
    dft_sin = jnp.sin(inner_phase)
    columns = lax.all_to_all(
        gated.reshape(shards, cols_dev, channels), "seq", split_axis=0, concat_axis=0, tiled=True
    )
    spectral = jnp.arange(2 * shards, dtype=jnp.int32)
    sources = jnp.arange(shards, dtype=jnp.int32)
    outer_phase = (
        2.0
        * math.pi
        / (2 * shards)
        * (spectral[:, None] * sources[None, :] % (2 * shards)).astype(jnp.float32)
    )
    z_real = jnp.einsum("ap,psc->asc", jnp.cos(outer_phase), columns, precision=precise)
    z_imag = -jnp.einsum("ap,psc->asc", jnp.sin(outer_phase), columns, precision=precise)
    held_cols = own_index * cols_dev + jnp.arange(cols_dev, dtype=jnp.int32)
    twist = (
        2.0
        * math.pi
        / period
        * (spectral[:, None] * held_cols[None, :] % period).astype(jnp.float32)
    )[:, :, None]
    twist_cos = jnp.cos(twist)
    twist_sin = jnp.sin(twist)
    turned_real = z_real * twist_cos + z_imag * twist_sin
    turned_imag = z_imag * twist_cos - z_real * twist_sin
    moved_real, moved_imag = (
        lax.all_to_all(
            turned_real.reshape(shards, 2, cols_dev, channels),
            "seq",
            split_axis=0,
            concat_axis=2,
            tiled=True,
        ),
        lax.all_to_all(
            turned_imag.reshape(shards, 2, cols_dev, channels),
            "seq",
            split_axis=0,
            concat_axis=2,
            tiled=True,
        ),
    )
    moved_real = moved_real.reshape(2, rows_dev, channels)
    moved_imag = moved_imag.reshape(2, rows_dev, channels)
    x_real = jnp.einsum("bj,tjc->tbc", dft_cos, moved_real, precision=precise) + jnp.einsum(
        "bj,tjc->tbc", dft_sin, moved_imag, precision=precise
    )
    x_imag = jnp.einsum("bj,tjc->tbc", dft_cos, moved_imag, precision=precise) - jnp.einsum(
        "bj,tjc->tbc", dft_sin, moved_real, precision=precise
    )
    held_freq = 2 * own_index + jnp.arange(2, dtype=jnp.int32)
    frequency = held_freq[:, None] + 2 * shards * indices[None, :]
    angles = (2.0 * math.pi / period * frequency.astype(jnp.float32))[:, :, None]
    parity = (1 - 2 * (held_freq % 2)).astype(jnp.float32)[:, None, None]
    spec_real, spec_imag = modal_spectrum(angles, parity, rate, residue, length)
    y_real = x_real * spec_real - x_imag * spec_imag
    y_imag = x_real * spec_imag + x_imag * spec_real
    g_real = jnp.einsum("bj,tbc->tjc", dft_cos, y_real, precision=precise) - jnp.einsum(
        "bj,tbc->tjc", dft_sin, y_imag, precision=precise
    )
    g_imag = jnp.einsum("bj,tbc->tjc", dft_cos, y_imag, precision=precise) + jnp.einsum(
        "bj,tbc->tjc", dft_sin, y_real, precision=precise
    )
    back_phase = (
        2.0
        * math.pi
        / period
        * (held_freq[:, None] * indices[None, :] % period).astype(jnp.float32)
    )[:, :, None]
    back_cos = jnp.cos(back_phase)
    back_sin = jnp.sin(back_phase)
    w_real = g_real * back_cos - g_imag * back_sin
    w_imag = g_imag * back_cos + g_real * back_sin
    w_real, w_imag = (
        lax.all_to_all(
            w_real.reshape(2, shards, cols_dev, channels),
            "seq",
            split_axis=1,
            concat_axis=0,
            tiled=True,
        ),
        lax.all_to_all(
            w_imag.reshape(2, shards, cols_dev, channels),
            "seq",
            split_axis=1,
            concat_axis=0,
            tiled=True,
        ),
    )
    w_real = w_real.reshape(2 * shards, cols_dev, channels)
    w_imag = w_imag.reshape(2 * shards, cols_dev, channels)
    out_rows = jnp.arange(2 * shards, dtype=jnp.int32)
    row_phase = (
        2.0
        * math.pi
        / (2 * shards)
        * (out_rows[:, None] * spectral[None, :] % (2 * shards)).astype(jnp.float32)
    )
    row_cos = jnp.cos(row_phase)
    row_sin = jnp.sin(row_phase)
    out_real = jnp.einsum("pa,asc->psc", row_cos, w_real, precision=precise) - jnp.einsum(
        "pa,asc->psc", row_sin, w_imag, precision=precise
    )
    out_imag = jnp.einsum("pa,asc->psc", row_cos, w_imag, precision=precise) + jnp.einsum(
        "pa,asc->psc", row_sin, w_real, precision=precise
    )
    recv_real, recv_imag = (
        lax.all_to_all(
            out_real.reshape(2, shards, cols_dev, channels),
            "seq",
            split_axis=1,
            concat_axis=2,
            tiled=True,
        ),
        lax.all_to_all(
            out_imag.reshape(2, shards, cols_dev, channels),
            "seq",
            split_axis=1,
            concat_axis=2,
            tiled=True,
        ),
    )
    longconv = recv_real[0, 0] / period
    hyena = (queries * (longconv + skip * gated)).astype(jnp.bfloat16)
    partial_out = jnp.dot(hyena, out_weight, preferred_element_type=jnp.float32)
    return lax.psum_scatter(partial_out, "tp", scatter_dimension=1, tiled=True).astype(jnp.bfloat16)


def solution(mesh):
    in_specs = (
        P("seq", "tp"),
        P("seq", "tp"),
        P("seq", "tp"),
        P(None, None, "tp"),
        P(None, "tp"),
        P(None, "tp"),
        P("tp"),
        P("tp", None),
    )
    out_specs = P("seq", "tp")
    return jax.shard_map(local, mesh=mesh, in_specs=in_specs, out_specs=out_specs, check_vma=False)
```

profile of v0, /device:TPU:1, one launch (start us, length us, event | category | flops | bytes accessed | tf_op | source)
XLA Modules:
  0.0 211.0 jit_solution(12294745965370006640)
XLA Ops:
  7.4 4.6 %collective-permute-start.2 = (bf16[6,256]{1,0:T(8,128)(2,1)S(1)}, bf16[6,256]{1,0:T(8,128)(2,1)S(1)}, u32[]{:S(2)}, u32[]{:S(2)}) collective-permute-start(bf16[6,256]{1,0:T(8,128)(2,1)S(1)} %slice.302), channel_id=1, source_target_pairs={{0,4},{4,8},{8,12},{12,16},{16,20},{20,24},{24,28},{28,32},{32,36}... | collective-permute-start | bytes 9224 | tf_op jit(solution)/shard_map/ppermute | solution.py:12
  12.7 1.9 collective-permute-start.1
  17.2 1.0 multiply_exponential_fusion.15
  18.3 1.1 sqrt_multiply_fusion.15
  22.1 16.5 %all-to-all-start = ((f32[128,1,256]{2,1,0:T(1,128)}), f32[128,1,256]{2,1,0:T(1,128)S(1)}, u32[]{:S(2)}, u32[]{:S(2)}) async-start(f32[128,1,256]{2,1,0:T(1,128)} %reshape.1693), calls=%async_computation | async-start | bytes 262144 | tf_op jit(solution)/shard_map/all_to_all | solution.py:76
  39.7 11.7 %all-to-all-done = f32[128,1,256]{2,1,0:T(1,128)S(1)} async-done(((f32[128,1,256]{2,1,0:T(1,128)}), f32[128,1,256]{2,1,0:T(1,128)S(1)}, u32[]{:S(2)}, u32[]{:S(2)}) %all-to-all-start) | async-done | bytes 131104 | tf_op jit(solution)/shard_map/all_to_all | solution.py:76
  54.0 5.6 %all-to-all-start.1 = ((f32[128,2,1,256]{3,1,2,0:T(2,128)}), f32[128,2,1,256]{3,1,2,0:T(2,128)S(1)}, u32[]{:S(2)}, u32[]{:S(2)}) async-start(f32[128,2,1,256]{3,1,2,0:T(2,128)} %bitcast.21), calls=%async_computation.1 | async-start | bytes 524288 | tf_op jit(solution)/shard_map/all_to_all | solution.py:101
  61.4 13.5 %all-to-all-done.1 = f32[128,2,1,256]{3,1,2,0:T(2,128)S(1)} async-done(((f32[128,2,1,256]{3,1,2,0:T(2,128)}), f32[128,2,1,256]{3,1,2,0:T(2,128)S(1)}, u32[]{:S(2)}, u32[]{:S(2)}) %all-to-all-start.1) | async-done | bytes 262176 | tf_op jit(solution)/shard_map/all_to_all | solution.py:101
  74.9 5.5 %all-to-all-start.2 = ((f32[128,2,1,256]{3,1,2,0:T(2,128)}), f32[128,2,1,256]{3,1,2,0:T(2,128)S(1)}, u32[]{:S(2)}, u32[]{:S(2)}) async-start(f32[128,2,1,256]{3,1,2,0:T(2,128)} %bitcast.26), calls=%async_computation.2 | async-start | bytes 524288 | tf_op jit(solution)/shard_map/all_to_all | solution.py:108
  81.4 14.4 %all-to-all-done.2 = f32[128,2,1,256]{3,1,2,0:T(2,128)S(1)} async-done(((f32[128,2,1,256]{3,1,2,0:T(2,128)}), f32[128,2,1,256]{3,1,2,0:T(2,128)S(1)}, u32[]{:S(2)}, u32[]{:S(2)}) %all-to-all-start.2) | async-done | bytes 262176 | tf_op jit(solution)/shard_map/all_to_all | solution.py:108
  97.2 2.6 %multiply_subtract_fusion = (f32[2,128,256]{1,2,0:T(8,128)S(1)}, f32[2,128,256]{1,2,0:T(8,128)S(1)}) fusion(f32[2,128,256]{1,2,0:T(8,128)S(1)} %fusion.1, f32[256]{0:T(256)S(1)} %bitcast.183, f32[256]{0:T(256)S(1)} %bitcast.259, f32[2,256]{1,0:T(2,128)S(1)} %get-tuple-element.113, f32[256]{0:T(256)S(1)} %bitcast.187, f32[256]{0:T(256)S(1)} %bitcast.185, ...), kind=kOutput, calls=%fused_computation.119 | convolution fusion | flops 113672192 | bytes 1378304 | tf_op jit(solution)/shard_map/bj,tjc->tbc/dot_general | solution.py:121
  99.8 2.5 %multiply_add_fusion = f32[2,128,256]{1,2,0:T(8,128)S(1)} fusion(f32[2,128,256]{1,2,0:T(8,128)S(1)} %get-tuple-element.115, f32[2,128,256]{1,2,0:T(8,128)S(1)} %fusion.1, f32[256]{0:T(256)S(1)} %bitcast.184, f32[256]{0:T(256)S(1)} %bitcast.260, f32[2,256]{1,0:T(2,128)S(1)} %get-tuple-element.113, f32[256]{0:T(256)S(1)} %bitcast.188, f32[256]{0:T(256)S(1)} %bitcast.186, ...), kind=kLoop, calls=%fused_computation.118 | loop fusion | flops 12713984 | bytes 854016 | tf_op jit(solution)/shard_map/add | solution.py:130
  105.6 5.5 %all-to-all-start.4 = ((f32[2,128,1,256]{3,0,2,1:T(2,128)}), f32[2,128,1,256]{3,0,2,1:T(2,128)S(1)}, u32[]{:S(2)}, u32[]{:S(2)}) async-start(f32[2,128,1,256]{3,0,2,1:T(2,128)} %copy.22), calls=%async_computation.4 | async-start | bytes 524288 | tf_op jit(solution)/shard_map/all_to_all | solution.py:155
  112.0 14.5 %all-to-all-done.4 = f32[2,128,1,256]{3,0,2,1:T(2,128)S(1)} async-done(((f32[2,128,1,256]{3,0,2,1:T(2,128)}), f32[2,128,1,256]{3,0,2,1:T(2,128)S(1)}, u32[]{:S(2)}, u32[]{:S(2)}) %all-to-all-start.4) | async-done | bytes 262176 | tf_op jit(solution)/shard_map/all_to_all | solution.py:155
  126.5 5.8 %all-to-all-start.3 = ((f32[2,128,1,256]{3,0,2,1:T(2,128)}), f32[2,128,1,256]{3,0,2,1:T(2,128)S(1)}, u32[]{:S(2)}, u32[]{:S(2)}) async-start(f32[2,128,1,256]{3,0,2,1:T(2,128)} %copy.21), calls=%async_computation.3 | async-start | bytes 524288 | tf_op jit(solution)/shard_map/all_to_all | solution.py:148
  132.5 15.2 %all-to-all-done.3 = f32[2,128,1,256]{3,0,2,1:T(2,128)S(1)} async-done(((f32[2,128,1,256]{3,0,2,1:T(2,128)}), f32[2,128,1,256]{3,0,2,1:T(2,128)S(1)}, u32[]{:S(2)}, u32[]{:S(2)}) %all-to-all-start.3) | async-done | bytes 262176 | tf_op jit(solution)/shard_map/all_to_all | solution.py:148
  147.8 1.6 fusion.60
  149.5 1.6 convolution_subtract_fusion
  152.1 5.5 %all-to-all-start.5 = ((f32[2,128,1,256]{3,2,0,1:T(1,128)}), f32[2,128,1,256]{3,2,0,1:T(1,128)S(1)}, u32[]{:S(2)}, u32[]{:S(2)}) async-start(f32[2,128,1,256]{3,2,0,1:T(1,128)} %copy.23), calls=%async_computation.5 | async-start | bytes 524288 | tf_op jit(solution)/shard_map/all_to_all | solution.py:181
  157.7 3.5 %collective-permute-start = (bf16[6,256]{1,0:T(8,128)(2,1)S(1)}, bf16[6,256]{1,0:T(8,128)(2,1)S(1)}, u32[]{:S(2)}, u32[]{:S(2)}) collective-permute-start(bf16[6,256]{1,0:T(8,128)(2,1)S(1)} %slice.274), channel_id=1, source_target_pairs={{0,4},{4,8},{8,12},{12,16},{16,20},{20,24},{24,28},{28,32},{32,36}... | collective-permute-start | bytes 9224 | tf_op jit(solution)/shard_map/ppermute | solution.py:12
  162.0 11.1 %all-to-all-done.5 = f32[2,128,1,256]{3,2,0,1:T(1,128)S(1)} async-done(((f32[2,128,1,256]{3,2,0,1:T(1,128)}), f32[2,128,1,256]{3,2,0,1:T(1,128)S(1)}, u32[]{:S(2)}, u32[]{:S(2)}) %all-to-all-start.5) | async-done | bytes 262176 | tf_op jit(solution)/shard_map/all_to_all | solution.py:181
  173.1 1.9 fusion.139
  175.1 27.3 %reduce-scatter.2.cloned.1.call-done = f32[128,1024]{1,0:T(8,128)} async-done(((f32[128,4096]{1,0:T(8,128)}), f32[128,1024]{1,0:T(8,128)}) %reduce-scatter.2.cloned.1.call-update) | async-done | bytes 524304 | tf_op jit(solution)/shard_map/reduce_scatter | solution.py:199
  202.4 1.8 convert_element_type.106
  (54 shorter events, 21.0 us)
Async XLA Ops:
  6.5 166.6 %copy-start = (bf16[256,4096]{1,0:T(8,128)(2,1)S(1)}, bf16[256,4096]{1,0:T(8,128)(2,1)}, u32[]{:S(2)}) copy-start(bf16[256,4096]{1,0:T(8,128)(2,1)} %param.15) | copy-start | bytes 6291460
  7.4 13.7 %collective-permute-start.2 = (bf16[6,256]{1,0:T(8,128)(2,1)S(1)}, bf16[6,256]{1,0:T(8,128)(2,1)S(1)}, u32[]{:S(2)}, u32[]{:S(2)}) collective-permute-start(bf16[6,256]{1,0:T(8,128)(2,1)S(1)} %slice.302), channel_id=1, source_target_pairs={{0,4},{4,8},{8,12},{12,16},{16,20},{20,24},{24,28},{28,32},{32,36}... | collective-permute-start | bytes 9224 | tf_op jit(solution)/shard_map/ppermute | solution.py:12
  12.7 8.5 %collective-permute-start.1 = (bf16[6,256]{1,0:T(8,128)(2,1)S(1)}, bf16[6,256]{1,0:T(8,128)(2,1)S(1)}, u32[]{:S(2)}, u32[]{:S(2)}) collective-permute-start(bf16[6,256]{1,0:T(8,128)(2,1)S(1)} %slice.288), channel_id=1, source_target_pairs={{0,4},{4,8},{8,12},{12,16},{16,20},{20,24},{24,28},{28,32},{32,36}... | collective-permute-start | bytes 9224 | tf_op jit(solution)/shard_map/ppermute | solution.py:12
  15.4 44.2 %copy-start.1 = (f32[16,256]{1,0:T(8,128)S(1)}, f32[16,256]{1,0:T(8,128)}, u32[]{:S(2)}) copy-start(f32[16,256]{1,0:T(8,128)} %param.13) | copy-start | bytes 49156
  22.1 29.3 %all-to-all-start = ((f32[128,1,256]{2,1,0:T(1,128)}), f32[128,1,256]{2,1,0:T(1,128)S(1)}, u32[]{:S(2)}, u32[]{:S(2)}) async-start(f32[128,1,256]{2,1,0:T(1,128)} %reshape.1693), calls=%async_computation | async-start | bytes 262144 | tf_op jit(solution)/shard_map/all_to_all | solution.py:76
  54.0 20.9 %all-to-all-start.1 = ((f32[128,2,1,256]{3,1,2,0:T(2,128)}), f32[128,2,1,256]{3,1,2,0:T(2,128)S(1)}, u32[]{:S(2)}, u32[]{:S(2)}) async-start(f32[128,2,1,256]{3,1,2,0:T(2,128)} %bitcast.21), calls=%async_computation.1 | async-start | bytes 524288 | tf_op jit(solution)/shard_map/all_to_all | solution.py:101
  74.9 20.9 %all-to-all-start.2 = ((f32[128,2,1,256]{3,1,2,0:T(2,128)}), f32[128,2,1,256]{3,1,2,0:T(2,128)S(1)}, u32[]{:S(2)}, u32[]{:S(2)}) async-start(f32[128,2,1,256]{3,1,2,0:T(2,128)} %bitcast.26), calls=%async_computation.2 | async-start | bytes 524288 | tf_op jit(solution)/shard_map/all_to_all | solution.py:108
  105.6 20.9 %all-to-all-start.4 = ((f32[2,128,1,256]{3,0,2,1:T(2,128)}), f32[2,128,1,256]{3,0,2,1:T(2,128)S(1)}, u32[]{:S(2)}, u32[]{:S(2)}) async-start(f32[2,128,1,256]{3,0,2,1:T(2,128)} %copy.22), calls=%async_computation.4 | async-start | bytes 524288 | tf_op jit(solution)/shard_map/all_to_all | solution.py:155
  126.5 21.1 %all-to-all-start.3 = ((f32[2,128,1,256]{3,0,2,1:T(2,128)}), f32[2,128,1,256]{3,0,2,1:T(2,128)S(1)}, u32[]{:S(2)}, u32[]{:S(2)}) async-start(f32[2,128,1,256]{3,0,2,1:T(2,128)} %copy.21), calls=%async_computation.3 | async-start | bytes 524288 | tf_op jit(solution)/shard_map/all_to_all | solution.py:148
  132.3 25.4 %copy-start.2 = (bf16[128,256]{1,0:T(8,128)(2,1)S(1)}, bf16[128,256]{1,0:T(8,128)(2,1)}, u32[]{:S(2)}) copy-start(bf16[128,256]{1,0:T(8,128)(2,1)} %param.8) | copy-start | bytes 196612
  147.7 25.5 %copy-start.3 = (f32[256]{0:T(256)S(1)}, f32[256]{0:T(256)}, u32[]{:S(2)}) copy-start(f32[256]{0:T(256)} %param.14) | copy-start | bytes 3076
  152.1 21.0 %all-to-all-start.5 = ((f32[2,128,1,256]{3,2,0,1:T(1,128)}), f32[2,128,1,256]{3,2,0,1:T(1,128)S(1)}, u32[]{:S(2)}, u32[]{:S(2)}) async-start(f32[2,128,1,256]{3,2,0,1:T(1,128)} %copy.23), calls=%async_computation.5 | async-start | bytes 524288 | tf_op jit(solution)/shard_map/all_to_all | solution.py:181
  157.6 44.8 %reduce-scatter.2.cloned.1.call-start = ((), (), s32[]{:S(2)}) async-start(), calls=%async_computation.7 | async-start | bytes 2621440 | tf_op jit(solution)/shard_map/reduce_scatter | solution.py:199
  157.7 4.3 %collective-permute-start = (bf16[6,256]{1,0:T(8,128)(2,1)S(1)}, bf16[6,256]{1,0:T(8,128)(2,1)S(1)}, u32[]{:S(2)}, u32[]{:S(2)}) collective-permute-start(bf16[6,256]{1,0:T(8,128)(2,1)S(1)} %slice.274), channel_id=1, source_target_pairs={{0,4},{4,8},{8,12},{12,16},{16,20},{20,24},{24,28},{28,32},{32,36}... | collective-permute-start | bytes 9224 | tf_op jit(solution)/shard_map/ppermute | solution.py:12
Sparse Core Ops, SparseCore 0:
  175.2 27.1 reduce-scatter.1
where the time goes:
time: 212 us; the launch traced here: 211 us
  waiting for transfers between devices  108 us (51%)
  starting transfers between devices  54.5 us (26%)
  matrix products  13.8 us (7%)
  between operations  13.8 us (7%)
  other arithmetic  11.5 us (5%)
  local copies, waits for them, and re-layouts  9.06 us (4%)
    reduce_scatter x1, waiting for transfers between devices, local(): lax.psum_scatter(partial_out, 'tp', scatter_dimension=1, tiled=True)  27.3 us
    all_to_all x1, starting transfers between devices, local(): lax.all_to_all(gated.reshape(shards, cols_dev, channels), 'seq', split_ax...  16.5 us
    all_to_all x1, waiting for transfers between devices, local(): lax.all_to_all(w_real.reshape(2, shards, cols_dev, channels), 'seq', spli...  15.2 us
    all_to_all x1, waiting for transfers between devices, local(): lax.all_to_all(w_imag.reshape(2, shards, cols_dev, channels), 'seq', spli...  14.5 us
    all_to_all x1, waiting for transfers between devices, local(): lax.all_to_all(turned_imag.reshape(shards, 2, cols_dev, channels), 'seq',...  14.4 us
    all_to_all x1, waiting for transfers between devices, local(): lax.all_to_all(turned_real.reshape(shards, 2, cols_dev, channels), 'seq',...  13.5 us
    all_to_all x1, waiting for transfers between devices, local(): lax.all_to_all(gated.reshape(shards, cols_dev, channels), 'seq', split_ax...  11.7 us
    all_to_all x1, waiting for transfers between devices, local(): lax.all_to_all(out_real.reshape(2, shards, cols_dev, channels), 'seq', sp...  11.1 us
  transfers between devices with their start and end apart: 10, of which 8 were waited for; matrix products, arithmetic and copies ran while one was open for 6% of the time, Pallas kernels for 0%

commit v1 on v0

v1 whole, which is shorter than its diff:
```python
import math

import jax
import jax.numpy as jnp
from jax import lax
from jax.experimental import pallas as pl
from jax.experimental.pallas import tpu as pltpu
from jax.sharding import Mesh, PartitionSpec as P

F32 = jnp.float32
BF16 = jnp.bfloat16
LANES = 128
SUBS = 8
RIM = 16


def shape(dims, dtype):
    return jax.ShapeDtypeStruct(dims, dtype)


def call(body, outs, scratch=(), flops=0, name=None):
    return pl.pallas_call(
        body,
        out_shape=outs,
        scratch_shapes=list(scratch),
        name=name,
    )


def row_of(ref, m, lanes):
    return ref[pl.ds(m, 1), lanes]


def wide(row):
    return jnp.broadcast_to(row, (SUBS, LANES))


def gate_body(q_ref, k_ref, v_ref, rim_ref, taps_ref, rate_ref, query_ref, gated_ref, begin_ref, state_ref, pad, held):
    rows, channels = q_ref.shape
    modes = rate_ref.shape[0]
    taps = taps_ref.shape[1]
    steps = rows // SUBS
    for i, ref in enumerate((q_ref, k_ref, v_ref)):
        pad[i, pl.ds(0, RIM), :] = rim_ref[pl.ds(i * RIM, RIM), :].astype(F32)
        pad[i, pl.ds(RIM, rows), :] = ref[...].astype(F32)
    block = 32
    for half in range(channels // LANES):
        lanes = pl.ds(half * LANES, LANES)
        for r in range(0, rows, block):
            sums = []
            for i in range(3):
                total = jnp.zeros((block, LANES), F32)
                for t in range(taps):
                    total = total + taps_ref[i, pl.ds(t, 1), lanes] * pad[i, pl.ds(RIM + r - t, block), lanes]
                sums.append(total)
            query_ref[half, pl.ds(r, block), :] = sums[0]
            gated_ref[half, pl.ds(r, block), :] = sums[1] * sums[2]
    sub = lax.broadcasted_iota(jnp.int32, (SUBS, LANES), 0)
    for half in range(channels // LANES):
        lanes = pl.ds(half * LANES, LANES)
        rates = [row_of(rate_ref, m, lanes) for m in range(modes)]
        retain = [wide(jnp.exp(-x)) for x in rates]
        state = [jnp.zeros((SUBS, LANES), F32) for _ in range(modes)]
        for step in range(steps):
            g = gated_ref[half, pl.ds(step, SUBS, stride=steps), :]
            state = [a * s + g for a, s in zip(retain, state)]
        for m in range(modes):
            s = state[m]
            for d in (1, 2, 4):
                drop = wide(jnp.exp(-(steps * d) * rates[m]))
                s = s + jnp.where(sub >= d, drop * pltpu.roll(s, d, 0), 0.0)
            held[pl.ds(m, 1), lanes] = s[SUBS - 1 :]
            begin_ref[m, :, lanes] = jnp.where(sub >= 1, pltpu.roll(s, 1, 0), 0.0)
    whole = held[...]
    for i in range(state_ref.shape[0]):
        state_ref[i] = whole


def plane_body(own, rows, parts_ref, rate_ref, before_ref, total_ref):
    me = lax.axis_index(own[0]) * 2 + lax.axis_index(own[1])
    drop = jnp.exp(-rows * rate_ref[...])
    before = jnp.zeros(rate_ref.shape, F32)
    total = jnp.zeros(rate_ref.shape, F32)
    for i in range(parts_ref.shape[0]):
        part = parts_ref[i]
        before = jnp.where(i < me, before * drop + part, before)
        total = total * drop + part
    before_ref[...] = before
    for i in range(total_ref.shape[0]):
        total_ref[i] = total


def mix_body(own, rows_plane, query_ref, gated_ref, begin_ref, before_ref, planes_ref, rate_ref, amp_ref, skip_ref, weight_ref, out_ref, hyena, carry):
    halves, rows, _ = query_ref.shape
    modes = rate_ref.shape[0]
    steps = rows // SUBS
    z = lax.axis_index(own[0])
    me = lax.axis_index(own[1]) * 2 + lax.axis_index(own[2])
    drop = jnp.exp(-rows_plane * rate_ref[...])
    behind = jnp.zeros(rate_ref.shape, F32)
    for i in range(planes_ref.shape[0]):
        behind = jnp.where(i < z, behind * drop + planes_ref[i], behind)
    carry[...] = before_ref[...] + jnp.exp(-(rows * me).astype(F32) * rate_ref[...]) * behind
    sub = lax.broadcasted_iota(jnp.int32, (SUBS, LANES), 0).astype(F32)
    for half in range(halves):
        lanes = pl.ds(half * LANES, LANES)
        rates = [row_of(rate_ref, m, lanes) for m in range(modes)]
        retain = [wide(jnp.exp(-x)) for x in rates]
        amp = [wide(row_of(amp_ref, m, lanes)) for m in range(modes)]
        skip = wide(row_of(skip_ref, 0, lanes))
        state = [
            begin_ref[m, :, lanes] + jnp.exp(-(steps * sub) * rates[m]) * row_of(carry, m, lanes)
            for m in range(modes)
        ]
        for step in range(steps):
            at = pl.ds(step, SUBS, stride=steps)
            g = gated_ref[half, at, :]
            state = [a * s + g for a, s in zip(retain, state)]
            terms = [a * s for a, s in zip(amp, state)] + [skip * g]
            while len(terms) > 1:
                terms = [x + y for x, y in zip(terms[::2], terms[1::2])] + terms[len(terms) // 2 * 2 :]
            hyena[half, at, :] = query_ref[half, at, :] * terms[0]
    left = jnp.concatenate([hyena[half].astype(BF16) for half in range(halves)], axis=1)
    width = out_ref.shape[2]
    block = 512
    for i in range(out_ref.shape[0]):
        for c in range(0, width, block):
            out_ref[i, :, pl.ds(c, block)] = jnp.dot(
                left, weight_ref[:, pl.ds(i * width + c, block)], preferred_element_type=F32
            ).astype(BF16)


def sum_body(parts_ref, out_ref):
    total = parts_ref[0].astype(F32)
    for i in range(1, parts_ref.shape[0]):
        total = total + parts_ref[i].astype(F32)
    out_ref[...] = total.astype(BF16)


def local(query_in, key_in, value_in, short_weight, residue, rate, skip, out_weight):
    rows, channels = query_in.shape
    modes = rate.shape[0]
    planes = lax.axis_size("z")
    plane = lax.axis_size("y") * lax.axis_size("core")
    parts = lax.axis_size("tp")
    width = out_weight.shape[1] // parts
    order = ("z", "y", "core")
    devices = planes * plane
    rims = jnp.concatenate([x[rows - RIM :] for x in (query_in, key_in, value_in)], axis=0)
    rims = lax.ppermute(rims, order, [(i, i + 1) for i in range(devices - 1)])
    amplitude = residue * jnp.sqrt(-jnp.expm1(-2.0 * rate))
    queries, gated, begin, states = call(
        gate_body,
        (
            shape((channels // LANES, rows, LANES), F32),
            shape((channels // LANES, rows, LANES), F32),
            shape((modes, SUBS, channels), F32),
            shape((plane, modes, channels), F32),
        ),
        (pltpu.VMEM((3, RIM + rows, channels), F32), pltpu.VMEM((modes, channels), F32)),
        name="gate",
    )(query_in, key_in, value_in, rims, short_weight, rate)
    states = lax.all_to_all(states, ("y", "core"), 0, 0, tiled=True)
    before, totals = call(
        lambda *refs: plane_body(("y", "core"), rows, *refs),
        (shape((modes, channels), F32), shape((planes, modes, channels), F32)),
        name="plane",
    )(states, rate)
    totals = lax.all_to_all(totals, "z", 0, 0, tiled=True)
    partial = call(
        lambda *refs: mix_body(order, rows * plane, *refs),
        shape((parts, rows, width), BF16),
        (pltpu.VMEM((channels // LANES, rows, LANES), F32), pltpu.VMEM((modes, channels), F32)),
        name="mix",
    )(queries, gated, begin, before, totals, rate, amplitude, skip.reshape(1, -1), out_weight)
    partial = lax.all_to_all(partial, "tp", 0, 0, tiled=True)
    return call(sum_body, shape((rows, width), BF16), name="total")(partial)


def solution(mesh):
    fine = Mesh(mesh.devices.reshape(8, 8, 2, 4), ("z", "y", "core", "tp"))
    seq = ("z", "y", "core")
    in_specs = (
        P(seq, "tp"),
        P(seq, "tp"),
        P(seq, "tp"),
        P(None, None, "tp"),
        P(None, "tp"),
        P(None, "tp"),
        P("tp"),
        P("tp", None),
    )
    return jax.shard_map(local, mesh=fine, in_specs=in_specs, out_specs=P(seq, "tp"), check_vma=False)
```

time: 212 us -> 79.4 us (0.37)
  waiting for transfers between devices: 108 us -> 12.5 us
  starting transfers between devices: 54.5 us -> 14.6 us
  blocking collectives: 0 us -> 36.9 us
  matrix products: 13.8 us -> 0 us
  between operations: 13.8 us -> 0.02 us
  other arithmetic: 11.5 us -> 1.36 us
  Pallas kernels: 0 us -> 9.81 us
  local copies, waits for them, and re-layouts: 9.06 us -> 3.36 us
    all_to_all x6 -> x1, waiting for transfers between devices: 80.4 us -> 8.24 us  [local(): totals = lax.all_to_all(totals, 'z', 0, 0, tiled=True)]
    all_to_all x0 -> x2, blocking collectives: none -> 36.9 us  [the longest x1 19 us: local(): partial = lax.all_to_all(partial, 'tp', 0, 0, tiled=True)]
    all_to_all x6 -> x1, starting transfers between devices: 44.4 us -> 10 us  [local(): totals = lax.all_to_all(totals, 'z', 0, 0, tiled=True)]
    reduce_scatter x1 -> x0, waiting for transfers between devices: 27.3 us -> none  [local(): lax.psum_scatter(partial_out, 'tp', scatter_dimension=1, tiled=True)]
    dot_general x13 -> x0, matrix products: 13.8 us -> none  [the longest x1 2.62 us: local(): jnp.einsum('bj,tjc->tbc', dft_sin, moved_real, precision=precise)]
    pallas_call x0 -> x4, Pallas kernels: none -> 9.81 us  [the longest x1 3.77 us: local(): call(lambda *refs: mix_body(order, rows * plane, *refs), shape((parts, ro...]
    ppermute x3 -> x1, starting transfers between devices: 10 us -> 4.58 us  [local(): rims = lax.ppermute(rims, order, [(i, i + 1) for i in range(devices - 1)])]
    reshape x6 -> x0, local copies, waits for them, and re-layouts: 5.07 us -> none  [the longest x1 0.97 us: local(): out_real.reshape(2, shards, cols_dev, channels)]
  transfers between devices with their start and end apart: 10 -> 2, of which waited for: 8 -> 2; matrix products, arithmetic and copies ran while one was open for 6% -> 2% of each run, Pallas kernels for 0% -> 0%
where the time goes in v1:
time: 79.4 us; the launch traced here: 78.6 us
  blocking collectives  36.9 us (46%)
  starting transfers between devices  14.6 us (18%)
  waiting for transfers between devices  12.5 us (16%)
  Pallas kernels  9.81 us (12%)
  local copies, waits for them, and re-layouts  3.36 us (4%)
  other arithmetic  1.36 us (2%)
    all_to_all x1, blocking collectives, local(): partial = lax.all_to_all(partial, 'tp', 0, 0, tiled=True)  19 us
    all_to_all x1, blocking collectives, local(): states = lax.all_to_all(states, ('y', 'core'), 0, 0, tiled=True)  17.9 us
    all_to_all x1, starting transfers between devices, local(): totals = lax.all_to_all(totals, 'z', 0, 0, tiled=True)  10 us
    all_to_all x1, waiting for transfers between devices, local(): totals = lax.all_to_all(totals, 'z', 0, 0, tiled=True)  8.24 us
    ppermute x1, starting transfers between devices, local(): rims = lax.ppermute(rims, order, [(i, i + 1) for i in range(devices - 1)])  4.58 us
    ppermute x1, waiting for transfers between devices, local(): rims = lax.ppermute(rims, order, [(i, i + 1) for i in range(devices - 1)])  4.24 us
    pallas_call x1, Pallas kernels, local(): call(lambda *refs: mix_body(order, rows * plane, *refs), shape((parts, ro...  3.77 us
    pallas_call x1, Pallas kernels, local(): call(gate_body, (shape((channels // LANES, rows, LANES), F32), shape((cha...  2.32 us
  transfers between devices with their start and end apart: 2, of which 2 were waited for; matrix products, arithmetic and copies ran while one was open for 2% of the time, Pallas kernels for 0%

profile of v1, /device:TPU:1, one launch (start us, length us, event | category | flops | bytes accessed | tf_op | source)
XLA Modules:
  0.0 78.6 jit_solution(11089736878895489582)
XLA Ops:
  0.0 0.7 slice.9
  0.7 0.7 slice.10
  1.4 0.7 slice.11
  2.1 4.6 %collective-permute-start = (bf16[48,256]{1,0:T(8,128)(2,1)S(1)}, bf16[48,256]{1,0:T(8,128)(2,1)S(1)}, u32[]{:S(2)}, u32[]{:S(2)}) collective-permute-start(bf16[48,256]{1,0:T(8,128)(2,1)S(1)} %pad_maximum_fusion), channel_id=1, source_target_pairs={{0,4},{4,8},{8,12},{12,16},{16,20},{20,24},{24,28},{28,32},{32,36}... | collective-permute-start | bytes 73736 | tf_op jit(solution)/shard_map/ppermute | solution.py:150
  6.7 4.2 %collective-permute-done.rim_ref = bf16[48,256]{1,0:T(8,128)(2,1)S(1)} collective-permute-done((bf16[48,256]{1,0:T(8,128)(2,1)S(1)}, bf16[48,256]{1,0:T(8,128)(2,1)S(1)}, u32[]{:S(2)}, u32[]{:S(2)}) %collective-permute-start) | collective-permute-done | bytes 24608 | tf_op jit(solution)/shard_map/ppermute | solution.py:150
  10.9 0.0 copy-start.1
  10.9 0.6 copy-done.1
  11.5 2.3 %gate.1 = (f32[2,128,128]{2,1,0:T(8,128)}, f32[2,128,128]{2,1,0:T(8,128)}, f32[16,8,256]{2,1,0:T(8,128)}, f32[16,16,256]{2,1,0:T(8,128)}) custom-call(bf16[128,256]{1,0:T(8,128)(2,1)} %q_ref.1, bf16[128,256]{1,0:T(8,128)(2,1)} %k_ref.1, bf16[128,256]{1,0:T(8,128)(2,1)} %v_ref.1, bf16[48,256]{1,0:T(8,128)(2,1)} %copy-done.1, f32[3,7,256]{2,1,0:T(8,128)} %taps_ref.1, ...), custom_call_target="tpu_custom_call" | custom-call | tf_op jit(solution)/shard_map/gate/pallas_call | solution.py:152
  13.9 17.9 %all_to_all.15.refs_0_ = f32[16,16,256]{2,1,0:T(8,128)} all-to-all(f32[16,16,256]{2,1,0:T(8,128)} %get-tuple-element.14), channel_id=1, replica_groups=mesh['z'=8,'y'=8,'core'=2,'tp'=4] {'y','core'}, dimensions={0} | all-to-all | bytes 524288 | tf_op jit(solution)/shard_map/all_to_all | solution.py:163
  31.8 1.7 %plane.1 = (f32[16,256]{1,0:T(8,128)}, f32[8,16,256]{2,1,0:T(8,128)}) custom-call(f32[16,16,256]{2,1,0:T(8,128)} %all_to_all.15.refs_0_, f32[16,256]{1,0:T(8,128)} %refs_5_.1), custom_call_target="tpu_custom_call" | custom-call | tf_op jit(solution)/shard_map/plane/pallas_call | solution.py:164
  33.5 10.0 %all-to-all-start.1 = ((f32[8,16,256]{2,1,0:T(8,128)}), f32[8,16,256]{2,1,0:T(8,128)S(1)}, u32[]{:S(2)}, u32[]{:S(2)}) async-start(f32[8,16,256]{2,1,0:T(8,128)} %get-tuple-element.16), calls=%async_computation.1 | async-start | bytes 262144 | tf_op jit(solution)/shard_map/all_to_all | solution.py:169
  43.5 1.4 %sqrt_multiply_fusion.refs_6_ = f32[16,256]{1,0:T(8,128)} fusion(f32[16,256]{1,0:T(8,128)} %param.12, f32[16,256]{1,0:T(8,128)} %refs_5_.1), kind=kLoop, calls=%fused_computation.1 | loop fusion | flops 12288 | bytes 49152 | tf_op jit(solution)/shard_map/mul | solution.py:151
  44.9 8.2 %all-to-all-done.1.refs_4_ = f32[8,16,256]{2,1,0:T(8,128)S(1)} async-done(((f32[8,16,256]{2,1,0:T(8,128)}), f32[8,16,256]{2,1,0:T(8,128)S(1)}, u32[]{:S(2)}, u32[]{:S(2)}) %all-to-all-start.1) | async-done | bytes 131104 | tf_op jit(solution)/shard_map/all_to_all | solution.py:169
  53.1 0.0 copy-start
  53.1 0.7 copy-done
  53.8 3.8 %mix.1 = bf16[4,128,1024]{2,1,0:T(8,128)(2,1)} custom-call(f32[2,128,128]{2,1,0:T(8,128)} %get-tuple-element.11.refs_0_, f32[2,128,128]{2,1,0:T(8,128)} %get-tuple-element.12.refs_1_, f32[16,8,256]{2,1,0:T(8,128)} %get-tuple-element.13.refs_2_, f32[16,256]{1,0:T(8,128)} %get-tuple-element.15.refs_3_, f32[8,16,256]{2,1,0:T(8,128)} %copy-done, ...), custom_call_target="tpu_custom_call" | custom-call | tf_op jit(solution)/shard_map/mix/pallas_call | solution.py:170
  57.5 19.0 %all_to_all.16.parts_ref = bf16[4,128,1024]{2,1,0:T(8,128)(2,1)} all-to-all(bf16[4,128,1024]{2,1,0:T(8,128)(2,1)} %mix.1), channel_id=1, replica_groups=mesh['z'=8,'y'=8,'core'=2,'tp'=4] {'tp'}, dimensions={0} | all-to-all | bytes 2097152 | tf_op jit(solution)/shard_map/all_to_all | solution.py:176
  76.5 2.1 %total.1 = bf16[128,1024]{1,0:T(8,128)(2,1)} custom-call(bf16[4,128,1024]{2,1,0:T(8,128)(2,1)} %all_to_all.16.parts_ref), custom_call_target="tpu_custom_call" | custom-call | tf_op jit(solution)/shard_map/total/pallas_call | solution.py:177
  (1 shorter events, 0.0 us)
Async XLA Ops:
  2.1 8.8 %collective-permute-start = (bf16[48,256]{1,0:T(8,128)(2,1)S(1)}, bf16[48,256]{1,0:T(8,128)(2,1)S(1)}, u32[]{:S(2)}, u32[]{:S(2)}) collective-permute-start(bf16[48,256]{1,0:T(8,128)(2,1)S(1)} %pad_maximum_fusion), channel_id=1, source_target_pairs={{0,4},{4,8},{8,12},{12,16},{16,20},{20,24},{24,28},{28,32},{32,36}... | collective-permute-start | bytes 73736 | tf_op jit(solution)/shard_map/ppermute | solution.py:150
  10.9 0.6 copy-start.1
  33.5 19.6 %all-to-all-start.1 = ((f32[8,16,256]{2,1,0:T(8,128)}), f32[8,16,256]{2,1,0:T(8,128)S(1)}, u32[]{:S(2)}, u32[]{:S(2)}) async-start(f32[8,16,256]{2,1,0:T(8,128)} %get-tuple-element.16), calls=%async_computation.1 | async-start | bytes 262144 | tf_op jit(solution)/shard_map/all_to_all | solution.py:169
  53.1 0.7 copy-start

commit v2 on v1

v2 whole, which is shorter than its diff:
```python
import jax
import jax.numpy as jnp
from jax import lax
from jax.experimental import pallas as pl
from jax.experimental.pallas import tpu as pltpu
from jax.sharding import Mesh, PartitionSpec as P

F32 = jnp.float32
BF16 = jnp.bfloat16
LANES = 128
SUBS = 8
RIM = 16
HEAD = 8
MIB = 1 << 20


def shape(dims, dtype):
    return jax.ShapeDtypeStruct(dims, dtype)


VMEM = pl.BlockSpec(memory_space=pltpu.VMEM)
HBM = pl.BlockSpec(memory_space=pltpu.HBM)


def call(body, specs, outs, name, scratch=(), mib=4):
    return pl.pallas_call(
        body,
        in_specs=specs,
        out_specs=jax.tree.map(lambda _: VMEM, outs),
        out_shape=outs,
        scratch_shapes=list(scratch),
        compiler_params=pltpu.CompilerParams(vmem_limit_bytes=mib * MIB),
        name=name,
    )


def fetch(sources, targets, sems):
    copies = [pltpu.make_async_copy(s, t, sems.at[i]) for i, (s, t) in enumerate(zip(sources, targets))]
    for copy in copies:
        copy.start()
    return copies


def row_of(ref, m, lanes):
    return ref[pl.ds(m, 1), lanes]


def wide(row):
    return jnp.broadcast_to(row, (SUBS, LANES))


def one_minus_exp(x):
    series = 1.0 / 362880.0
    for n in (40320, 5040, 720, 120, 24, 6, 2, 1):
        series = 1.0 / n - x * series
    return jnp.where(x < 0.25, x * series, 1.0 - jnp.exp(-x))


def rim_body(q_ref, k_ref, v_ref, out_ref, sems):
    rows = q_ref.shape[0]
    refs = (q_ref, k_ref, v_ref)
    copies = fetch(
        [ref.at[pl.ds(rows - RIM, RIM), :] for ref in refs],
        [out_ref.at[pl.ds(i * RIM, RIM), :] for i in range(3)],
        sems,
    )
    for copy in copies:
        copy.wait()


def gate_body(
    q_hbm, k_hbm, v_hbm, taps_hbm, rate_hbm, residue_hbm,
    query_ref, gated_ref, begin_ref, state_ref, head_ref, taps_ref, rate_ref, amp_ref,
    streams, residue_ref, pad, sems,
):
    _, rows, channels = streams.shape
    modes = rate_ref.shape[0]
    taps = taps_ref.shape[1]
    steps = rows // SUBS
    copies = fetch(
        (q_hbm, k_hbm, v_hbm, taps_hbm, rate_hbm, residue_hbm),
        (streams.at[0], streams.at[1], streams.at[2], taps_ref, rate_ref, residue_ref),
        sems,
    )
    for copy in copies:
        copy.wait()
    amp_ref[...] = residue_ref[...] * jnp.sqrt(one_minus_exp(2.0 * rate_ref[...]))
    for i in range(3):
        pad[i, pl.ds(0, HEAD), :] = jnp.zeros((HEAD, channels), F32)
        pad[i, pl.ds(HEAD, rows), :] = streams[i].astype(F32)
    block = 32
    for half in range(channels // LANES):
        lanes = pl.ds(half * LANES, LANES)
        for r in range(0, rows, block):
            sums = []
            for i in range(3):
                total = jnp.zeros((block, LANES), F32)
                for t in range(taps):
                    total = total + taps_ref[i, pl.ds(t, 1), lanes] * pad[i, pl.ds(HEAD + r - t, block), lanes]
                sums.append(total)
                if r == 0:
                    head_ref[i, :, lanes] = total[:HEAD]
            query_ref[half, pl.ds(r, block), :] = sums[0]
            gated_ref[half, pl.ds(r, block), :] = sums[1] * sums[2]
    sub = lax.broadcasted_iota(jnp.int32, (SUBS, LANES), 0)
    for half in range(channels // LANES):
        lanes = pl.ds(half * LANES, LANES)
        rates = [row_of(rate_ref, m, lanes) for m in range(modes)]
        retain = [wide(jnp.exp(-x)) for x in rates]
        state = [jnp.zeros((SUBS, LANES), F32) for _ in range(modes)]
        for step in range(steps):
            g = gated_ref[half, pl.ds(step, SUBS, stride=steps), :]
            state = [a * s + g for a, s in zip(retain, state)]
        for m in range(modes):
            s = state[m]
            for d in (1, 2, 4):
                drop = wide(jnp.exp(-(steps * d) * rates[m]))
                s = s + jnp.where(sub >= d, drop * pltpu.roll(s, d, 0), 0.0)
            state_ref[pl.ds(m, 1), lanes] = s[SUBS - 1 :]
            begin_ref[m, :, lanes] = jnp.where(sub >= 1, pltpu.roll(s, 1, 0), 0.0)


def join_body(rows, rim_ref, head_ref, taps_ref, rate_ref, state_ref, out_ref, late_ref, top_ref, pad):
    modes, channels = rate_ref.shape
    taps = taps_ref.shape[1]
    sums = []
    for i in range(3):
        pad[i, pl.ds(0, HEAD), :] = rim_ref[pl.ds(i * RIM, RIM), :].astype(F32)[RIM - HEAD :]
        pad[i, pl.ds(HEAD, HEAD), :] = jnp.zeros((HEAD, channels), F32)
        total = head_ref[i]
        for t in range(1, taps):
            total = total + taps_ref[i, pl.ds(t, 1), :] * pad[i, pl.ds(HEAD - t, HEAD), :]
        sums.append(total)
    gated = sums[1] * sums[2]
    top_ref[0] = sums[0]
    top_ref[1] = gated
    more = gated - head_ref[1] * head_ref[2]
    rate = rate_ref[...]
    retain = jnp.exp(-rate)
    late = jnp.broadcast_to(more[:1], rate.shape)
    for i in range(1, taps - 1):
        late = retain * late + more[i : i + 1]
    late_ref[...] = late
    whole = state_ref[...] + jnp.exp(-(rows - taps + 1) * rate) * late
    for i in range(out_ref.shape[0]):
        out_ref[i] = whole


def plane_body(rows, parts_ref, rate_ref, before_ref, total_ref):
    me = lax.axis_index("y") * lax.axis_size("core") + lax.axis_index("core")
    drop = jnp.exp(-rows * rate_ref[...])
    before = jnp.zeros(rate_ref.shape, F32)
    total = jnp.zeros(rate_ref.shape, F32)
    for i in range(parts_ref.shape[0]):
        part = parts_ref[i]
        before = jnp.where(i < me, before * drop + part, before)
        total = total * drop + part
    before_ref[...] = before
    for i in range(total_ref.shape[0]):
        total_ref[i] = total


def mix_body(
    taps, plane_rows, query_ref, gated_ref, begin_ref, late_ref, top_ref, before_ref, planes_ref, rate_ref, amp_ref,
    skip_hbm, weight_hbm, out_ref, hyena, carry, skip_ref, weight, sems,
):
    halves, rows, _ = query_ref.shape
    modes = rate_ref.shape[0]
    steps = rows // SUBS
    parts, _, width = out_ref.shape
    copies = fetch(
        [skip_hbm] + [weight_hbm.at[:, pl.ds(i * width, width)] for i in range(parts)],
        [skip_ref] + [weight.at[i] for i in range(parts)],
        sems,
    )
    z = lax.axis_index("z")
    me = lax.axis_index("y") * lax.axis_size("core") + lax.axis_index("core")
    rate = rate_ref[...]
    drop = jnp.exp(-plane_rows * rate)
    behind = jnp.zeros(rate.shape, F32)
    for i in range(planes_ref.shape[0]):
        behind = jnp.where(i < z, behind * drop + planes_ref[i], behind)
    carried = before_ref[...] + jnp.exp(-(rows * me).astype(F32) * rate) * behind
    carry[0] = carried
    carry[1] = carried + jnp.exp((taps - 1) * rate) * late_ref[...]
    sub = lax.broadcasted_iota(jnp.int32, (SUBS, LANES), 0)
    ahead = sub.astype(F32) * float(steps)
    copies[0].wait()
    for half in range(halves):
        lanes = pl.ds(half * LANES, LANES)
        rates = [row_of(rate_ref, m, lanes) for m in range(modes)]
        retain = [wide(jnp.exp(-x)) for x in rates]
        amp = [wide(row_of(amp_ref, m, lanes)) for m in range(modes)]
        skip = wide(row_of(skip_ref, 0, lanes))
        state = [
            begin_ref[m, :, lanes]
            + jnp.exp(-ahead * rates[m])
            * jnp.where(sub >= 1, row_of(carry.at[1], m, lanes), row_of(carry.at[0], m, lanes))
            for m in range(modes)
        ]
        for step in range(steps):
            at = pl.ds(step, SUBS, stride=steps)
            g = gated_ref[half, at, :]
            query = query_ref[half, at, :]
            if step < taps - 1:
                query = jnp.where(sub >= 1, query, top_ref[0, pl.ds(step, 1), lanes])
                g = jnp.where(sub >= 1, g, top_ref[1, pl.ds(step, 1), lanes])
            state = [a * s + g for a, s in zip(retain, state)]
            terms = [a * s for a, s in zip(amp, state)] + [skip * g]
            while len(terms) > 1:
                terms = [x + y for x, y in zip(terms[::2], terms[1::2])] + terms[len(terms) // 2 * 2 :]
            hyena[half, at, :] = query * terms[0]
    left = jnp.concatenate([hyena[half].astype(BF16) for half in range(halves)], axis=1)
    block = 512
    for i in range(parts):
        copies[1 + i].wait()
        for c in range(0, width, block):
            out_ref[i, :, pl.ds(c, block)] = jnp.dot(
                left, weight[i, :, pl.ds(c, block)], preferred_element_type=F32
            ).astype(BF16)


def sum_body(parts_ref, out_ref):
    total = parts_ref[0].astype(F32)
    for i in range(1, parts_ref.shape[0]):
        total = total + parts_ref[i].astype(F32)
    out_ref[...] = total.astype(BF16)


def local(query_in, key_in, value_in, short_weight, residue, rate, skip, out_weight):
    rows, channels = query_in.shape
    modes = rate.shape[0]
    taps = short_weight.shape[1]
    planes = lax.axis_size("z")
    plane = lax.axis_size("y") * lax.axis_size("core")
    parts = lax.axis_size("tp")
    width = out_weight.shape[1] // parts
    order = ("z", "y", "core")
    devices = planes * plane
    by_half = (channels // LANES, rows, LANES)
    skip = skip.reshape(1, -1)
    query_in, key_in, value_in, short_weight, residue, rate, skip, out_weight = (
        pltpu.with_memory_space_constraint(x, pltpu.HBM)
        for x in (query_in, key_in, value_in, short_weight, residue, rate, skip, out_weight)
    )
    rims = call(
        rim_body, [HBM] * 3, shape((3 * RIM, channels), BF16), "rims", [pltpu.SemaphoreType.DMA((3,))]
    )(query_in, key_in, value_in)
    rims = lax.ppermute(rims, order, [(i, i + 1) for i in range(devices - 1)])
    queries, gated, begin, states, heads, taps_here, rate, amplitude = call(
        gate_body,
        [HBM] * 6,
        (
            shape(by_half, F32),
            shape(by_half, F32),
            shape((modes, SUBS, channels), F32),
            shape((modes, channels), F32),
            shape((3, HEAD, channels), F32),
            shape(short_weight.shape, F32),
            shape((modes, channels), F32),
            shape((modes, channels), F32),
        ),
        "gate",
        [
            pltpu.VMEM((3, rows, channels), BF16),
            pltpu.VMEM((modes, channels), F32),
            pltpu.VMEM((3, HEAD + rows, channels), F32),
            pltpu.SemaphoreType.DMA((6,)),
        ],
    )(query_in, key_in, value_in, short_weight, rate, residue)
    states, late, top = call(
        lambda *refs: join_body(rows, *refs),
        [VMEM] * 5,
        (
            shape((plane, modes, channels), F32),
            shape((modes, channels), F32),
            shape((2, HEAD, channels), F32),
        ),
        "join",
        [pltpu.VMEM((3, 2 * HEAD, channels), F32)],
    )(rims, heads, taps_here, rate, states)
    states = lax.all_to_all(states, ("y", "core"), 0, 0, tiled=True)
    before, totals = call(
        lambda *refs: plane_body(rows, *refs),
        [VMEM] * 2,
        (shape((modes, channels), F32), shape((planes, modes, channels), F32)),
        "plane",
    )(states, rate)
    totals = lax.all_to_all(totals, "z", 0, 0, tiled=True)
    partial = call(
        lambda *refs: mix_body(taps, rows * plane, *refs),
        [VMEM] * 9 + [HBM] * 2,
        shape((parts, rows, width), BF16),
        "mix",
        [
            pltpu.VMEM(by_half, F32),
            pltpu.VMEM((2, modes, channels), F32),
            pltpu.VMEM((1, channels), F32),
            pltpu.VMEM((parts, channels, width), BF16),
            pltpu.SemaphoreType.DMA((1 + parts,)),
        ],
        8,
    )(queries, gated, begin, late, top, before, totals, rate, amplitude, skip, out_weight)
    partial = lax.all_to_all(partial, "tp", 0, 0, tiled=True)
    return call(sum_body, [VMEM], shape((rows, width), BF16), "total")(partial)


def solution(mesh):
    fine = Mesh(mesh.devices.reshape(8, 8, 2, 4), ("z", "y", "core", "tp"))
    seq = ("z", "y", "core")
    in_specs = (
        P(seq, "tp"),
        P(seq, "tp"),
        P(seq, "tp"),
        P(None, None, "tp"),
        P(None, "tp"),
        P(None, "tp"),
        P("tp"),
        P("tp", None),
    )
    return jax.shard_map(local, mesh=fine, in_specs=in_specs, out_specs=P(seq, "tp"), check_vma=False)
```

time: 79.4 us -> 68.1 us (0.86)
  blocking collectives: 36.9 us -> 55.1 us
  starting transfers between devices: 14.6 us -> 4.59 us
  waiting for transfers between devices: 12.5 us -> 2.61 us
  Pallas kernels: 9.81 us -> 5.41 us
  local copies, waits for them, and re-layouts: 3.36 us -> 0 us
  other arithmetic: 1.36 us -> 0 us
    all_to_all x0 -> x1, blocking collectives: none -> 19.4 us  [local(): totals = lax.all_to_all(totals, 'z', 0, 0, tiled=True)]
    all_to_all x1 -> x0, starting transfers between devices: 10 us -> none  [local(): totals = lax.all_to_all(totals, 'z', 0, 0, tiled=True)]
    all_to_all x1 -> x0, waiting for transfers between devices: 8.24 us -> none  [local(): totals = lax.all_to_all(totals, 'z', 0, 0, tiled=True)]
    pallas_call x4 -> x6, Pallas kernels: 9.81 us -> 5.41 us  [the longest x1 2.06 us: local(): call(lambda *refs: mix_body(taps, rows * plane, *refs), [VMEM] * 9 + [HBM...]
    slice x3 -> x0, local copies, waits for them, and re-layouts: 2.09 us -> none  [local(): x[rows - RIM:]]
    ppermute x1, waiting for transfers between devices: 4.24 us -> 2.61 us  [local(): rims = lax.ppermute(rims, order, [(i, i + 1) for i in range(devices - 1)])]
    mul x1 -> x0, other arithmetic: 1.36 us -> none  [local(): amplitude = residue * jnp.sqrt(-jnp.expm1(-2.0 * rate))]
    unnamed x4 -> x0, local copies, waits for them, and re-layouts: 1.27 us -> none
  transfers between devices with their start and end apart: 2 -> 1, of which waited for: 2 -> 1; matrix products, arithmetic and copies ran while one was open for 2% -> 0% of each run, Pallas kernels for 0% -> 2%
where the time goes in v2:
time: 68.1 us; the launch traced here: 67.7 us
  blocking collectives  55.1 us (81%)
  Pallas kernels  5.41 us (8%)
  starting transfers between devices  4.59 us (7%)
  waiting for transfers between devices  2.61 us (4%)
    all_to_all x1, blocking collectives, local(): totals = lax.all_to_all(totals, 'z', 0, 0, tiled=True)  19.4 us
    all_to_all x1, blocking collectives, local(): partial = lax.all_to_all(partial, 'tp', 0, 0, tiled=True)  18 us
    all_to_all x1, blocking collectives, local(): states = lax.all_to_all(states, ('y', 'core'), 0, 0, tiled=True)  17.6 us
    ppermute x1, starting transfers between devices, local(): rims = lax.ppermute(rims, order, [(i, i + 1) for i in range(devices - 1)])  4.59 us
    ppermute x1, waiting for transfers between devices, local(): rims = lax.ppermute(rims, order, [(i, i + 1) for i in range(devices - 1)])  2.61 us
    pallas_call x1, Pallas kernels, local(): call(lambda *refs: mix_body(taps, rows * plane, *refs), [VMEM] * 9 + [HBM...  2.06 us
    pallas_call x1, Pallas kernels, local(): call(gate_body, [HBM] * 6, (shape(by_half, F32), shape(by_half, F32), sha...  1.63 us
  transfers between devices with their start and end apart: 1, of which 1 were waited for; matrix products, arithmetic and copies ran while one was open for 0% of the time, Pallas kernels for 2%

profile of v2, /device:TPU:1, one launch (start us, length us, event | category | flops | bytes accessed | tf_op | source)
XLA Modules:
  0.0 67.7 jit_solution(17539870063829913732)
XLA Ops:
  0.0 0.8 %rims.1 = bf16[48,256]{1,0:T(8,128)(2,1)S(1)} custom-call(bf16[128,256]{1,0:T(8,128)(2,1)} %q_ref.1, bf16[128,256]{1,0:T(8,128)(2,1)} %k_ref.1, bf16[128,256]{1,0:T(8,128)(2,1)} %v_ref.1), custom_call_target="tpu_custom_call" | custom-call | tf_op jit(solution)/shard_map/rims/pallas_call | solution.py:246
  0.8 4.6 %collective-permute-start = (bf16[48,256]{1,0:T(8,128)(2,1)S(1)}, bf16[48,256]{1,0:T(8,128)(2,1)S(1)}, u32[]{:S(2)}, u32[]{:S(2)}) collective-permute-start(bf16[48,256]{1,0:T(8,128)(2,1)S(1)} %rims.1), channel_id=1, source_target_pairs={{0,4},{4,8},{8,12},{12,16},{16,20},{20,24},{24,28},{28,32},{32,36}... | collective-permute-start | bytes 73736 | tf_op jit(solution)/shard_map/ppermute | solution.py:249
  5.4 1.6 %gate.1 = (f32[2,128,128]{2,1,0:T(8,128)S(1)}, f32[2,128,128]{2,1,0:T(8,128)S(1)}, f32[16,8,256]{2,1,0:T(8,128)S(1)}, f32[16,256]{1,0:T(8,128)S(1)}, f32[3,8,256...) custom-call(bf16[128,256]{1,0:T(8,128)(2,1)} %q_ref.1, ...), custom_call_target="tpu_custom_call" | custom-call | tf_op jit(solution)/shard_map/gate/pallas_call | solution.py:250
  7.0 2.6 %collective-permute-done.refs_0_ = bf16[48,256]{1,0:T(8,128)(2,1)S(1)} collective-permute-done((bf16[48,256]{1,0:T(8,128)(2,1)S(1)}, bf16[48,256]{1,0:T(8,128)(2,1)S(1)}, u32[]{:S(2)}, u32[]{:S(2)}) %collective-permute-start) | collective-permute-done | bytes 24608 | tf_op jit(solution)/shard_map/ppermute | solution.py:249
  9.6 0.1 join.1
  9.7 17.6 %all_to_all.15.refs_0_ = f32[16,16,256]{2,1,0:T(8,128)S(1)} all-to-all(f32[16,16,256]{2,1,0:T(8,128)S(1)} %get-tuple-element.27), channel_id=1, replica_groups=mesh['z'=8,'y'=8,'core'=2,'tp'=4] {'y','core'}, dimensions={0} | all-to-all | bytes 524288 | tf_op jit(solution)/shard_map/all_to_all | solution.py:282
  27.3 0.1 plane.1
  27.4 19.4 %all_to_all.16.refs_6_ = f32[8,16,256]{2,1,0:T(8,128)S(1)} all-to-all(f32[8,16,256]{2,1,0:T(8,128)S(1)} %get-tuple-element.29), channel_id=1, replica_groups=mesh['z'=8,'y'=8,'core'=2,'tp'=4] {'z'}, dimensions={0} | all-to-all | bytes 262144 | tf_op jit(solution)/shard_map/all_to_all | solution.py:289
  46.8 2.1 %mix.1 = bf16[4,128,1024]{2,1,0:T(8,128)(2,1)S(1)} custom-call(f32[2,128,128]{2,1,0:T(8,128)S(1)} %get-tuple-element.18.refs_0_, f32[2,128,128]{2,1,0:T(8,128)S(1)} %get-tuple-element.19.refs_1_, f32[16,8,256]{2,1,0:T(8,128)S(1)} %get-tuple-element.20.refs_2_, f32[16,256]{1,0:T(8,128)S(1)} %get-tuple-element.25.refs_3_, ...), custom_call_target="tpu_custom_call" | custom-call | tf_op jit(solution)/shard_map/mix/pallas_call | solution.py:290
  48.9 18.0 %all_to_all.17.parts_ref = bf16[4,128,1024]{2,1,0:T(8,128)(2,1)S(1)} all-to-all(bf16[4,128,1024]{2,1,0:T(8,128)(2,1)S(1)} %mix.1), channel_id=1, replica_groups=mesh['z'=8,'y'=8,'core'=2,'tp'=4] {'tp'}, dimensions={0} | all-to-all | bytes 2097152 | tf_op jit(solution)/shard_map/all_to_all | solution.py:304
  66.9 0.8 %total.1 = bf16[128,1024]{1,0:T(8,128)(2,1)} custom-call(bf16[4,128,1024]{2,1,0:T(8,128)(2,1)S(1)} %all_to_all.17.parts_ref), custom_call_target="tpu_custom_call" | custom-call | tf_op jit(solution)/shard_map/total/pallas_call | solution.py:305
Async XLA Ops:
  0.8 8.8 %collective-permute-start = (bf16[48,256]{1,0:T(8,128)(2,1)S(1)}, bf16[48,256]{1,0:T(8,128)(2,1)S(1)}, u32[]{:S(2)}, u32[]{:S(2)}) collective-permute-start(bf16[48,256]{1,0:T(8,128)(2,1)S(1)} %rims.1), channel_id=1, source_target_pairs={{0,4},{4,8},{8,12},{12,16},{16,20},{20,24},{24,28},{28,32},{32,36}... | collective-permute-start | bytes 73736 | tf_op jit(solution)/shard_map/ppermute | solution.py:249

commit v3 on v2

--- a/solution.py
+++ b/solution.py
@@ -141,7 +141,7 @@
     for i in range(1, taps - 1):
         late = retain * late + more[i : i + 1]
     late_ref[...] = late
-    whole = state_ref[...] + jnp.exp(-(rows - taps + 1) * rate) * late
+    whole = (state_ref[...] + jnp.exp(-(rows - taps + 1) * rate) * late).astype(BF16)
     for i in range(out_ref.shape[0]):
         out_ref[i] = whole
 
@@ -152,12 +152,12 @@
     before = jnp.zeros(rate_ref.shape, F32)
     total = jnp.zeros(rate_ref.shape, F32)
     for i in range(parts_ref.shape[0]):
-        part = parts_ref[i]
+        part = parts_ref[i].astype(F32)
         before = jnp.where(i < me, before * drop + part, before)
         total = total * drop + part
     before_ref[...] = before
     for i in range(total_ref.shape[0]):
-        total_ref[i] = total
+        total_ref[i] = total.astype(BF16)
 
 
 def mix_body(
@@ -179,7 +179,7 @@
     drop = jnp.exp(-plane_rows * rate)
     behind = jnp.zeros(rate.shape, F32)
     for i in range(planes_ref.shape[0]):
-        behind = jnp.where(i < z, behind * drop + planes_ref[i], behind)
+        behind = jnp.where(i < z, behind * drop + planes_ref[i].astype(F32), behind)
     carried = before_ref[...] + jnp.exp(-(rows * me).astype(F32) * rate) * behind
     carry[0] = carried
     carry[1] = carried + jnp.exp((taps - 1) * rate) * late_ref[...]
@@ -272,7 +272,7 @@
         lambda *refs: join_body(rows, *refs),
         [VMEM] * 5,
         (
-            shape((plane, modes, channels), F32),
+            shape((plane, modes, channels), BF16),
             shape((modes, channels), F32),
             shape((2, HEAD, channels), F32),
         ),
@@ -283,7 +283,7 @@
     before, totals = call(
         lambda *refs: plane_body(rows, *refs),
         [VMEM] * 2,
-        (shape((modes, channels), F32), shape((planes, modes, channels), F32)),
+        (shape((modes, channels), F32), shape((planes, modes, channels), BF16)),
         "plane",
     )(states, rate)
     totals = lax.all_to_all(totals, "z", 0, 0, tiled=True)

time: 68.1 us -> 62.9 us (0.924)
  blocking collectives: 55.1 us -> 49.6 us
    all_to_all x1, blocking collectives: 17.6 us -> 15.1 us  [local(): states = lax.all_to_all(states, ('y', 'core'), 0, 0, tiled=True)]
    all_to_all x1, blocking collectives: 19.4 us -> 17.3 us  [local(): totals = lax.all_to_all(totals, 'z', 0, 0, tiled=True)]
    all_to_all x1, blocking collectives: 18 us -> 17.2 us  [local(): partial = lax.all_to_all(partial, 'tp', 0, 0, tiled=True)]
  transfers between devices with their start and end apart: 1 -> 1, of which waited for: 1 -> 1; matrix products, arithmetic and copies ran while one was open for 0% -> 0% of each run, Pallas kernels for 2% -> 3%
where the time goes in v3:
time: 62.9 us; the launch traced here: 62.3 us
  blocking collectives  49.6 us (79%)
  Pallas kernels  5.41 us (9%)
  starting transfers between devices  4.59 us (7%)
  waiting for transfers between devices  2.61 us (4%)
    all_to_all x1, blocking collectives, local(): totals = lax.all_to_all(totals, 'z', 0, 0, tiled=True)  17.3 us
    all_to_all x1, blocking collectives, local(): partial = lax.all_to_all(partial, 'tp', 0, 0, tiled=True)  17.2 us
    all_to_all x1, blocking collectives, local(): states = lax.all_to_all(states, ('y', 'core'), 0, 0, tiled=True)  15.1 us
    ppermute x1, starting transfers between devices, local(): rims = lax.ppermute(rims, order, [(i, i + 1) for i in range(devices - 1)])  4.59 us
    ppermute x1, waiting for transfers between devices, local(): rims = lax.ppermute(rims, order, [(i, i + 1) for i in range(devices - 1)])  2.61 us
    pallas_call x1, Pallas kernels, local(): call(lambda *refs: mix_body(taps, rows * plane, *refs), [VMEM] * 9 + [HBM...  2.06 us
    pallas_call x1, Pallas kernels, local(): call(gate_body, [HBM] * 6, (shape(by_half, F32), shape(by_half, F32), sha...  1.63 us
  transfers between devices with their start and end apart: 1, of which 1 were waited for; matrix products, arithmetic and copies ran while one was open for 0% of the time, Pallas kernels for 3%

profile of v3, /device:TPU:1, one launch (start us, length us, event | category | flops | bytes accessed | tf_op | source)
XLA Modules:
  0.0 62.3 jit_solution(18019474602981848564)
XLA Ops:
  0.0 0.8 %rims.1 = bf16[48,256]{1,0:T(8,128)(2,1)S(1)} custom-call(bf16[128,256]{1,0:T(8,128)(2,1)} %q_ref.1, bf16[128,256]{1,0:T(8,128)(2,1)} %k_ref.1, bf16[128,256]{1,0:T(8,128)(2,1)} %v_ref.1), custom_call_target="tpu_custom_call" | custom-call | tf_op jit(solution)/shard_map/rims/pallas_call | solution.py:246
  0.8 4.6 %collective-permute-start = (bf16[48,256]{1,0:T(8,128)(2,1)S(1)}, bf16[48,256]{1,0:T(8,128)(2,1)S(1)}, u32[]{:S(2)}, u32[]{:S(2)}) collective-permute-start(bf16[48,256]{1,0:T(8,128)(2,1)S(1)} %rims.1), channel_id=1, source_target_pairs={{0,4},{4,8},{8,12},{12,16},{16,20},{20,24},{24,28},{28,32},{32,36}... | collective-permute-start | bytes 73736 | tf_op jit(solution)/shard_map/ppermute | solution.py:249
  5.4 1.6 %gate.1 = (f32[2,128,128]{2,1,0:T(8,128)S(1)}, f32[2,128,128]{2,1,0:T(8,128)S(1)}, f32[16,8,256]{2,1,0:T(8,128)S(1)}, f32[16,256]{1,0:T(8,128)S(1)}, f32[3,8,256...) custom-call(bf16[128,256]{1,0:T(8,128)(2,1)} %q_ref.1, ...), custom_call_target="tpu_custom_call" | custom-call | tf_op jit(solution)/shard_map/gate/pallas_call | solution.py:250
  7.0 2.6 %collective-permute-done.refs_0_ = bf16[48,256]{1,0:T(8,128)(2,1)S(1)} collective-permute-done((bf16[48,256]{1,0:T(8,128)(2,1)S(1)}, bf16[48,256]{1,0:T(8,128)(2,1)S(1)}, u32[]{:S(2)}, u32[]{:S(2)}) %collective-permute-start) | collective-permute-done | bytes 24608 | tf_op jit(solution)/shard_map/ppermute | solution.py:249
  9.6 0.1 join.1
  9.7 15.1 %all_to_all.15.refs_0_ = bf16[16,16,256]{2,1,0:T(8,128)(2,1)S(1)} all-to-all(bf16[16,16,256]{2,1,0:T(8,128)(2,1)S(1)} %get-tuple-element.27), channel_id=1, replica_groups=mesh['z'=8,'y'=8,'core'=2,'tp'=4] {'y','core'}, dimensions={0} | all-to-all | bytes 262144 | tf_op jit(solution)/shard_map/all_to_all | solution.py:282
  24.8 0.1 plane.1
  24.8 17.3 %all_to_all.16.refs_6_ = bf16[8,16,256]{2,1,0:T(8,128)(2,1)S(1)} all-to-all(bf16[8,16,256]{2,1,0:T(8,128)(2,1)S(1)} %get-tuple-element.29), channel_id=1, replica_groups=mesh['z'=8,'y'=8,'core'=2,'tp'=4] {'z'}, dimensions={0} | all-to-all | bytes 131072 | tf_op jit(solution)/shard_map/all_to_all | solution.py:289
  42.1 2.1 %mix.1 = bf16[4,128,1024]{2,1,0:T(8,128)(2,1)S(1)} custom-call(f32[2,128,128]{2,1,0:T(8,128)S(1)} %get-tuple-element.18.refs_0_, f32[2,128,128]{2,1,0:T(8,128)S(1)} %get-tuple-element.19.refs_1_, f32[16,8,256]{2,1,0:T(8,128)S(1)} %get-tuple-element.20.refs_2_, f32[16,256]{1,0:T(8,128)S(1)} %get-tuple-element.25.refs_3_, ...), custom_call_target="tpu_custom_call" | custom-call | tf_op jit(solution)/shard_map/mix/pallas_call | solution.py:290
  44.2 17.2 %all_to_all.17.parts_ref = bf16[4,128,1024]{2,1,0:T(8,128)(2,1)S(1)} all-to-all(bf16[4,128,1024]{2,1,0:T(8,128)(2,1)S(1)} %mix.1), channel_id=1, replica_groups=mesh['z'=8,'y'=8,'core'=2,'tp'=4] {'tp'}, dimensions={0} | all-to-all | bytes 2097152 | tf_op jit(solution)/shard_map/all_to_all | solution.py:304
  61.4 0.8 %total.1 = bf16[128,1024]{1,0:T(8,128)(2,1)} custom-call(bf16[4,128,1024]{2,1,0:T(8,128)(2,1)S(1)} %all_to_all.17.parts_ref), custom_call_target="tpu_custom_call" | custom-call | tf_op jit(solution)/shard_map/total/pallas_call | solution.py:305
Async XLA Ops:
  0.8 8.8 %collective-permute-start = (bf16[48,256]{1,0:T(8,128)(2,1)S(1)}, bf16[48,256]{1,0:T(8,128)(2,1)S(1)}, u32[]{:S(2)}, u32[]{:S(2)}) collective-permute-start(bf16[48,256]{1,0:T(8,128)(2,1)S(1)} %rims.1), channel_id=1, source_target_pairs={{0,4},{4,8},{8,12},{12,16},{16,20},{20,24},{24,28},{28,32},{32,36}... | collective-permute-start | bytes 73736 | tf_op jit(solution)/shard_map/ppermute | solution.py:249

commit v4 on v3

--- a/solution.py
+++ b/solution.py
@@ -69,10 +69,12 @@
 
 
 def gate_body(
-    q_hbm, k_hbm, v_hbm, taps_hbm, rate_hbm, residue_hbm,
-    query_ref, gated_ref, begin_ref, state_ref, head_ref, taps_ref, rate_ref, amp_ref,
-    streams, residue_ref, pad, sems,
+    q_hbm, k_hbm, v_hbm, taps_hbm, rate_hbm, residue_hbm, weight_hbm,
+    query_ref, gated_ref, begin_ref, state_ref, head_ref, taps_ref, rate_ref, amp_ref, *rest,
 ):
+    *blocks, streams, residue_ref, pad, sems = rest
+    here, parts = lax.axis_index("tp"), lax.axis_size("tp")
+    width = blocks[0].shape[1]
     _, rows, channels = streams.shape
     modes = rate_ref.shape[0]
     taps = taps_ref.shape[1]
@@ -81,6 +83,11 @@
         (q_hbm, k_hbm, v_hbm, taps_hbm, rate_hbm, residue_hbm),
         (streams.at[0], streams.at[1], streams.at[2], taps_ref, rate_ref, residue_ref),
         sems,
+    )
+    sent = fetch(
+        [weight_hbm.at[:, pl.ds(lax.rem(here + d, parts) * width, width)] for d in range(1, parts)],
+        blocks,
+        sems.at[pl.ds(6, parts - 1)],
     )
     for copy in copies:
         copy.wait()
@@ -118,6 +125,8 @@
                 s = s + jnp.where(sub >= d, drop * pltpu.roll(s, d, 0), 0.0)
             state_ref[pl.ds(m, 1), lanes] = s[SUBS - 1 :]
             begin_ref[m, :, lanes] = jnp.where(sub >= 1, pltpu.roll(s, 1, 0), 0.0)
+    for copy in sent:
+        copy.wait()
 
 
 def join_body(rows, rim_ref, head_ref, taps_ref, rate_ref, state_ref, out_ref, late_ref, top_ref, pad):
@@ -162,17 +171,12 @@
 
 def mix_body(
     taps, plane_rows, query_ref, gated_ref, begin_ref, late_ref, top_ref, before_ref, planes_ref, rate_ref, amp_ref,
-    skip_hbm, weight_hbm, out_ref, hyena, carry, skip_ref, weight, sems,
+    skip_hbm, out_ref, hyena, carry, skip_ref, sems,
 ):
     halves, rows, _ = query_ref.shape
     modes = rate_ref.shape[0]
     steps = rows // SUBS
-    parts, _, width = out_ref.shape
-    copies = fetch(
-        [skip_hbm] + [weight_hbm.at[:, pl.ds(i * width, width)] for i in range(parts)],
-        [skip_ref] + [weight.at[i] for i in range(parts)],
-        sems,
-    )
+    copies = fetch([skip_hbm], [skip_ref], sems)
     z = lax.axis_index("z")
     me = lax.axis_index("y") * lax.axis_size("core") + lax.axis_index("core")
     rate = rate_ref[...]
@@ -211,20 +215,29 @@
                 terms = [x + y for x, y in zip(terms[::2], terms[1::2])] + terms[len(terms) // 2 * 2 :]
             hyena[half, at, :] = query * terms[0]
     left = jnp.concatenate([hyena[half].astype(BF16) for half in range(halves)], axis=1)
+    for i in range(out_ref.shape[0]):
+        out_ref[i] = left
+
+
+def project_body(left_ref, weight_hbm, *rest):
+    *others, out_ref, own, sem = rest
+    parts, _, _ = left_ref.shape
+    width = out_ref.shape[1]
+    here = lax.axis_index("tp")
+    copy = pltpu.make_async_copy(weight_hbm.at[:, pl.ds(here * width, width)], own, sem)
+    copy.start()
     block = 512
-    for i in range(parts):
-        copies[1 + i].wait()
-        for c in range(0, width, block):
-            out_ref[i, :, pl.ds(c, block)] = jnp.dot(
-                left, weight[i, :, pl.ds(c, block)], preferred_element_type=F32
-            ).astype(BF16)
-
-
-def sum_body(parts_ref, out_ref):
-    total = parts_ref[0].astype(F32)
-    for i in range(1, parts_ref.shape[0]):
-        total = total + parts_ref[i].astype(F32)
-    out_ref[...] = total.astype(BF16)
+    for c in range(0, width, block):
+        at = pl.ds(c, block)
+        total = jnp.zeros((out_ref.shape[0], block), F32)
+        for d in range(1, parts):
+            total += jnp.dot(
+                left_ref[lax.rem(here + parts - d, parts)], others[d - 1][:, at], preferred_element_type=F32
+            )
+        if c == 0:
+            copy.wait()
+        total += jnp.dot(left_ref[here], own[:, at], preferred_element_type=F32)
+        out_ref[:, at] = total.astype(BF16)
 
 
 def local(query_in, key_in, value_in, short_weight, residue, rate, skip, out_weight):
@@ -247,9 +260,9 @@
         rim_body, [HBM] * 3, shape((3 * RIM, channels), BF16), "rims", [pltpu.SemaphoreType.DMA((3,))]
     )(query_in, key_in, value_in)
     rims = lax.ppermute(rims, order, [(i, i + 1) for i in range(devices - 1)])
-    queries, gated, begin, states, heads, taps_here, rate, amplitude = call(
+    queries, gated, begin, states, heads, taps_here, rate, amplitude, *blocks = call(
         gate_body,
-        [HBM] * 6,
+        [HBM] * 7,
         (
             shape(by_half, F32),
             shape(by_half, F32),
@@ -259,15 +272,20 @@
             shape(short_weight.shape, F32),
             shape((modes, channels), F32),
             shape((modes, channels), F32),
+            *[shape((channels, width), BF16)] * (parts - 1),
         ),
         "gate",
         [
             pltpu.VMEM((3, rows, channels), BF16),
             pltpu.VMEM((modes, channels), F32),
             pltpu.VMEM((3, HEAD + rows, channels), F32),
-            pltpu.SemaphoreType.DMA((6,)),
+            pltpu.SemaphoreType.DMA((6 + parts - 1,)),
         ],
-    )(query_in, key_in, value_in, short_weight, rate, residue)
+    )(query_in, key_in, value_in, short_weight, rate, residue, out_weight)
+    blocks = [
+        lax.ppermute(block, "tp", [(i, (i + d) % parts) for i in range(parts)])
+        for d, block in enumerate(blocks, start=1)
+    ]
     states, late, top = call(
         lambda *refs: join_body(rows, *refs),
         [VMEM] * 5,
@@ -287,22 +305,26 @@
         "plane",
     )(states, rate)
     totals = lax.all_to_all(totals, "z", 0, 0, tiled=True)
-    partial = call(
+    hyena = call(
         lambda *refs: mix_body(taps, rows * plane, *refs),
-        [VMEM] * 9 + [HBM] * 2,
-        shape((parts, rows, width), BF16),
+        [VMEM] * 9 + [HBM],
+        shape((parts, rows, channels), BF16),
         "mix",
         [
             pltpu.VMEM(by_half, F32),
             pltpu.VMEM((2, modes, channels), F32),
             pltpu.VMEM((1, channels), F32),
-            pltpu.VMEM((parts, channels, width), BF16),
-            pltpu.SemaphoreType.DMA((1 + parts,)),
+            pltpu.SemaphoreType.DMA((1,)),
         ],
-        8,
-    )(queries, gated, begin, late, top, before, totals, rate, amplitude, skip, out_weight)
-    partial = lax.all_to_all(partial, "tp", 0, 0, tiled=True)
-    return call(sum_body, [VMEM], shape((rows, width), BF16), "total")(partial)
+    )(queries, gated, begin, late, top, before, totals, rate, amplitude, skip)
+    hyena = lax.all_to_all(hyena, "tp", 0, 0, tiled=True)
+    return call(
+        project_body,
+        [VMEM, HBM] + [VMEM] * (parts - 1),
+        shape((rows, width), BF16),
+        "project",
+        [pltpu.VMEM((channels, width), BF16), pltpu.SemaphoreType.DMA],
+    )(hyena, out_weight, *blocks)
 
 
 def solution(mesh):

time: 62.9 us -> 59.9 us (0.952)
  the two profiles are of different devices: /device:TPU:1 before, /device:TPU:8 now
where the time goes in v4:
time: 59.9 us; the launch traced here: 59.4 us
  starting transfers between devices  25.5 us (43%)
  blocking collectives  18.5 us (31%)
  Pallas kernels  7.98 us (13%)
  waiting for transfers between devices  7.4 us (12%)
    all_to_all x1, blocking collectives, local(): totals = lax.all_to_all(totals, 'z', 0, 0, tiled=True)  18.5 us
    ppermute x3, starting transfers between devices, local(): lax.ppermute(block, 'tp', [(i, (i + d) % parts) for i in range(parts)])  11.4 us
    all_to_all x1, starting transfers between devices, local(): states = lax.all_to_all(states, ('y', 'core'), 0, 0, tiled=True)  8.75 us
    all_to_all x1, waiting for transfers between devices, local(): hyena = lax.all_to_all(hyena, 'tp', 0, 0, tiled=True)  6.61 us
    all_to_all x1, starting transfers between devices, local(): hyena = lax.all_to_all(hyena, 'tp', 0, 0, tiled=True)  3.42 us
    pallas_call x1, Pallas kernels, local(): call(gate_body, [HBM] * 7, (shape(by_half, F32), shape(by_half, F32), sha...  2.46 us
    pallas_call x1, Pallas kernels, local(): call(project_body, [VMEM, HBM] + [VMEM] * (parts - 1), shape((rows, width...  2.17 us
    ppermute x1, starting transfers between devices, local(): rims = lax.ppermute(rims, order, [(i, i + 1) for i in range(devices - 1)])  1.92 us
  transfers between devices with their start and end apart: 6, of which 2 were waited for; matrix products, arithmetic and copies ran while one was open for 0% of the time, Pallas kernels for 7%

profile of v4, /device:TPU:8, one launch (start us, length us, event | category | flops | bytes accessed | tf_op | source)
XLA Modules:
  0.0 59.4 jit_solution(4878077333925953699)
XLA Ops:
  0.0 0.8 %rims.1 = bf16[48,256]{1,0:T(8,128)(2,1)S(1)} custom-call(bf16[128,256]{1,0:T(8,128)(2,1)} %q_ref.1, bf16[128,256]{1,0:T(8,128)(2,1)} %k_ref.1, bf16[128,256]{1,0:T(8,128)(2,1)} %v_ref.1), custom_call_target="tpu_custom_call" | custom-call | tf_op jit(solution)/shard_map/rims/pallas_call | solution.py:259
  0.8 1.9 %collective-permute-start = (bf16[48,256]{1,0:T(8,128)(2,1)S(1)}, bf16[48,256]{1,0:T(8,128)(2,1)S(1)}, u32[]{:S(2)}, u32[]{:S(2)}) collective-permute-start(bf16[48,256]{1,0:T(8,128)(2,1)S(1)} %rims.1), channel_id=1, source_target_pairs={{0,4},{4,8},{8,12},{12,16},{16,20},{20,24},{24,28},{28,32},{32,36}... | collective-permute-start | bytes 73736 | tf_op jit(solution)/shard_map/ppermute | solution.py:262
  2.7 2.5 %gate.1 = (f32[2,128,128]{2,1,0:T(8,128)S(1)}, f32[2,128,128]{2,1,0:T(8,128)S(1)}, f32[16,8,256]{2,1,0:T(8,128)S(1)}, f32[16,256]{1,0:T(8,128)S(1)}, f32[3,8,256...) custom-call(bf16[128,256]{1,0:T(8,128)(2,1)} %q_ref.1, ...), custom_call_target="tpu_custom_call" | custom-call | tf_op jit(solution)/shard_map/gate/pallas_call | solution.py:263
  5.2 0.8 %collective-permute-done.refs_0_ = bf16[48,256]{1,0:T(8,128)(2,1)S(1)} collective-permute-done((bf16[48,256]{1,0:T(8,128)(2,1)S(1)}, bf16[48,256]{1,0:T(8,128)(2,1)S(1)}, u32[]{:S(2)}, u32[]{:S(2)}) %collective-permute-start) | collective-permute-done | bytes 24608 | tf_op jit(solution)/shard_map/ppermute | solution.py:262
  5.9 0.7 %join.1 = (bf16[16,16,256]{2,1,0:T(8,128)(2,1)}, f32[16,256]{1,0:T(8,128)S(1)}, f32[2,8,256]{2,1,0:T(8,128)S(1)}) custom-call(bf16[48,256]{1,0:T(8,128)(2,1)S(1)} %collective-permute-done.refs_0_, f32[3,8,256]{2,1,0:T(8,128)S(1)} %get-tuple-element.24.refs_1_, f32[3,7,256]{2,1,0:T(8,128)S(1)} %get-tuple-element.25.refs_2_, ...), custom_call_target="tpu_custom_call" | custom-call | tf_op jit(solution)/shard_map/join/pallas_call | solution.py:289
  6.7 8.8 %all-to-all-start = ((bf16[16,16,256]{2,1,0:T(8,128)(2,1)}), bf16[16,16,256]{2,1,0:T(8,128)(2,1)S(1)}, u32[]{:S(2)}, u32[]{:S(2)}) async-start(bf16[16,16,256]{2,1,0:T(8,128)(2,1)} %get-tuple-element.30), calls=%async_computation | async-start | bytes 262144 | tf_op jit(solution)/shard_map/all_to_all | solution.py:300
  15.4 3.4 %collective-permute-start.1 = (bf16[256,1024]{1,0:T(8,128)(2,1)}, bf16[256,1024]{1,0:T(8,128)(2,1)S(1)}, u32[]{:S(2)}, u32[]{:S(2)}) collective-permute-start(bf16[256,1024]{1,0:T(8,128)(2,1)} %get-tuple-element.34), channel_id=1, source_target_pairs={{0,1},{1,2},{2,3},{3,0},{4,5},{5,6},{6,7},{7,4},{8,9},{9,10},{10,1... | collective-permute-start | bytes 1572872 | tf_op jit(solution)/shard_map/ppermute | solution.py:286
  18.8 4.6 %collective-permute-start.2 = (bf16[256,1024]{1,0:T(8,128)(2,1)S(1)}, bf16[256,1024]{1,0:T(8,128)(2,1)S(1)}, u32[]{:S(2)}, u32[]{:S(2)}) collective-permute-start(bf16[256,1024]{1,0:T(8,128)(2,1)S(1)} %get-tuple-element.35), channel_id=1, source_target_pairs={{0,2},{1,3},{2,0},{3,1},{4,6},{5,7},{6,4},{7,5},{8,10},{9,11},{10,... | collective-permute-start | bytes 1572872 | tf_op jit(solution)/shard_map/ppermute | solution.py:286
  23.4 3.3 %collective-permute-start.3 = (bf16[256,1024]{1,0:T(8,128)(2,1)S(1)}, bf16[256,1024]{1,0:T(8,128)(2,1)S(1)}, u32[]{:S(2)}, u32[]{:S(2)}) collective-permute-start(bf16[256,1024]{1,0:T(8,128)(2,1)S(1)} %get-tuple-element.36), channel_id=1, source_target_pairs={{0,3},{1,0},{2,1},{3,2},{4,7},{5,4},{6,5},{7,6},{8,11},{9,8},{10,9... | collective-permute-start | bytes 1572872 | tf_op jit(solution)/shard_map/ppermute | solution.py:286
  26.8 0.0 all-to-all-done.refs_0_
  26.8 0.1 plane.1
  26.9 18.5 %all_to_all.15.refs_6_ = bf16[8,16,256]{2,1,0:T(8,128)(2,1)S(1)} all-to-all(bf16[8,16,256]{2,1,0:T(8,128)(2,1)S(1)} %get-tuple-element.32), channel_id=1, replica_groups=mesh['z'=8,'y'=8,'core'=2,'tp'=4] {'z'}, dimensions={0} | all-to-all | bytes 131072 | tf_op jit(solution)/shard_map/all_to_all | solution.py:307
  45.4 1.8 %mix.1 = bf16[4,128,256]{2,1,0:T(8,128)(2,1)} custom-call(f32[2,128,128]{2,1,0:T(8,128)S(1)} %get-tuple-element.21.refs_0_, f32[2,128,128]{2,1,0:T(8,128)S(1)} %get-tuple-element.22.refs_1_, f32[16,8,256]{2,1,0:T(8,128)S(1)} %get-tuple-element.23.refs_2_, f32[16,256]{1,0:T(8,128)S(1)} %get-tuple-element.28.refs_3_, ...), custom_call_target="tpu_custom_call" | custom-call | tf_op jit(solution)/shard_map/mix/pallas_call | solution.py:308
  47.2 3.4 %all-to-all-start.2 = ((bf16[4,128,256]{2,1,0:T(8,128)(2,1)}), bf16[4,128,256]{2,1,0:T(8,128)(2,1)S(1)}, u32[]{:S(2)}, u32[]{:S(2)}) async-start(bf16[4,128,256]{2,1,0:T(8,128)(2,1)} %mix.1), calls=%async_computation.2 | async-start | bytes 524288 | tf_op jit(solution)/shard_map/all_to_all | solution.py:320
  50.6 0.0 collective-permute-done.1.rest_0_
  50.6 0.0 collective-permute-done.2.rest_1_
  50.6 0.0 collective-permute-done.3.rest_2_
  50.6 6.6 %all-to-all-done.2.left_ref = bf16[4,128,256]{2,1,0:T(8,128)(2,1)S(1)} async-done(((bf16[4,128,256]{2,1,0:T(8,128)(2,1)}), bf16[4,128,256]{2,1,0:T(8,128)(2,1)S(1)}, u32[]{:S(2)}, u32[]{:S(2)}) %all-to-all-start.2) | async-done | bytes 262176 | tf_op jit(solution)/shard_map/all_to_all | solution.py:320
  57.3 2.2 %project.1 = bf16[128,1024]{1,0:T(8,128)(2,1)} custom-call(bf16[4,128,256]{2,1,0:T(8,128)(2,1)S(1)} %all-to-all-done.2.left_ref, bf16[256,4096]{1,0:T(8,128)(2,1)} %weight_hbm.3, bf16[256,1024]{1,0:T(8,128)(2,1)S(1)} %collective-permute-done.1.rest_0_, bf16[256,1024]{1,0:T(8,128)(2,1)S(1)} %collective-permute-done.2.rest_1_, ...), custom_call_target="tpu_custom_call" | custom-call | tf_op jit(solution)/shard_map/project/pallas_call | solution.py:321
Async XLA Ops:
  0.8 5.2 %collective-permute-start = (bf16[48,256]{1,0:T(8,128)(2,1)S(1)}, bf16[48,256]{1,0:T(8,128)(2,1)S(1)}, u32[]{:S(2)}, u32[]{:S(2)}) collective-permute-start(bf16[48,256]{1,0:T(8,128)(2,1)S(1)} %rims.1), channel_id=1, source_target_pairs={{0,4},{4,8},{8,12},{12,16},{16,20},{20,24},{24,28},{28,32},{32,36}... | collective-permute-start | bytes 73736 | tf_op jit(solution)/shard_map/ppermute | solution.py:262
  6.7 20.1 %all-to-all-start = ((bf16[16,16,256]{2,1,0:T(8,128)(2,1)}), bf16[16,16,256]{2,1,0:T(8,128)(2,1)S(1)}, u32[]{:S(2)}, u32[]{:S(2)}) async-start(bf16[16,16,256]{2,1,0:T(8,128)(2,1)} %get-tuple-element.30), calls=%async_computation | async-start | bytes 262144 | tf_op jit(solution)/shard_map/all_to_all | solution.py:300
  15.4 35.2 %collective-permute-start.1 = (bf16[256,1024]{1,0:T(8,128)(2,1)}, bf16[256,1024]{1,0:T(8,128)(2,1)S(1)}, u32[]{:S(2)}, u32[]{:S(2)}) collective-permute-start(bf16[256,1024]{1,0:T(8,128)(2,1)} %get-tuple-element.34), channel_id=1, source_target_pairs={{0,1},{1,2},{2,3},{3,0},{4,5},{5,6},{6,7},{7,4},{8,9},{9,10},{10,1... | collective-permute-start | bytes 1572872 | tf_op jit(solution)/shard_map/ppermute | solution.py:286
  18.8 31.8 %collective-permute-start.2 = (bf16[256,1024]{1,0:T(8,128)(2,1)S(1)}, bf16[256,1024]{1,0:T(8,128)(2,1)S(1)}, u32[]{:S(2)}, u32[]{:S(2)}) collective-permute-start(bf16[256,1024]{1,0:T(8,128)(2,1)S(1)} %get-tuple-element.35), channel_id=1, source_target_pairs={{0,2},{1,3},{2,0},{3,1},{4,6},{5,7},{6,4},{7,5},{8,10},{9,11},{10,... | collective-permute-start | bytes 1572872 | tf_op jit(solution)/shard_map/ppermute | solution.py:286
  23.4 27.2 %collective-permute-start.3 = (bf16[256,1024]{1,0:T(8,128)(2,1)S(1)}, bf16[256,1024]{1,0:T(8,128)(2,1)S(1)}, u32[]{:S(2)}, u32[]{:S(2)}) collective-permute-start(bf16[256,1024]{1,0:T(8,128)(2,1)S(1)} %get-tuple-element.36), channel_id=1, source_target_pairs={{0,3},{1,0},{2,1},{3,2},{4,7},{5,4},{6,5},{7,6},{8,11},{9,8},{10,9... | collective-permute-start | bytes 1572872 | tf_op jit(solution)/shard_map/ppermute | solution.py:286
  47.2 10.1 %all-to-all-start.2 = ((bf16[4,128,256]{2,1,0:T(8,128)(2,1)}), bf16[4,128,256]{2,1,0:T(8,128)(2,1)S(1)}, u32[]{:S(2)}, u32[]{:S(2)}) async-start(bf16[4,128,256]{2,1,0:T(8,128)(2,1)} %mix.1), calls=%async_computation.2 | async-start | bytes 524288 | tf_op jit(solution)/shard_map/all_to_all | solution.py:320

commit v5 on v3

--- a/solution.py
+++ b/solution.py
@@ -22,11 +22,11 @@
 HBM = pl.BlockSpec(memory_space=pltpu.HBM)
 
 
-def call(body, specs, outs, name, scratch=(), mib=4):
+def call(body, specs, outs, name, scratch=(), mib=4, out_spec=VMEM):
     return pl.pallas_call(
         body,
         in_specs=specs,
-        out_specs=jax.tree.map(lambda _: VMEM, outs),
+        out_specs=jax.tree.map(lambda _: out_spec, outs),
         out_shape=outs,
         scratch_shapes=list(scratch),
         compiler_params=pltpu.CompilerParams(vmem_limit_bytes=mib * MIB),
@@ -119,8 +119,27 @@
             state_ref[pl.ds(m, 1), lanes] = s[SUBS - 1 :]
             begin_ref[m, :, lanes] = jnp.where(sub >= 1, pltpu.roll(s, 1, 0), 0.0)
 
-
-def join_body(rows, rim_ref, head_ref, taps_ref, rate_ref, state_ref, out_ref, late_ref, top_ref, pad):
+def join_body(
+    rows, rim_ref, head_ref, taps_ref, rate_ref, state_ref, weight_hbm, out_ref, late_ref, top_ref, *rest
+):
+    *blocks, pad, sems = rest
+    here, parts = lax.axis_index("tp"), lax.axis_size("tp")
+    width = blocks[0].shape[1]
+    core = lax.axis_index("core")
+    height = blocks[1].shape[0]
+    side = lax.rem(here + jnp.where(core == 0, 1, parts - 1), parts)
+    across = lax.rem(here + 2, parts)
+    sent = fetch(
+        (
+            weight_hbm.at[:, pl.ds(pl.multiple_of(side * width, LANES), width)],
+            weight_hbm.at[
+                pl.ds(pl.multiple_of(core * height, height), height),
+                pl.ds(pl.multiple_of(across * width, LANES), width),
+            ],
+        ),
+        blocks,
+        sems,
+    )
     modes, channels = rate_ref.shape
     taps = taps_ref.shape[1]
     sums = []
@@ -144,6 +163,8 @@
     whole = (state_ref[...] + jnp.exp(-(rows - taps + 1) * rate) * late).astype(BF16)
     for i in range(out_ref.shape[0]):
         out_ref[i] = whole
+    for copy in sent:
+        copy.wait()
 
 
 def plane_body(rows, parts_ref, rate_ref, before_ref, total_ref):
@@ -162,17 +183,12 @@
 
 def mix_body(
     taps, plane_rows, query_ref, gated_ref, begin_ref, late_ref, top_ref, before_ref, planes_ref, rate_ref, amp_ref,
-    skip_hbm, weight_hbm, out_ref, hyena, carry, skip_ref, weight, sems,
+    skip_hbm, out_ref, hyena, carry, skip_ref, sems,
 ):
     halves, rows, _ = query_ref.shape
     modes = rate_ref.shape[0]
     steps = rows // SUBS
-    parts, _, width = out_ref.shape
-    copies = fetch(
-        [skip_hbm] + [weight_hbm.at[:, pl.ds(i * width, width)] for i in range(parts)],
-        [skip_ref] + [weight.at[i] for i in range(parts)],
-        sems,
-    )
+    copies = fetch([skip_hbm], [skip_ref], sems)
     z = lax.axis_index("z")
     me = lax.axis_index("y") * lax.axis_size("core") + lax.axis_index("core")
     rate = rate_ref[...]
@@ -211,20 +227,43 @@
                 terms = [x + y for x, y in zip(terms[::2], terms[1::2])] + terms[len(terms) // 2 * 2 :]
             hyena[half, at, :] = query * terms[0]
     left = jnp.concatenate([hyena[half].astype(BF16) for half in range(halves)], axis=1)
-    block = 512
-    for i in range(parts):
-        copies[1 + i].wait()
-        for c in range(0, width, block):
-            out_ref[i, :, pl.ds(c, block)] = jnp.dot(
-                left, weight[i, :, pl.ds(c, block)], preferred_element_type=F32
-            ).astype(BF16)
-
-
-def sum_body(parts_ref, out_ref):
-    total = parts_ref[0].astype(F32)
-    for i in range(1, parts_ref.shape[0]):
-        total = total + parts_ref[i].astype(F32)
-    out_ref[...] = total.astype(BF16)
+    for i in range(out_ref.shape[0]):
+        out_ref[i] = left
+
+
+def project_body(left_ref, weight_hbm, side_ref, half_ref, swap_side_ref, swap_half_ref, out_hbm, own, done, sems):
+    parts = left_ref.shape[0]
+    here = lax.axis_index("tp")
+    core = lax.axis_index("core")
+    blocks, _, block = done.shape
+    width = own.shape[1]
+    height = half_ref.shape[0]
+    fetched = pltpu.make_async_copy(weight_hbm.at[:, pl.ds(here * width, width)], own, sems.at[blocks])
+    fetched.start()
+    behind, ahead = lax.rem(here + parts - 1, parts), lax.rem(here + 1, parts)
+    across = lax.rem(here + 2, parts)
+    mine = pl.ds(pl.multiple_of(core * height, height), height)
+    mates = pl.ds(pl.multiple_of((1 - core) * height, height), height)
+    pairs = [
+        (left_ref[jnp.where(core == 0, behind, ahead)], side_ref),
+        (left_ref[jnp.where(core == 0, ahead, behind)], swap_side_ref),
+        (left_ref[across, :, mine], half_ref),
+        (left_ref[across, :, mates], swap_half_ref),
+        (left_ref[here], own),
+    ]
+    copies = []
+    for b in range(blocks):
+        at = pl.ds(b * block, block)
+        total = jnp.zeros(done.shape[1:], F32)
+        for left, right in pairs:
+            if b == 0 and right is own:
+                fetched.wait()
+            total += jnp.dot(left, right[:, at], preferred_element_type=F32)
+        done[b] = total.astype(BF16)
+        copies.append(pltpu.make_async_copy(done.at[b], out_hbm.at[:, at], sems.at[b]))
+        copies[-1].start()
+    for copy in copies:
+        copy.wait()
 
 
 def local(query_in, key_in, value_in, short_weight, residue, rate, skip, out_weight):
@@ -268,17 +307,27 @@
             pltpu.SemaphoreType.DMA((6,)),
         ],
     )(query_in, key_in, value_in, short_weight, rate, residue)
-    states, late, top = call(
+    states, late, top, *blocks = call(
         lambda *refs: join_body(rows, *refs),
-        [VMEM] * 5,
+        [VMEM] * 5 + [HBM],
         (
             shape((plane, modes, channels), BF16),
             shape((modes, channels), F32),
             shape((2, HEAD, channels), F32),
+            shape((channels, width), BF16),
+            shape((channels // 2, width), BF16),
         ),
         "join",
-        [pltpu.VMEM((3, 2 * HEAD, channels), F32)],
-    )(rims, heads, taps_here, rate, states)
+        [pltpu.VMEM((3, 2 * HEAD, channels), F32), pltpu.SemaphoreType.DMA((2,))],
+    )(rims, heads, taps_here, rate, states, out_weight)
+    side, half = blocks
+    cores = lax.axis_size("core")
+    places = [(c, t) for c in range(cores) for t in range(parts)]
+    side = lax.ppermute(
+        side, ("core", "tp"), [(c * parts + t, c * parts + (t + (1 if c == 0 else -1)) % parts) for c, t in places]
+    )
+    half = lax.ppermute(half, "tp", [(t, (t + 2) % parts) for t in range(parts)])
+    swapped = [lax.ppermute(x, "core", [(c, cores - 1 - c) for c in range(cores)]) for x in (side, half)]
     states = lax.all_to_all(states, ("y", "core"), 0, 0, tiled=True)
     before, totals = call(
         lambda *refs: plane_body(rows, *refs),
@@ -287,22 +336,32 @@
         "plane",
     )(states, rate)
     totals = lax.all_to_all(totals, "z", 0, 0, tiled=True)
-    partial = call(
+    hyena = call(
         lambda *refs: mix_body(taps, rows * plane, *refs),
-        [VMEM] * 9 + [HBM] * 2,
-        shape((parts, rows, width), BF16),
+        [VMEM] * 9 + [HBM],
+        shape((parts, rows, channels), BF16),
         "mix",
         [
             pltpu.VMEM(by_half, F32),
             pltpu.VMEM((2, modes, channels), F32),
             pltpu.VMEM((1, channels), F32),
-            pltpu.VMEM((parts, channels, width), BF16),
-            pltpu.SemaphoreType.DMA((1 + parts,)),
+            pltpu.SemaphoreType.DMA((1,)),
         ],
-        8,
-    )(queries, gated, begin, late, top, before, totals, rate, amplitude, skip, out_weight)
-    partial = lax.all_to_all(partial, "tp", 0, 0, tiled=True)
-    return call(sum_body, [VMEM], shape((rows, width), BF16), "total")(partial)
+    )(queries, gated, begin, late, top, before, totals, rate, amplitude, skip)
+    hyena = lax.all_to_all(hyena, "tp", 0, 0, tiled=True)
+    block = 256
+    return call(
+        project_body,
+        [VMEM, HBM] + [VMEM] * 4,
+        shape((rows, width), BF16),
+        "project",
+        [
+            pltpu.VMEM((channels, width), BF16),
+            pltpu.VMEM((width // block, rows, block), BF16),
+            pltpu.SemaphoreType.DMA((width // block + 1,)),
+        ],
+        out_spec=HBM,
+    )(hyena, out_weight, side, half, *swapped)
 
 
 def solution(mesh):

time: 62.9 us -> 62.5 us (level)
  blocking collectives: 49.6 us -> 0 us
  starting transfers between devices: 4.59 us -> 36.5 us
  waiting for transfers between devices: 2.61 us -> 16.1 us
  Pallas kernels: 5.41 us -> 8.95 us
    all_to_all x3 -> x0, blocking collectives: 49.6 us -> none  [the longest x1 17.3 us: local(): totals = lax.all_to_all(totals, 'z', 0, 0, tiled=True)]
    all_to_all x0 -> x3, starting transfers between devices: none -> 21.4 us  [the longest x1 10 us: local(): totals = lax.all_to_all(totals, 'z', 0, 0, tiled=True)]
    all_to_all x0 -> x3, waiting for transfers between devices: none -> 13.5 us  [the longest x1 5.53 us: local(): hyena = lax.all_to_all(hyena, 'tp', 0, 0, tiled=True)]
    ppermute x0 -> x4, starting transfers between devices: none -> 10.5 us  [the longest x1 4.38 us: local(): lax.ppermute(half, 'tp', [(t, (t + 2) % parts) for t in range(parts)])]
    pallas_call x2, Pallas kernels: 0.9 us -> 4.08 us  [the longest x1 2.28 us: local(): call(project_body, [VMEM, HBM] + [VMEM] * 4, shape((rows, width), BF16),...]
  transfers between devices with their start and end apart: 1 -> 8, of which waited for: 1 -> 4; matrix products, arithmetic and copies ran while one was open for 0% -> 0% of each run, Pallas kernels for 3% -> 7%
where the time goes in v5:
time: 62.5 us; the launch traced here: 61.6 us
  starting transfers between devices  36.5 us (58%)
  waiting for transfers between devices  16.1 us (26%)
  Pallas kernels  8.95 us (14%)
    all_to_all x1, starting transfers between devices, local(): totals = lax.all_to_all(totals, 'z', 0, 0, tiled=True)  10 us
    all_to_all x1, starting transfers between devices, local(): states = lax.all_to_all(states, ('y', 'core'), 0, 0, tiled=True)  7.62 us
    all_to_all x1, waiting for transfers between devices, local(): hyena = lax.all_to_all(hyena, 'tp', 0, 0, tiled=True)  5.53 us
    all_to_all x1, waiting for transfers between devices, local(): totals = lax.all_to_all(totals, 'z', 0, 0, tiled=True)  5.5 us
    ppermute x1, starting transfers between devices, local(): rims = lax.ppermute(rims, order, [(i, i + 1) for i in range(devices - 1)])  4.59 us
    ppermute x1, starting transfers between devices, local(): lax.ppermute(half, 'tp', [(t, (t + 2) % parts) for t in range(parts)])  4.38 us
    ppermute x2, starting transfers between devices, local(): lax.ppermute(x, 'core', [(c, cores - 1 - c) for c in range(cores)])  4.19 us
    all_to_all x1, starting transfers between devices, local(): hyena = lax.all_to_all(hyena, 'tp', 0, 0, tiled=True)  3.73 us
  transfers between devices with their start and end apart: 8, of which 4 were waited for; matrix products, arithmetic and copies ran while one was open for 0% of the time, Pallas kernels for 7%

profile of v5, /device:TPU:1, one launch (start us, length us, event | category | flops | bytes accessed | tf_op | source)
XLA Modules:
  0.0 61.6 jit_solution(4336443860033897148)
XLA Ops:
  0.0 0.8 %rims.1 = bf16[48,256]{1,0:T(8,128)(2,1)S(1)} custom-call(bf16[128,256]{1,0:T(8,128)(2,1)} %q_ref.1, bf16[128,256]{1,0:T(8,128)(2,1)} %k_ref.1, bf16[128,256]{1,0:T(8,128)(2,1)} %v_ref.1), custom_call_target="tpu_custom_call" | custom-call | tf_op jit(solution)/shard_map/rims/pallas_call | solution.py:285
  0.8 4.6 %collective-permute-start = (bf16[48,256]{1,0:T(8,128)(2,1)S(1)}, bf16[48,256]{1,0:T(8,128)(2,1)S(1)}, u32[]{:S(2)}, u32[]{:S(2)}) collective-permute-start(bf16[48,256]{1,0:T(8,128)(2,1)S(1)} %rims.1), channel_id=1, source_target_pairs={{0,4},{4,8},{8,12},{12,16},{16,20},{20,24},{24,28},{28,32},{32,36}... | collective-permute-start | bytes 73736 | tf_op jit(solution)/shard_map/ppermute | solution.py:288
  5.4 1.6 %gate.1 = (f32[2,128,128]{2,1,0:T(8,128)S(1)}, f32[2,128,128]{2,1,0:T(8,128)S(1)}, f32[16,8,256]{2,1,0:T(8,128)S(1)}, f32[16,256]{1,0:T(8,128)S(1)}, f32[3,8,256...) custom-call(bf16[128,256]{1,0:T(8,128)(2,1)} %q_ref.1, ...), custom_call_target="tpu_custom_call" | custom-call | tf_op jit(solution)/shard_map/gate/pallas_call | solution.py:289
  7.0 2.6 %collective-permute-done.refs_0_ = bf16[48,256]{1,0:T(8,128)(2,1)S(1)} collective-permute-done((bf16[48,256]{1,0:T(8,128)(2,1)S(1)}, bf16[48,256]{1,0:T(8,128)(2,1)S(1)}, u32[]{:S(2)}, u32[]{:S(2)}) %collective-permute-start) | collective-permute-done | bytes 24608 | tf_op jit(solution)/shard_map/ppermute | solution.py:288
  9.6 1.8 %join.1 = (bf16[16,16,256]{2,1,0:T(8,128)(2,1)}, f32[16,256]{1,0:T(8,128)S(1)}, f32[2,8,256]{2,1,0:T(8,128)S(1)}, bf16[256,1024]{1,0:T(8,128)(2,1)S(1)}, bf16[128,1024]{1,0:T(8,128)(2,1)S(1)}) custom-call(bf16[48,256]{1,0:T(8,128)(2,1)S(1)} %collective-permute-done.refs_0_, f32[3,8,256]{2,1,0:T(8,128)S(1)} %get-tuple-element.23.refs_1_, ...), custom_call_target="tpu_custom_call" | custom-call | tf_op jit(solution)/shard_map/join/pallas_call | solution.py:310
  11.4 1.9 %collective-permute-start.1 = (bf16[256,1024]{1,0:T(8,128)(2,1)S(1)}, bf16[256,1024]{1,0:T(8,128)(2,1)S(1)}, u32[]{:S(2)}, u32[]{:S(2)}) collective-permute-start(bf16[256,1024]{1,0:T(8,128)(2,1)S(1)} %get-tuple-element.33), channel_id=1, source_target_pairs={{0,1},{1,2},{2,3},{3,0},{4,7},{5,4},{6,5},{7,6},{8,9},{9,10},{10,1... | collective-permute-start | bytes 1572872 | tf_op jit(solution)/shard_map/ppermute | solution.py:326
  13.3 7.6 %all-to-all-start = ((bf16[16,16,256]{2,1,0:T(8,128)(2,1)}), bf16[16,16,256]{2,1,0:T(8,128)(2,1)S(1)}, u32[]{:S(2)}, u32[]{:S(2)}) async-start(bf16[16,16,256]{2,1,0:T(8,128)(2,1)} %get-tuple-element.29), calls=%async_computation | async-start | bytes 262144 | tf_op jit(solution)/shard_map/all_to_all | solution.py:331
  21.0 4.4 %collective-permute-start.2 = (bf16[128,1024]{1,0:T(8,128)(2,1)S(1)}, bf16[128,1024]{1,0:T(8,128)(2,1)S(1)}, u32[]{:S(2)}, u32[]{:S(2)}) collective-permute-start(bf16[128,1024]{1,0:T(8,128)(2,1)S(1)} %get-tuple-element.34), channel_id=1, source_target_pairs={{0,2},{1,3},{2,0},{3,1},{4,6},{5,7},{6,4},{7,5},{8,10},{9,11},{10,... | collective-permute-start | bytes 786440 | tf_op jit(solution)/shard_map/ppermute | solution.py:329
  25.4 0.0 collective-permute-done.1.side_ref
  25.4 2.3 %collective-permute-start.3 = (bf16[256,1024]{1,0:T(8,128)(2,1)S(1)}, bf16[256,1024]{1,0:T(8,128)(2,1)S(1)}, u32[]{:S(2)}, u32[]{:S(2)}) collective-permute-start(bf16[256,1024]{1,0:T(8,128)(2,1)S(1)} %collective-permute-done.1.side_ref), channel_id=1, source_target_pairs={{0,4},{4,0},{1,5},{5,1},{2,6},{6,2},{3,7},{7,3},{8,12},{12,8},{9,1... | collective-permute-start | bytes 1572872 | tf_op jit(solution)/shard_map/ppermute | solution.py:330
  27.6 2.5 %all-to-all-done.refs_0_ = bf16[16,16,256]{2,1,0:T(8,128)(2,1)S(1)} async-done(((bf16[16,16,256]{2,1,0:T(8,128)(2,1)}), bf16[16,16,256]{2,1,0:T(8,128)(2,1)S(1)}, u32[]{:S(2)}, u32[]{:S(2)}) %all-to-all-start) | async-done | bytes 131104 | tf_op jit(solution)/shard_map/all_to_all | solution.py:331
  30.1 0.7 %plane.1 = (f32[16,256]{1,0:T(8,128)S(1)}, bf16[8,16,256]{2,1,0:T(8,128)(2,1)}) custom-call(bf16[16,16,256]{2,1,0:T(8,128)(2,1)S(1)} %all-to-all-done.refs_0_, f32[16,256]{1,0:T(8,128)S(1)} %get-tuple-element.25.refs_3_.refs_1_.refs_7_), custom_call_target="tpu_custom_call" | custom-call | tf_op jit(solution)/shard_map/plane/pallas_call | solution.py:332
  30.8 10.0 %all-to-all-start.1 = ((bf16[8,16,256]{2,1,0:T(8,128)(2,1)}), bf16[8,16,256]{2,1,0:T(8,128)(2,1)S(1)}, u32[]{:S(2)}, u32[]{:S(2)}) async-start(bf16[8,16,256]{2,1,0:T(8,128)(2,1)} %get-tuple-element.31), calls=%async_computation.1 | async-start | bytes 131072 | tf_op jit(solution)/shard_map/all_to_all | solution.py:338
  40.9 0.0 collective-permute-done.2.half_ref
  40.9 1.9 %collective-permute-start.4 = (bf16[128,1024]{1,0:T(8,128)(2,1)S(1)}, bf16[128,1024]{1,0:T(8,128)(2,1)S(1)}, u32[]{:S(2)}, u32[]{:S(2)}) collective-permute-start(bf16[128,1024]{1,0:T(8,128)(2,1)S(1)} %collective-permute-done.2.half_ref), channel_id=1, source_target_pairs={{0,4},{4,0},{1,5},{5,1},{2,6},{6,2},{3,7},{7,3},{8,12},{12,8},{9,1... | collective-permute-start | bytes 786440 | tf_op jit(solution)/shard_map/ppermute | solution.py:330
  42.8 5.5 %all-to-all-done.1.refs_6_ = bf16[8,16,256]{2,1,0:T(8,128)(2,1)S(1)} async-done(((bf16[8,16,256]{2,1,0:T(8,128)(2,1)}), bf16[8,16,256]{2,1,0:T(8,128)(2,1)S(1)}, u32[]{:S(2)}, u32[]{:S(2)}) %all-to-all-start.1) | async-done | bytes 65568 | tf_op jit(solution)/shard_map/all_to_all | solution.py:338
  48.3 1.8 %mix.1 = bf16[4,128,256]{2,1,0:T(8,128)(2,1)} custom-call(f32[2,128,128]{2,1,0:T(8,128)S(1)} %get-tuple-element.20.refs_0_, f32[2,128,128]{2,1,0:T(8,128)S(1)} %get-tuple-element.21.refs_1_, f32[16,8,256]{2,1,0:T(8,128)S(1)} %get-tuple-element.22.refs_2_, f32[16,256]{1,0:T(8,128)S(1)} %get-tuple-element.27.refs_3_, ...), custom_call_target="tpu_custom_call" | custom-call | tf_op jit(solution)/shard_map/mix/pallas_call | solution.py:339
  50.1 3.7 %all-to-all-start.2 = ((bf16[4,128,256]{2,1,0:T(8,128)(2,1)}), bf16[4,128,256]{2,1,0:T(8,128)(2,1)S(1)}, u32[]{:S(2)}, u32[]{:S(2)}) async-start(bf16[4,128,256]{2,1,0:T(8,128)(2,1)} %mix.1), calls=%async_computation.2 | async-start | bytes 524288 | tf_op jit(solution)/shard_map/all_to_all | solution.py:351
  53.8 0.0 collective-permute-done.4.swap_half_ref
  53.8 5.5 %all-to-all-done.2.left_ref = bf16[4,128,256]{2,1,0:T(8,128)(2,1)S(1)} async-done(((bf16[4,128,256]{2,1,0:T(8,128)(2,1)}), bf16[4,128,256]{2,1,0:T(8,128)(2,1)S(1)}, u32[]{:S(2)}, u32[]{:S(2)}) %all-to-all-start.2) | async-done | bytes 262176 | tf_op jit(solution)/shard_map/all_to_all | solution.py:351
  59.4 0.0 collective-permute-done.3.swap_side_ref
  59.4 2.3 %project.1 = bf16[128,1024]{1,0:T(8,128)(2,1)} custom-call(bf16[4,128,256]{2,1,0:T(8,128)(2,1)S(1)} %all-to-all-done.2.left_ref, bf16[256,4096]{1,0:T(8,128)(2,1)} %weight_hbm.1, bf16[256,1024]{1,0:T(8,128)(2,1)S(1)} %collective-permute-done.1.side_ref, bf16[128,1024]{1,0:T(8,128)(2,1)S(1)} %collective-permute-done.2.half_ref, ...), custom_call_target="tpu_custom_call" | custom-call | tf_op jit(solution)/shard_map/project/pallas_call | solution.py:353
Async XLA Ops:
  0.8 8.8 %collective-permute-start = (bf16[48,256]{1,0:T(8,128)(2,1)S(1)}, bf16[48,256]{1,0:T(8,128)(2,1)S(1)}, u32[]{:S(2)}, u32[]{:S(2)}) collective-permute-start(bf16[48,256]{1,0:T(8,128)(2,1)S(1)} %rims.1), channel_id=1, source_target_pairs={{0,4},{4,8},{8,12},{12,16},{16,20},{20,24},{24,28},{28,32},{32,36}... | collective-permute-start | bytes 73736 | tf_op jit(solution)/shard_map/ppermute | solution.py:288
  11.4 13.9 %collective-permute-start.1 = (bf16[256,1024]{1,0:T(8,128)(2,1)S(1)}, bf16[256,1024]{1,0:T(8,128)(2,1)S(1)}, u32[]{:S(2)}, u32[]{:S(2)}) collective-permute-start(bf16[256,1024]{1,0:T(8,128)(2,1)S(1)} %get-tuple-element.33), channel_id=1, source_target_pairs={{0,1},{1,2},{2,3},{3,0},{4,7},{5,4},{6,5},{7,6},{8,9},{9,10},{10,1... | collective-permute-start | bytes 1572872 | tf_op jit(solution)/shard_map/ppermute | solution.py:326
  13.3 16.8 %all-to-all-start = ((bf16[16,16,256]{2,1,0:T(8,128)(2,1)}), bf16[16,16,256]{2,1,0:T(8,128)(2,1)S(1)}, u32[]{:S(2)}, u32[]{:S(2)}) async-start(bf16[16,16,256]{2,1,0:T(8,128)(2,1)} %get-tuple-element.29), calls=%async_computation | async-start | bytes 262144 | tf_op jit(solution)/shard_map/all_to_all | solution.py:331
  21.0 19.9 %collective-permute-start.2 = (bf16[128,1024]{1,0:T(8,128)(2,1)S(1)}, bf16[128,1024]{1,0:T(8,128)(2,1)S(1)}, u32[]{:S(2)}, u32[]{:S(2)}) collective-permute-start(bf16[128,1024]{1,0:T(8,128)(2,1)S(1)} %get-tuple-element.34), channel_id=1, source_target_pairs={{0,2},{1,3},{2,0},{3,1},{4,6},{5,7},{6,4},{7,5},{8,10},{9,11},{10,... | collective-permute-start | bytes 786440 | tf_op jit(solution)/shard_map/ppermute | solution.py:329
  25.4 34.0 %collective-permute-start.3 = (bf16[256,1024]{1,0:T(8,128)(2,1)S(1)}, bf16[256,1024]{1,0:T(8,128)(2,1)S(1)}, u32[]{:S(2)}, u32[]{:S(2)}) collective-permute-start(bf16[256,1024]{1,0:T(8,128)(2,1)S(1)} %collective-permute-done.1.side_ref), channel_id=1, source_target_pairs={{0,4},{4,0},{1,5},{5,1},{2,6},{6,2},{3,7},{7,3},{8,12},{12,8},{9,1... | collective-permute-start | bytes 1572872 | tf_op jit(solution)/shard_map/ppermute | solution.py:330
  30.8 17.5 %all-to-all-start.1 = ((bf16[8,16,256]{2,1,0:T(8,128)(2,1)}), bf16[8,16,256]{2,1,0:T(8,128)(2,1)S(1)}, u32[]{:S(2)}, u32[]{:S(2)}) async-start(bf16[8,16,256]{2,1,0:T(8,128)(2,1)} %get-tuple-element.31), calls=%async_computation.1 | async-start | bytes 131072 | tf_op jit(solution)/shard_map/all_to_all | solution.py:338
  40.9 13.0 %collective-permute-start.4 = (bf16[128,1024]{1,0:T(8,128)(2,1)S(1)}, bf16[128,1024]{1,0:T(8,128)(2,1)S(1)}, u32[]{:S(2)}, u32[]{:S(2)}) collective-permute-start(bf16[128,1024]{1,0:T(8,128)(2,1)S(1)} %collective-permute-done.2.half_ref), channel_id=1, source_target_pairs={{0,4},{4,0},{1,5},{5,1},{2,6},{6,2},{3,7},{7,3},{8,12},{12,8},{9,1... | collective-permute-start | bytes 786440 | tf_op jit(solution)/shard_map/ppermute | solution.py:330
  50.1 9.3 %all-to-all-start.2 = ((bf16[4,128,256]{2,1,0:T(8,128)(2,1)}), bf16[4,128,256]{2,1,0:T(8,128)(2,1)S(1)}, u32[]{:S(2)}, u32[]{:S(2)}) async-start(bf16[4,128,256]{2,1,0:T(8,128)(2,1)} %mix.1), calls=%async_computation.2 | async-start | bytes 524288 | tf_op jit(solution)/shard_map/all_to_all | solution.py:351

commit v6 on v4

--- a/solution.py
+++ b/solution.py
@@ -19,14 +19,16 @@
 
 
 VMEM = pl.BlockSpec(memory_space=pltpu.VMEM)
+ANY = pl.BlockSpec(memory_space=pl.ANY)
 HBM = pl.BlockSpec(memory_space=pltpu.HBM)
 
 
-def call(body, specs, outs, name, scratch=(), mib=4):
+def call(body, specs, outs, name, scratch=(), mib=4, out_spec=VMEM, aliases=None):
     return pl.pallas_call(
         body,
         in_specs=specs,
-        out_specs=jax.tree.map(lambda _: VMEM, outs),
+        out_specs=out_spec if isinstance(out_spec, tuple) else jax.tree.map(lambda _: out_spec, outs),
+        input_output_aliases=aliases or {},
         out_shape=outs,
         scratch_shapes=list(scratch),
         compiler_params=pltpu.CompilerParams(vmem_limit_bytes=mib * MIB),
@@ -69,8 +71,8 @@
 
 
 def gate_body(
-    q_hbm, k_hbm, v_hbm, taps_hbm, rate_hbm, residue_hbm, weight_hbm,
-    query_ref, gated_ref, begin_ref, state_ref, head_ref, taps_ref, rate_ref, amp_ref, *rest,
+    q_hbm, k_hbm, v_hbm, taps_hbm, rate_hbm, residue_hbm, skip_hbm, weight_hbm,
+    query_ref, gated_ref, begin_ref, state_ref, head_ref, taps_ref, rate_ref, amp_ref, skip_ref, *rest,
 ):
     *blocks, streams, residue_ref, pad, sems = rest
     here, parts = lax.axis_index("tp"), lax.axis_size("tp")
@@ -80,14 +82,14 @@
     taps = taps_ref.shape[1]
     steps = rows // SUBS
     copies = fetch(
-        (q_hbm, k_hbm, v_hbm, taps_hbm, rate_hbm, residue_hbm),
-        (streams.at[0], streams.at[1], streams.at[2], taps_ref, rate_ref, residue_ref),
+        (q_hbm, k_hbm, v_hbm, taps_hbm, rate_hbm, residue_hbm, skip_hbm),
+        (streams.at[0], streams.at[1], streams.at[2], taps_ref, rate_ref, residue_ref, skip_ref),
         sems,
     )
     sent = fetch(
         [weight_hbm.at[:, pl.ds(lax.rem(here + d, parts) * width, width)] for d in range(1, parts)],
         blocks,
-        sems.at[pl.ds(6, parts - 1)],
+        sems.at[pl.ds(7, parts - 1)],
     )
     for copy in copies:
         copy.wait()
@@ -171,12 +173,14 @@
 
 def mix_body(
     taps, plane_rows, query_ref, gated_ref, begin_ref, late_ref, top_ref, before_ref, planes_ref, rate_ref, amp_ref,
-    skip_hbm, out_ref, hyena, carry, skip_ref, sems,
+    skip_ref, weight_hbm, out_ref, own_ref, hyena, carry, sem,
 ):
     halves, rows, _ = query_ref.shape
     modes = rate_ref.shape[0]
     steps = rows // SUBS
-    copies = fetch([skip_hbm], [skip_ref], sems)
+    width = own_ref.shape[1]
+    own = pltpu.make_async_copy(weight_hbm.at[:, pl.ds(lax.axis_index("tp") * width, width)], own_ref, sem)
+    own.start()
     z = lax.axis_index("z")
     me = lax.axis_index("y") * lax.axis_size("core") + lax.axis_index("core")
     rate = rate_ref[...]
@@ -189,7 +193,6 @@
     carry[1] = carried + jnp.exp((taps - 1) * rate) * late_ref[...]
     sub = lax.broadcasted_iota(jnp.int32, (SUBS, LANES), 0)
     ahead = sub.astype(F32) * float(steps)
-    copies[0].wait()
     for half in range(halves):
         lanes = pl.ds(half * LANES, LANES)
         rates = [row_of(rate_ref, m, lanes) for m in range(modes)]
@@ -217,27 +220,27 @@
     left = jnp.concatenate([hyena[half].astype(BF16) for half in range(halves)], axis=1)
     for i in range(out_ref.shape[0]):
         out_ref[i] = left
-
-
-def project_body(left_ref, weight_hbm, *rest):
-    *others, out_ref, own, sem = rest
-    parts, _, _ = left_ref.shape
-    width = out_ref.shape[1]
+    own.wait()
+
+
+def project_body(left_ref, own_ref, *rest):
+    *others, out_hbm, done, sems = rest
+    parts = left_ref.shape[0]
     here = lax.axis_index("tp")
-    copy = pltpu.make_async_copy(weight_hbm.at[:, pl.ds(here * width, width)], own, sem)
-    copy.start()
-    block = 512
-    for c in range(0, width, block):
-        at = pl.ds(c, block)
-        total = jnp.zeros((out_ref.shape[0], block), F32)
+    blocks, _, block = done.shape
+    copies = []
+    for b in range(blocks):
+        at = pl.ds(b * block, block)
+        total = jnp.dot(left_ref[here], own_ref[:, at], preferred_element_type=F32)
         for d in range(1, parts):
             total += jnp.dot(
                 left_ref[lax.rem(here + parts - d, parts)], others[d - 1][:, at], preferred_element_type=F32
             )
-        if c == 0:
-            copy.wait()
-        total += jnp.dot(left_ref[here], own[:, at], preferred_element_type=F32)
-        out_ref[:, at] = total.astype(BF16)
+        done[b] = total.astype(BF16)
+        copies.append(pltpu.make_async_copy(done.at[b], out_hbm.at[:, at], sems.at[b]))
+        copies[-1].start()
+    for copy in copies:
+        copy.wait()
 
 
 def local(query_in, key_in, value_in, short_weight, residue, rate, skip, out_weight):
@@ -260,9 +263,9 @@
         rim_body, [HBM] * 3, shape((3 * RIM, channels), BF16), "rims", [pltpu.SemaphoreType.DMA((3,))]
     )(query_in, key_in, value_in)
     rims = lax.ppermute(rims, order, [(i, i + 1) for i in range(devices - 1)])
-    queries, gated, begin, states, heads, taps_here, rate, amplitude, *blocks = call(
+    queries, gated, begin, states, heads, taps_here, rate, amplitude, skip, *blocks = call(
         gate_body,
-        [HBM] * 7,
+        [HBM] * 8,
         (
             shape(by_half, F32),
             shape(by_half, F32),
@@ -272,6 +275,7 @@
             shape(short_weight.shape, F32),
             shape((modes, channels), F32),
             shape((modes, channels), F32),
+            shape((1, channels), F32),
             *[shape((channels, width), BF16)] * (parts - 1),
         ),
         "gate",
@@ -279,9 +283,9 @@
             pltpu.VMEM((3, rows, channels), BF16),
             pltpu.VMEM((modes, channels), F32),
             pltpu.VMEM((3, HEAD + rows, channels), F32),
-            pltpu.SemaphoreType.DMA((6 + parts - 1,)),
+            pltpu.SemaphoreType.DMA((7 + parts - 1,)),
         ],
-    )(query_in, key_in, value_in, short_weight, rate, residue, out_weight)
+    )(query_in, key_in, value_in, short_weight, rate, residue, skip, out_weight)
     blocks = [
         lax.ppermute(block, "tp", [(i, (i + d) % parts) for i in range(parts)])
         for d, block in enumerate(blocks, start=1)
@@ -305,26 +309,27 @@
         "plane",
     )(states, rate)
     totals = lax.all_to_all(totals, "z", 0, 0, tiled=True)
-    hyena = call(
+    hyena, own = call(
         lambda *refs: mix_body(taps, rows * plane, *refs),
-        [VMEM] * 9 + [HBM],
-        shape((parts, rows, channels), BF16),
+        [VMEM] * 10 + [HBM],
+        (shape((parts, rows, channels), BF16), shape((channels, width), BF16)),
         "mix",
         [
             pltpu.VMEM(by_half, F32),
             pltpu.VMEM((2, modes, channels), F32),
-            pltpu.VMEM((1, channels), F32),
-            pltpu.SemaphoreType.DMA((1,)),
+            pltpu.SemaphoreType.DMA,
         ],
-    )(queries, gated, begin, late, top, before, totals, rate, amplitude, skip)
+    )(queries, gated, begin, late, top, before, totals, rate, amplitude, skip, out_weight)
     hyena = lax.all_to_all(hyena, "tp", 0, 0, tiled=True)
+    block = 256
     return call(
         project_body,
-        [VMEM, HBM] + [VMEM] * (parts - 1),
+        [VMEM] * (2 + len(blocks)),
         shape((rows, width), BF16),
         "project",
-        [pltpu.VMEM((channels, width), BF16), pltpu.SemaphoreType.DMA],
-    )(hyena, out_weight, *blocks)
+        [pltpu.VMEM((width // block, rows, block), BF16), pltpu.SemaphoreType.DMA((width // block,))],
+        out_spec=HBM,
+    )(hyena, own, *blocks)
 
 
 def solution(mesh):

time: 59.9 us -> 58.9 us (0.983)
  Pallas kernels: 7.98 us -> 7.11 us
    pallas_call x3, Pallas kernels: 6.42 us -> 5.55 us  [the longest x1 2.65 us: local(): call(gate_body, [HBM] * 8, (shape(by_half, F32), shape(by_half, F32), sha...]
  transfers between devices with their start and end apart: 6 -> 6, of which waited for: 2 -> 2; matrix products, arithmetic and copies ran while one was open for 0% -> 0% of each run, Pallas kernels for 7% -> 8%
where the time goes in v6:
time: 58.9 us; the launch traced here: 58.4 us
  starting transfers between devices  25.5 us (43%)
  blocking collectives  18.5 us (31%)
  waiting for transfers between devices  7.2 us (12%)
  Pallas kernels  7.11 us (12%)
    all_to_all x1, blocking collectives, local(): totals = lax.all_to_all(totals, 'z', 0, 0, tiled=True)  18.5 us
    ppermute x3, starting transfers between devices, local(): lax.ppermute(block, 'tp', [(i, (i + d) % parts) for i in range(parts)])  11.4 us
    all_to_all x1, starting transfers between devices, local(): states = lax.all_to_all(states, ('y', 'core'), 0, 0, tiled=True)  8.75 us
    all_to_all x1, waiting for transfers between devices, local(): hyena = lax.all_to_all(hyena, 'tp', 0, 0, tiled=True)  6.61 us
    all_to_all x1, starting transfers between devices, local(): hyena = lax.all_to_all(hyena, 'tp', 0, 0, tiled=True)  3.42 us
    pallas_call x1, Pallas kernels, local(): call(gate_body, [HBM] * 8, (shape(by_half, F32), shape(by_half, F32), sha...  2.65 us
    ppermute x1, starting transfers between devices, local(): rims = lax.ppermute(rims, order, [(i, i + 1) for i in range(devices - 1)])  1.92 us
    pallas_call x1, Pallas kernels, local(): call(lambda *refs: mix_body(taps, rows * plane, *refs), [VMEM] * 10 + [HB...  1.76 us
  transfers between devices with their start and end apart: 6, of which 2 were waited for; matrix products, arithmetic and copies ran while one was open for 0% of the time, Pallas kernels for 8%

profile of v6, /device:TPU:8, one launch (start us, length us, event | category | flops | bytes accessed | tf_op | source)
XLA Modules:
  0.0 58.4 jit_solution(9489756967942124597)
XLA Ops:
  0.0 0.8 %rims.1 = bf16[48,256]{1,0:T(8,128)(2,1)S(1)} custom-call(bf16[128,256]{1,0:T(8,128)(2,1)} %q_ref.1, bf16[128,256]{1,0:T(8,128)(2,1)} %k_ref.1, bf16[128,256]{1,0:T(8,128)(2,1)} %v_ref.1), custom_call_target="tpu_custom_call" | custom-call | tf_op jit(solution)/shard_map/rims/pallas_call | solution.py:262
  0.8 1.9 %collective-permute-start = (bf16[48,256]{1,0:T(8,128)(2,1)S(1)}, bf16[48,256]{1,0:T(8,128)(2,1)S(1)}, u32[]{:S(2)}, u32[]{:S(2)}) collective-permute-start(bf16[48,256]{1,0:T(8,128)(2,1)S(1)} %rims.1), channel_id=1, source_target_pairs={{0,4},{4,8},{8,12},{12,16},{16,20},{20,24},{24,28},{28,32},{32,36}... | collective-permute-start | bytes 73736 | tf_op jit(solution)/shard_map/ppermute | solution.py:265
  2.7 2.6 %gate.1 = (f32[2,128,128]{2,1,0:T(8,128)S(1)}, f32[2,128,128]{2,1,0:T(8,128)S(1)}, f32[16,8,256]{2,1,0:T(8,128)S(1)}, f32[16,256]{1,0:T(8,128)S(1)}, f32[3,8,256...) custom-call(bf16[128,256]{1,0:T(8,128)(2,1)} %q_ref.1, ...), custom_call_target="tpu_custom_call" | custom-call | tf_op jit(solution)/shard_map/gate/pallas_call | solution.py:266
  5.3 0.6 collective-permute-done.refs_0_
  5.9 0.7 %join.1 = (bf16[16,16,256]{2,1,0:T(8,128)(2,1)}, f32[16,256]{1,0:T(8,128)S(1)}, f32[2,8,256]{2,1,0:T(8,128)S(1)}) custom-call(bf16[48,256]{1,0:T(8,128)(2,1)S(1)} %collective-permute-done.refs_0_, f32[3,8,256]{2,1,0:T(8,128)S(1)} %get-tuple-element.27.refs_1_, f32[3,7,256]{2,1,0:T(8,128)S(1)} %get-tuple-element.28.refs_2_, ...), custom_call_target="tpu_custom_call" | custom-call | tf_op jit(solution)/shard_map/join/pallas_call | solution.py:293
  6.7 8.8 %all-to-all-start = ((bf16[16,16,256]{2,1,0:T(8,128)(2,1)}), bf16[16,16,256]{2,1,0:T(8,128)(2,1)S(1)}, u32[]{:S(2)}, u32[]{:S(2)}) async-start(bf16[16,16,256]{2,1,0:T(8,128)(2,1)} %get-tuple-element.33), calls=%async_computation | async-start | bytes 262144 | tf_op jit(solution)/shard_map/all_to_all | solution.py:304
  15.4 3.4 %collective-permute-start.1 = (bf16[256,1024]{1,0:T(8,128)(2,1)}, bf16[256,1024]{1,0:T(8,128)(2,1)S(1)}, u32[]{:S(2)}, u32[]{:S(2)}) collective-permute-start(bf16[256,1024]{1,0:T(8,128)(2,1)} %get-tuple-element.40), channel_id=1, source_target_pairs={{0,1},{1,2},{2,3},{3,0},{4,5},{5,6},{6,7},{7,4},{8,9},{9,10},{10,1... | collective-permute-start | bytes 1572872 | tf_op jit(solution)/shard_map/ppermute | solution.py:290
  18.8 4.6 %collective-permute-start.2 = (bf16[256,1024]{1,0:T(8,128)(2,1)}, bf16[256,1024]{1,0:T(8,128)(2,1)S(1)}, u32[]{:S(2)}, u32[]{:S(2)}) collective-permute-start(bf16[256,1024]{1,0:T(8,128)(2,1)} %get-tuple-element.41), channel_id=1, source_target_pairs={{0,2},{1,3},{2,0},{3,1},{4,6},{5,7},{6,4},{7,5},{8,10},{9,11},{10,... | collective-permute-start | bytes 1572872 | tf_op jit(solution)/shard_map/ppermute | solution.py:290
  23.4 3.3 %collective-permute-start.3 = (bf16[256,1024]{1,0:T(8,128)(2,1)S(1)}, bf16[256,1024]{1,0:T(8,128)(2,1)S(1)}, u32[]{:S(2)}, u32[]{:S(2)}) collective-permute-start(bf16[256,1024]{1,0:T(8,128)(2,1)S(1)} %get-tuple-element.42), channel_id=1, source_target_pairs={{0,3},{1,0},{2,1},{3,2},{4,7},{5,4},{6,5},{7,6},{8,11},{9,8},{10,9... | collective-permute-start | bytes 1572872 | tf_op jit(solution)/shard_map/ppermute | solution.py:290
  26.8 0.0 all-to-all-done.refs_0_
  26.8 0.1 plane.1
  26.9 18.5 %all_to_all.15.refs_6_ = bf16[8,16,256]{2,1,0:T(8,128)(2,1)S(1)} all-to-all(bf16[8,16,256]{2,1,0:T(8,128)(2,1)S(1)} %get-tuple-element.35), channel_id=1, replica_groups=mesh['z'=8,'y'=8,'core'=2,'tp'=4] {'z'}, dimensions={0} | all-to-all | bytes 131072 | tf_op jit(solution)/shard_map/all_to_all | solution.py:311
  45.4 1.8 %mix.1 = (bf16[4,128,256]{2,1,0:T(8,128)(2,1)}, bf16[256,1024]{1,0:T(8,128)(2,1)S(1)}) custom-call(f32[2,128,128]{2,1,0:T(8,128)S(1)} %get-tuple-element.24.refs_0_, f32[2,128,128]{2,1,0:T(8,128)S(1)} %get-tuple-element.25.refs_1_, f32[16,8,256]{2,1,0:T(8,128)S(1)} %get-tuple-element.26.refs_2_, f32[16,256]{1,0:T(8,128)S(1)} %get-tuple-element.31.refs_3_, ...), custom_call_target="tpu_custom_call" | custom-call | tf_op jit(solution)/shard_map/mix/pallas_call | solution.py:312
  47.2 3.4 %all-to-all-start.2 = ((bf16[4,128,256]{2,1,0:T(8,128)(2,1)}), bf16[4,128,256]{2,1,0:T(8,128)(2,1)S(1)}, u32[]{:S(2)}, u32[]{:S(2)}) async-start(bf16[4,128,256]{2,1,0:T(8,128)(2,1)} %get-tuple-element.38), calls=%async_computation.2 | async-start | bytes 524288 | tf_op jit(solution)/shard_map/all_to_all | solution.py:323
  50.6 0.0 collective-permute-done.1.rest_0_
  50.6 0.0 collective-permute-done.2.rest_1_
  50.6 0.0 collective-permute-done.3.rest_2_
  50.6 6.6 %all-to-all-done.2.left_ref = bf16[4,128,256]{2,1,0:T(8,128)(2,1)S(1)} async-done(((bf16[4,128,256]{2,1,0:T(8,128)(2,1)}), bf16[4,128,256]{2,1,0:T(8,128)(2,1)S(1)}, u32[]{:S(2)}, u32[]{:S(2)}) %all-to-all-start.2) | async-done | bytes 262176 | tf_op jit(solution)/shard_map/all_to_all | solution.py:323
  57.2 1.1 %project.1 = bf16[128,1024]{1,0:T(8,128)(2,1)} custom-call(bf16[4,128,256]{2,1,0:T(8,128)(2,1)S(1)} %all-to-all-done.2.left_ref, bf16[256,1024]{1,0:T(8,128)(2,1)S(1)} %get-tuple-element.39.own_ref, bf16[256,1024]{1,0:T(8,128)(2,1)S(1)} %collective-permute-done.1.rest_0_, bf16[256,1024]{1,0:T(8,128)(2,1)S(1)} %collective-permute-done.2.rest_1_, ...), custom_call_target="tpu_custom_call" | custom-call | tf_op jit(solution)/shard_map/project/pallas_call | solution.py:325
Async XLA Ops:
  0.8 5.2 %collective-permute-start = (bf16[48,256]{1,0:T(8,128)(2,1)S(1)}, bf16[48,256]{1,0:T(8,128)(2,1)S(1)}, u32[]{:S(2)}, u32[]{:S(2)}) collective-permute-start(bf16[48,256]{1,0:T(8,128)(2,1)S(1)} %rims.1), channel_id=1, source_target_pairs={{0,4},{4,8},{8,12},{12,16},{16,20},{20,24},{24,28},{28,32},{32,36}... | collective-permute-start | bytes 73736 | tf_op jit(solution)/shard_map/ppermute | solution.py:265
  6.7 20.1 %all-to-all-start = ((bf16[16,16,256]{2,1,0:T(8,128)(2,1)}), bf16[16,16,256]{2,1,0:T(8,128)(2,1)S(1)}, u32[]{:S(2)}, u32[]{:S(2)}) async-start(bf16[16,16,256]{2,1,0:T(8,128)(2,1)} %get-tuple-element.33), calls=%async_computation | async-start | bytes 262144 | tf_op jit(solution)/shard_map/all_to_all | solution.py:304
  15.4 35.2 %collective-permute-start.1 = (bf16[256,1024]{1,0:T(8,128)(2,1)}, bf16[256,1024]{1,0:T(8,128)(2,1)S(1)}, u32[]{:S(2)}, u32[]{:S(2)}) collective-permute-start(bf16[256,1024]{1,0:T(8,128)(2,1)} %get-tuple-element.40), channel_id=1, source_target_pairs={{0,1},{1,2},{2,3},{3,0},{4,5},{5,6},{6,7},{7,4},{8,9},{9,10},{10,1... | collective-permute-start | bytes 1572872 | tf_op jit(solution)/shard_map/ppermute | solution.py:290
  18.8 31.8 %collective-permute-start.2 = (bf16[256,1024]{1,0:T(8,128)(2,1)}, bf16[256,1024]{1,0:T(8,128)(2,1)S(1)}, u32[]{:S(2)}, u32[]{:S(2)}) collective-permute-start(bf16[256,1024]{1,0:T(8,128)(2,1)} %get-tuple-element.41), channel_id=1, source_target_pairs={{0,2},{1,3},{2,0},{3,1},{4,6},{5,7},{6,4},{7,5},{8,10},{9,11},{10,... | collective-permute-start | bytes 1572872 | tf_op jit(solution)/shard_map/ppermute | solution.py:290
  23.4 27.2 %collective-permute-start.3 = (bf16[256,1024]{1,0:T(8,128)(2,1)S(1)}, bf16[256,1024]{1,0:T(8,128)(2,1)S(1)}, u32[]{:S(2)}, u32[]{:S(2)}) collective-permute-start(bf16[256,1024]{1,0:T(8,128)(2,1)S(1)} %get-tuple-element.42), channel_id=1, source_target_pairs={{0,3},{1,0},{2,1},{3,2},{4,7},{5,4},{6,5},{7,6},{8,11},{9,8},{10,9... | collective-permute-start | bytes 1572872 | tf_op jit(solution)/shard_map/ppermute | solution.py:290
  47.2 10.1 %all-to-all-start.2 = ((bf16[4,128,256]{2,1,0:T(8,128)(2,1)}), bf16[4,128,256]{2,1,0:T(8,128)(2,1)S(1)}, u32[]{:S(2)}, u32[]{:S(2)}) async-start(bf16[4,128,256]{2,1,0:T(8,128)(2,1)} %get-tuple-element.38), calls=%async_computation.2 | async-start | bytes 524288 | tf_op jit(solution)/shard_map/all_to_all | solution.py:323

commit v7 on v6

--- a/solution.py
+++ b/solution.py
@@ -12,6 +12,8 @@
 RIM = 16
 HEAD = 8
 MIB = 1 << 20
+RATE = 1.15e9
+EARLY = 3
 
 
 def shape(dims, dtype):
@@ -23,12 +25,13 @@
 HBM = pl.BlockSpec(memory_space=pltpu.HBM)
 
 
-def call(body, specs, outs, name, scratch=(), mib=4, out_spec=VMEM, aliases=None):
+def call(body, specs, outs, name, scratch=(), mib=4, out_spec=VMEM, aliases=None, us=0):
     return pl.pallas_call(
         body,
         in_specs=specs,
         out_specs=out_spec if isinstance(out_spec, tuple) else jax.tree.map(lambda _: out_spec, outs),
         input_output_aliases=aliases or {},
+        cost_estimate=pl.CostEstimate(flops=int(us * RATE), bytes_accessed=0, transcendentals=0) if us else None,
         out_shape=outs,
         scratch_shapes=list(scratch),
         compiler_params=pltpu.CompilerParams(vmem_limit_bytes=mib * MIB),
@@ -86,11 +89,28 @@
         (streams.at[0], streams.at[1], streams.at[2], taps_ref, rate_ref, residue_ref, skip_ref),
         sems,
     )
-    sent = fetch(
-        [weight_hbm.at[:, pl.ds(lax.rem(here + d, parts) * width, width)] for d in range(1, parts)],
-        blocks,
-        sems.at[pl.ds(7, parts - 1)],
-    )
+    is_early = lax.axis_index("z") < EARLY
+    views = [weight_hbm.at[:, pl.ds(lax.rem(here + d, parts) * width, width)] for d in range(1, parts)]
+    height = blocks[1].shape[0]
+    mine = pl.ds(pl.multiple_of(lax.axis_index("core") * height, height), height)
+    across = pltpu.make_async_copy(
+        weight_hbm.at[mine, pl.ds(lax.rem(here + 2, parts) * width, width)], blocks[1], sems.at[7]
+    )
+    across.start()
+
+    def sides(targets):
+        return [pltpu.make_async_copy(v, t, sems.at[8 + i]) for i, (v, t) in enumerate(zip(views[::2], targets))]
+
+    @pl.when(is_early)
+    def _():
+        for copy in sides((blocks[0], blocks[2])):
+            copy.start()
+
+    @pl.when(jnp.logical_not(is_early))
+    def _():
+        for copy in sides((blocks[3], blocks[4])):
+            copy.start()
+
     for copy in copies:
         copy.wait()
     amp_ref[...] = residue_ref[...] * jnp.sqrt(one_minus_exp(2.0 * rate_ref[...]))
@@ -127,11 +147,13 @@
                 s = s + jnp.where(sub >= d, drop * pltpu.roll(s, d, 0), 0.0)
             state_ref[pl.ds(m, 1), lanes] = s[SUBS - 1 :]
             begin_ref[m, :, lanes] = jnp.where(sub >= 1, pltpu.roll(s, 1, 0), 0.0)
-    for copy in sent:
+    across.wait()
+    for copy in sides((blocks[0], blocks[2])):
         copy.wait()
 
 
-def join_body(rows, rim_ref, head_ref, taps_ref, rate_ref, state_ref, out_ref, late_ref, top_ref, pad):
+def join_body(rows, rim_ref, head_ref, taps_ref, rate_ref, state_ref, *rest):
+    out_ref, late_ref, top_ref, pad = *rest[3:6], rest[-1]
     modes, channels = rate_ref.shape
     taps = taps_ref.shape[1]
     sums = []
@@ -157,7 +179,7 @@
         out_ref[i] = whole
 
 
-def plane_body(rows, parts_ref, rate_ref, before_ref, total_ref):
+def plane_body(rows, parts_ref, rate_ref, _a, _b, before_ref, total_ref, _same_a, _same_b):
     me = lax.axis_index("y") * lax.axis_size("core") + lax.axis_index("core")
     drop = jnp.exp(-rows * rate_ref[...])
     before = jnp.zeros(rate_ref.shape, F32)
@@ -173,7 +195,7 @@
 
 def mix_body(
     taps, plane_rows, query_ref, gated_ref, begin_ref, late_ref, top_ref, before_ref, planes_ref, rate_ref, amp_ref,
-    skip_ref, weight_hbm, out_ref, own_ref, hyena, carry, sem,
+    skip_ref, weight_hbm, _a, _b, _c, out_ref, own_ref, _same_a, _same_b, _same_c, hyena, carry, sem,
 ):
     halves, rows, _ = query_ref.shape
     modes = rate_ref.shape[0]
@@ -223,24 +245,60 @@
     own.wait()
 
 
-def project_body(left_ref, own_ref, *rest):
-    *others, out_hbm, done, sems = rest
+def project_body(
+    left_ref, own_ref, side_ref, half_ref, other_ref, late_side_ref, late_other_ref, other_half_ref, out_hbm, done, sems
+):
     parts = left_ref.shape[0]
     here = lax.axis_index("tp")
+    core = lax.axis_index("core")
     blocks, _, block = done.shape
-    copies = []
-    for b in range(blocks):
-        at = pl.ds(b * block, block)
-        total = jnp.dot(left_ref[here], own_ref[:, at], preferred_element_type=F32)
-        for d in range(1, parts):
-            total += jnp.dot(
-                left_ref[lax.rem(here + parts - d, parts)], others[d - 1][:, at], preferred_element_type=F32
-            )
-        done[b] = total.astype(BF16)
-        copies.append(pltpu.make_async_copy(done.at[b], out_hbm.at[:, at], sems.at[b]))
-        copies[-1].start()
-    for copy in copies:
-        copy.wait()
+    height = half_ref.shape[0]
+
+    def rows_of(core):
+        return pl.ds(pl.multiple_of(core * height, height), height)
+
+    def run(side, other):
+        across = left_ref.at[lax.rem(here + 2, parts)]
+        pairs = [
+            (left_ref[here], own_ref),
+            (left_ref[lax.rem(here + parts - 1, parts)], side),
+            (left_ref[lax.rem(here + 1, parts)], other),
+            (across[:, rows_of(core)], half_ref),
+            (across[:, rows_of(1 - core)], other_half_ref),
+        ]
+        copies = []
+        for b in range(blocks):
+            at = pl.ds(b * block, block)
+            total = jnp.zeros(done.shape[1:], F32)
+            for left, right in pairs:
+                total += jnp.dot(left, right[:, at], preferred_element_type=F32)
+            done[b] = total.astype(BF16)
+            copies.append(pltpu.make_async_copy(done.at[b], out_hbm.at[:, at], sems.at[b]))
+            copies[-1].start()
+        for copy in copies:
+            copy.wait()
+
+    early = lax.axis_index("z") < EARLY
+
+    @pl.when(early)
+    def _():
+        run(side_ref, other_ref)
+
+    @pl.when(jnp.logical_not(early))
+    def _():
+        run(late_side_ref, late_other_ref)
+
+
+def sent_on(block, d, planes):
+    parts = lax.axis_size("tp")
+    plane = lax.axis_size("y") * lax.axis_size("core")
+    route = [
+        ((z * plane + i) * parts + t, (z * plane + i) * parts + (t + d) % parts)
+        for z in planes
+        for i in range(plane)
+        for t in range(parts)
+    ]
+    return lax.ppermute(block, ("z", "y", "core", "tp"), route)
 
 
 def local(query_in, key_in, value_in, short_weight, residue, rate, skip, out_weight):
@@ -254,6 +312,7 @@
     order = ("z", "y", "core")
     devices = planes * plane
     by_half = (channels // LANES, rows, LANES)
+    block_shapes = [pltpu.HBM((r, width), BF16) for r in (channels, channels // 2, channels)]
     skip = skip.reshape(1, -1)
     query_in, key_in, value_in, short_weight, residue, rate, skip, out_weight = (
         pltpu.with_memory_space_constraint(x, pltpu.HBM)
@@ -276,60 +335,76 @@
             shape((modes, channels), F32),
             shape((modes, channels), F32),
             shape((1, channels), F32),
-            *[shape((channels, width), BF16)] * (parts - 1),
+            *block_shapes,
+            *block_shapes[::2],
         ),
         "gate",
         [
             pltpu.VMEM((3, rows, channels), BF16),
             pltpu.VMEM((modes, channels), F32),
             pltpu.VMEM((3, HEAD + rows, channels), F32),
-            pltpu.SemaphoreType.DMA((7 + parts - 1,)),
+            pltpu.SemaphoreType.DMA((10,)),
         ],
+        out_spec=(*[VMEM] * 9, *[HBM] * 5),
     )(query_in, key_in, value_in, short_weight, rate, residue, skip, out_weight)
-    blocks = [
-        lax.ppermute(block, "tp", [(i, (i + d) % parts) for i in range(parts)])
-        for d, block in enumerate(blocks, start=1)
-    ]
-    states, late, top = call(
+    begin = pltpu.with_memory_space_constraint(begin, pltpu.VMEM)
+    states, late, top, *blocks[:3] = call(
         lambda *refs: join_body(rows, *refs),
-        [VMEM] * 5,
+        [VMEM] * 5 + [ANY] * 3,
         (
             shape((plane, modes, channels), BF16),
             shape((modes, channels), F32),
             shape((2, HEAD, channels), F32),
+            *block_shapes,
         ),
         "join",
         [pltpu.VMEM((3, 2 * HEAD, channels), F32)],
-    )(rims, heads, taps_here, rate, states)
+        out_spec=(VMEM, VMEM, VMEM, *[ANY] * 3),
+        aliases={5 + i: 3 + i for i in range(3)},
+    )(rims, heads, taps_here, rate, states, *blocks[:3])
+    early = [sent_on(block, d, range(EARLY if d != 2 else planes)) for d, block in enumerate(blocks[:3], start=1)]
     states = lax.all_to_all(states, ("y", "core"), 0, 0, tiled=True)
-    before, totals = call(
+    before, totals, *blocks = call(
         lambda *refs: plane_body(rows, *refs),
-        [VMEM] * 2,
-        (shape((modes, channels), F32), shape((planes, modes, channels), BF16)),
+        [VMEM] * 2 + [ANY] * 2,
+        (
+            shape((modes, channels), F32),
+            shape((planes, modes, channels), BF16),
+            *block_shapes[::2],
+        ),
         "plane",
-    )(states, rate)
+        us=2,
+        out_spec=(VMEM, VMEM, ANY, ANY),
+        aliases={2: 2, 3: 3},
+    )(states, rate, *blocks[3:])
+    later = [sent_on(block, d, range(EARLY, planes)) for d, block in zip((1, 3), blocks)]
+    before = pltpu.with_memory_space_constraint(before, pltpu.VMEM)
     totals = lax.all_to_all(totals, "z", 0, 0, tiled=True)
-    hyena, own = call(
+    hyena, own, *early = call(
         lambda *refs: mix_body(taps, rows * plane, *refs),
-        [VMEM] * 10 + [HBM],
-        (shape((parts, rows, channels), BF16), shape((channels, width), BF16)),
+        [VMEM] * 10 + [HBM] + [ANY] * 3,
+        (shape((parts, rows, channels), BF16), shape((channels, width), BF16), *[shape(x.shape, BF16) for x in block_shapes]),
         "mix",
         [
             pltpu.VMEM(by_half, F32),
             pltpu.VMEM((2, modes, channels), F32),
             pltpu.SemaphoreType.DMA,
         ],
-    )(queries, gated, begin, late, top, before, totals, rate, amplitude, skip, out_weight)
+        out_spec=(VMEM, VMEM, ANY, ANY, ANY),
+        aliases={11: 2, 12: 3, 13: 4},
+        us=2,
+    )(queries, gated, begin, late, top, before, totals, rate, amplitude, skip, out_weight, *early)
+    other_half = lax.ppermute(early[1], "core", [(0, 1), (1, 0)])
     hyena = lax.all_to_all(hyena, "tp", 0, 0, tiled=True)
     block = 256
     return call(
         project_body,
-        [VMEM] * (2 + len(blocks)),
+        [VMEM] * 8,
         shape((rows, width), BF16),
         "project",
         [pltpu.VMEM((width // block, rows, block), BF16), pltpu.SemaphoreType.DMA((width // block,))],
         out_spec=HBM,
-    )(hyena, own, *blocks)
+    )(hyena, own, *early, *later, other_half)
 
 
 def solution(mesh):

time: 58.9 us -> 97 us (1.65)
  the two profiles are of different devices: /device:TPU:8 before, /device:TPU:1 now
where the time goes in v7:
time: 97 us; the launch traced here: 96.4 us
  Pallas kernels  45.4 us (47%)
  starting transfers between devices  34.6 us (36%)
  blocking collectives  10.3 us (11%)
  waiting for transfers between devices  6.06 us (6%)
    pallas_call x1, Pallas kernels, local(): call(gate_body, [HBM] * 8, (shape(by_half, F32), shape(by_half, F32), sha...  40.9 us
    ppermute x5, starting transfers between devices, sent_on(): return lax.ppermute(block, ('z', 'y', 'core', 'tp'), route)  10.8 us
    all_to_all x1, blocking collectives, local(): hyena = lax.all_to_all(hyena, 'tp', 0, 0, tiled=True)  10.3 us
    all_to_all x1, starting transfers between devices, local(): totals = lax.all_to_all(totals, 'z', 0, 0, tiled=True)  9.22 us
    all_to_all x1, starting transfers between devices, local(): states = lax.all_to_all(states, ('y', 'core'), 0, 0, tiled=True)  6.87 us
    ppermute x1, starting transfers between devices, local(): rims = lax.ppermute(rims, order, [(i, i + 1) for i in range(devices - 1)])  4.59 us
    all_to_all x1, waiting for transfers between devices, local(): totals = lax.all_to_all(totals, 'z', 0, 0, tiled=True)  3.92 us
    ppermute x1, starting transfers between devices, local(): other_half = lax.ppermute(early[1], 'core', [(0, 1), (1, 0)])  3.1 us
  transfers between devices with their start and end apart: 9, of which 2 were waited for; matrix products, arithmetic and copies ran while one was open for 0% of the time, Pallas kernels for 44%

profile of v7, /device:TPU:1, one launch (start us, length us, event | category | flops | bytes accessed | tf_op | source)
XLA Modules:
  0.0 96.4 jit_solution(18444150261772230770)
XLA Ops:
  0.0 0.8 rims.1
  0.8 4.6 %collective-permute-start = (bf16[48,256]{1,0:T(8,128)(2,1)S(1)}, bf16[48,256]{1,0:T(8,128)(2,1)S(1)}, u32[]{:S(2)}, u32[]{:S(2)}) collective-permute-start(bf16[48,256]{1,0:T(8,128)(2,1)S(1)} %rims.1), channel_id=1, source_target_pairs={{0,4},{4,8},{8,12},{12,16},{16,20},{20,24},{24,28},{28,32},{32,36}... | collective-permute-start | bytes 73736 | tf_op jit(solution)/shard_map/ppermute | solution.py:324
  5.4 40.9 %gate.1 = (f32[2,128,128]{2,1,0:T(8,128)S(1)}, f32[2,128,128]{2,1,0:T(8,128)S(1)}, f32[16,8,256]{2,1,0:T(8,128)S(1)}, f32[16,256]{1,0:T(8,128)S(1)}, f32[3,8,256...) custom-call(bf16[128,256]{1,0:T(8,128)(2,1)} %q_ref.1, ...), custom_call_target="tpu_custom_call" | custom-call | tf_op jit(solution)/shard_map/gate/pallas_call | solution.py:325
  46.3 0.0 collective-permute-done.refs_0_
  46.3 0.7 join.1
  47.0 6.9 %all-to-all-start = ((bf16[16,16,256]{2,1,0:T(8,128)(2,1)}), bf16[16,16,256]{2,1,0:T(8,128)(2,1)S(1)}, u32[]{:S(2)}, u32[]{:S(2)}) async-start(bf16[16,16,256]{2,1,0:T(8,128)(2,1)} %get-tuple-element.46), calls=%async_computation | async-start | bytes 262144 | tf_op jit(solution)/shard_map/all_to_all | solution.py:366
  53.9 2.6 %collective-permute-start.1 = (bf16[256,1024]{1,0:T(8,128)(2,1)}, bf16[256,1024]{1,0:T(8,128)(2,1)S(1)}, u32[]{:S(2)}, u32[]{:S(2)}) collective-permute-start(bf16[256,1024]{1,0:T(8,128)(2,1)} %get-tuple-element.53), channel_id=1, source_target_pairs={{0,1},{1,2},{2,3},{3,0},{4,5},{5,6},{6,7},{7,4},{8,9},{9,10},{10,1... | collective-permute-start | bytes 1572872 | tf_op jit(solution)/shard_map/ppermute | solution.py:301
  56.5 3.9 %collective-permute-start.3 = (bf16[256,1024]{1,0:T(8,128)(2,1)}, bf16[256,1024]{1,0:T(8,128)(2,1)S(1)}, u32[]{:S(2)}, u32[]{:S(2)}) collective-permute-start(bf16[256,1024]{1,0:T(8,128)(2,1)} %get-tuple-element.55), channel_id=1, source_target_pairs={{0,3},{1,0},{2,1},{3,2},{4,7},{5,4},{6,5},{7,6},{8,11},{9,8},{10,9... | collective-permute-start | bytes 1572872 | tf_op jit(solution)/shard_map/ppermute | solution.py:301
  60.4 2.9 %collective-permute-start.2 = (bf16[128,1024]{1,0:T(8,128)(2,1)}, bf16[128,1024]{1,0:T(8,128)(2,1)S(1)}, u32[]{:S(2)}, u32[]{:S(2)}) collective-permute-start(bf16[128,1024]{1,0:T(8,128)(2,1)} %get-tuple-element.54), channel_id=1, source_target_pairs={{0,2},{1,3},{2,0},{3,1},{4,6},{5,7},{6,4},{7,5},{8,10},{9,11},{10,... | collective-permute-start | bytes 786440 | tf_op jit(solution)/shard_map/ppermute | solution.py:301
  63.4 0.7 plane.1
  64.0 9.2 %all-to-all-start.1 = ((bf16[8,16,256]{2,1,0:T(8,128)(2,1)}), bf16[8,16,256]{2,1,0:T(8,128)(2,1)S(1)}, u32[]{:S(2)}, u32[]{:S(2)}) async-start(bf16[8,16,256]{2,1,0:T(8,128)(2,1)} %get-tuple-element.50), calls=%async_computation.1 | async-start | bytes 131072 | tf_op jit(solution)/shard_map/all_to_all | solution.py:382
  73.3 0.7 collective-permute-start.4
  74.0 0.7 collective-permute-start.5
  74.7 2.1 %collective-permute-done.2.refs_12_ = bf16[128,1024]{1,0:T(8,128)(2,1)S(1)} collective-permute-done((bf16[128,1024]{1,0:T(8,128)(2,1)}, bf16[128,1024]{1,0:T(8,128)(2,1)S(1)}, u32[]{:S(2)}, u32[]{:S(2)}) %collective-permute-start.2) | collective-permute-done | bytes 262176 | tf_op jit(solution)/shard_map/ppermute | solution.py:301
  76.8 3.9 %all-to-all-done.1.refs_6_ = bf16[8,16,256]{2,1,0:T(8,128)(2,1)S(1)} async-done(((bf16[8,16,256]{2,1,0:T(8,128)(2,1)}), bf16[8,16,256]{2,1,0:T(8,128)(2,1)S(1)}, u32[]{:S(2)}, u32[]{:S(2)}) %all-to-all-start.1) | async-done | bytes 65568 | tf_op jit(solution)/shard_map/all_to_all | solution.py:382
  80.7 0.0 collective-permute-done.1.refs_11_
  80.7 0.0 collective-permute-done.3.refs_13_
  80.7 1.1 %mix.1 = (bf16[4,128,256]{2,1,0:T(8,128)(2,1)S(1)}, bf16[256,1024]{1,0:T(8,128)(2,1)S(1)}, bf16[256,1024]{1,0:T(8,128)(2,1)S(1)}, bf16[128,1024]{1,0:T(8,128)(2,1)S(1)}, bf16[256,1024]{1,0:T(8,128)(2,1)S(1)}) custom-call(f32[2,128,128]{2,1,0:T(8,128)S(1)} %get-tuple-element.34.refs_0_, ...), custom_call_target="tpu_custom_call", output_to_operand_aliasing={{2}: (11, {}), {3}: (12, {}), {4}: (13, {})} | custom-call | flops 2300000000 | tf_op jit(solution)/shard_map/mix/pallas_call | solution.py:383
  81.8 3.1 %collective-permute-start.6 = (bf16[128,1024]{1,0:T(8,128)(2,1)S(1)}, bf16[128,1024]{1,0:T(8,128)(2,1)S(1)}, u32[]{:S(2)}, u32[]{:S(2)}) collective-permute-start(bf16[128,1024]{1,0:T(8,128)(2,1)S(1)} %get-tuple-element.59.half_ref), channel_id=1, source_target_pairs={{0,4},{4,0},{1,5},{5,1},{2,6},{6,2},{3,7},{7,3},{8,12},{12,8},{9,1... | collective-permute-start | bytes 786440 | tf_op jit(solution)/shard_map/ppermute | solution.py:397
  84.9 10.3 %all_to_all.15.left_ref = bf16[4,128,256]{2,1,0:T(8,128)(2,1)S(1)} all-to-all(bf16[4,128,256]{2,1,0:T(8,128)(2,1)S(1)} %get-tuple-element.56), channel_id=1, replica_groups=mesh['z'=8,'y'=8,'core'=2,'tp'=4] {'tp'}, dimensions={0} | all-to-all | bytes 524288 | tf_op jit(solution)/shard_map/all_to_all | solution.py:398
  95.2 0.0 collective-permute-done.4.late_side_ref
  95.2 0.0 collective-permute-done.5.late_other_ref
  95.2 0.0 collective-permute-done.6.other_half_ref
  95.2 1.2 %project.1 = bf16[128,1024]{1,0:T(8,128)(2,1)} custom-call(bf16[4,128,256]{2,1,0:T(8,128)(2,1)S(1)} %all_to_all.15.left_ref, bf16[256,1024]{1,0:T(8,128)(2,1)S(1)} %get-tuple-element.57.own_ref, bf16[256,1024]{1,0:T(8,128)(2,1)S(1)} %get-tuple-element.58.side_ref, bf16[128,1024]{1,0:T(8,128)(2,1)S(1)} %get-tuple-element.59.half_ref, ...), custom_call_target="tpu_custom_call" | custom-call | tf_op jit(solution)/shard_map/project/pallas_call | solution.py:400
  (1 shorter events, 0.0 us)
Async XLA Ops:
  0.8 45.6 %collective-permute-start = (bf16[48,256]{1,0:T(8,128)(2,1)S(1)}, bf16[48,256]{1,0:T(8,128)(2,1)S(1)}, u32[]{:S(2)}, u32[]{:S(2)}) collective-permute-start(bf16[48,256]{1,0:T(8,128)(2,1)S(1)} %rims.1), channel_id=1, source_target_pairs={{0,4},{4,8},{8,12},{12,16},{16,20},{20,24},{24,28},{28,32},{32,36}... | collective-permute-start | bytes 73736 | tf_op jit(solution)/shard_map/ppermute | solution.py:324
  47.0 16.3 %all-to-all-start = ((bf16[16,16,256]{2,1,0:T(8,128)(2,1)}), bf16[16,16,256]{2,1,0:T(8,128)(2,1)S(1)}, u32[]{:S(2)}, u32[]{:S(2)}) async-start(bf16[16,16,256]{2,1,0:T(8,128)(2,1)} %get-tuple-element.46), calls=%async_computation | async-start | bytes 262144 | tf_op jit(solution)/shard_map/all_to_all | solution.py:366
  53.9 26.8 %collective-permute-start.1 = (bf16[256,1024]{1,0:T(8,128)(2,1)}, bf16[256,1024]{1,0:T(8,128)(2,1)S(1)}, u32[]{:S(2)}, u32[]{:S(2)}) collective-permute-start(bf16[256,1024]{1,0:T(8,128)(2,1)} %get-tuple-element.53), channel_id=1, source_target_pairs={{0,1},{1,2},{2,3},{3,0},{4,5},{5,6},{6,7},{7,4},{8,9},{9,10},{10,1... | collective-permute-start | bytes 1572872 | tf_op jit(solution)/shard_map/ppermute | solution.py:301
  56.5 24.2 %collective-permute-start.3 = (bf16[256,1024]{1,0:T(8,128)(2,1)}, bf16[256,1024]{1,0:T(8,128)(2,1)S(1)}, u32[]{:S(2)}, u32[]{:S(2)}) collective-permute-start(bf16[256,1024]{1,0:T(8,128)(2,1)} %get-tuple-element.55), channel_id=1, source_target_pairs={{0,3},{1,0},{2,1},{3,2},{4,7},{5,4},{6,5},{7,6},{8,11},{9,8},{10,9... | collective-permute-start | bytes 1572872 | tf_op jit(solution)/shard_map/ppermute | solution.py:301
  60.4 16.4 %collective-permute-start.2 = (bf16[128,1024]{1,0:T(8,128)(2,1)}, bf16[128,1024]{1,0:T(8,128)(2,1)S(1)}, u32[]{:S(2)}, u32[]{:S(2)}) collective-permute-start(bf16[128,1024]{1,0:T(8,128)(2,1)} %get-tuple-element.54), channel_id=1, source_target_pairs={{0,2},{1,3},{2,0},{3,1},{4,6},{5,7},{6,4},{7,5},{8,10},{9,11},{10,... | collective-permute-start | bytes 786440 | tf_op jit(solution)/shard_map/ppermute | solution.py:301
  64.0 16.6 %all-to-all-start.1 = ((bf16[8,16,256]{2,1,0:T(8,128)(2,1)}), bf16[8,16,256]{2,1,0:T(8,128)(2,1)S(1)}, u32[]{:S(2)}, u32[]{:S(2)}) async-start(bf16[8,16,256]{2,1,0:T(8,128)(2,1)} %get-tuple-element.50), calls=%async_computation.1 | async-start | bytes 131072 | tf_op jit(solution)/shard_map/all_to_all | solution.py:382
  73.3 21.9 %collective-permute-start.4 = (bf16[256,1024]{1,0:T(8,128)(2,1)}, bf16[256,1024]{1,0:T(8,128)(2,1)S(1)}, u32[]{:S(2)}, u32[]{:S(2)}) collective-permute-start(bf16[256,1024]{1,0:T(8,128)(2,1)} %get-tuple-element.61), channel_id=1, source_target_pairs={{192,193},{193,194},{194,195},{195,192},{196,197},{197,198},{198,1... | collective-permute-start | bytes 1572872 | tf_op jit(solution)/shard_map/ppermute | solution.py:301
  74.0 21.3 %collective-permute-start.5 = (bf16[256,1024]{1,0:T(8,128)(2,1)}, bf16[256,1024]{1,0:T(8,128)(2,1)S(1)}, u32[]{:S(2)}, u32[]{:S(2)}) collective-permute-start(bf16[256,1024]{1,0:T(8,128)(2,1)} %get-tuple-element.62), channel_id=1, source_target_pairs={{192,195},{193,192},{194,193},{195,194},{196,199},{197,196},{198,1... | collective-permute-start | bytes 1572872 | tf_op jit(solution)/shard_map/ppermute | solution.py:301
  81.8 13.4 %collective-permute-start.6 = (bf16[128,1024]{1,0:T(8,128)(2,1)S(1)}, bf16[128,1024]{1,0:T(8,128)(2,1)S(1)}, u32[]{:S(2)}, u32[]{:S(2)}) collective-permute-start(bf16[128,1024]{1,0:T(8,128)(2,1)S(1)} %get-tuple-element.59.half_ref), channel_id=1, source_target_pairs={{0,4},{4,0},{1,5},{5,1},{2,6},{6,2},{3,7},{7,3},{8,12},{12,8},{9,1... | collective-permute-start | bytes 786440 | tf_op jit(solution)/shard_map/ppermute | solution.py:397

commit v8 on v6

--- a/solution.py
+++ b/solution.py
@@ -12,6 +12,7 @@
 RIM = 16
 HEAD = 8
 MIB = 1 << 20
+RATE = 1.15e9
 
 
 def shape(dims, dtype):
@@ -23,12 +24,13 @@
 HBM = pl.BlockSpec(memory_space=pltpu.HBM)
 
 
-def call(body, specs, outs, name, scratch=(), mib=4, out_spec=VMEM, aliases=None):
+def call(body, specs, outs, name, scratch=(), mib=4, out_spec=VMEM, aliases=None, us=0):
     return pl.pallas_call(
         body,
         in_specs=specs,
         out_specs=out_spec if isinstance(out_spec, tuple) else jax.tree.map(lambda _: out_spec, outs),
         input_output_aliases=aliases or {},
+        cost_estimate=pl.CostEstimate(flops=int(us * RATE), bytes_accessed=0, transcendentals=0) if us else None,
         out_shape=outs,
         scratch_shapes=list(scratch),
         compiler_params=pltpu.CompilerParams(vmem_limit_bytes=mib * MIB),
@@ -157,7 +159,7 @@
         out_ref[i] = whole
 
 
-def plane_body(rows, parts_ref, rate_ref, before_ref, total_ref):
+def plane_body(rows, parts_ref, rate_ref, _block, before_ref, total_ref, _same_block):
     me = lax.axis_index("y") * lax.axis_size("core") + lax.axis_index("core")
     drop = jnp.exp(-rows * rate_ref[...])
     before = jnp.zeros(rate_ref.shape, F32)
@@ -223,19 +225,23 @@
     own.wait()
 
 
-def project_body(left_ref, own_ref, *rest):
-    *others, out_hbm, done, sems = rest
-    parts = left_ref.shape[0]
+def order_body(left_ref, _side, _across, out_ref, _same_side, _same_across):
+    parts, _, channels = left_ref.shape
     here = lax.axis_index("tp")
+    for d in range(parts):
+        out_ref[:, pl.ds(d * channels, channels)] = left_ref[lax.rem(here + parts - d, parts)]
+
+
+def project_body(left_ref, *rest):
+    *rights, out_hbm, done, sems = rest
     blocks, _, block = done.shape
+    channels = rights[0].shape[0]
     copies = []
     for b in range(blocks):
         at = pl.ds(b * block, block)
-        total = jnp.dot(left_ref[here], own_ref[:, at], preferred_element_type=F32)
-        for d in range(1, parts):
-            total += jnp.dot(
-                left_ref[lax.rem(here + parts - d, parts)], others[d - 1][:, at], preferred_element_type=F32
-            )
+        total = jnp.zeros(done.shape[1:], F32)
+        for d, right in enumerate(rights):
+            total += jnp.dot(left_ref[:, pl.ds(d * channels, channels)], right[:, at], preferred_element_type=F32)
         done[b] = total.astype(BF16)
         copies.append(pltpu.make_async_copy(done.at[b], out_hbm.at[:, at], sems.at[b]))
         copies[-1].start()
@@ -286,10 +292,10 @@
             pltpu.SemaphoreType.DMA((7 + parts - 1,)),
         ],
     )(query_in, key_in, value_in, short_weight, rate, residue, skip, out_weight)
-    blocks = [
-        lax.ppermute(block, "tp", [(i, (i + d) % parts) for i in range(parts)])
-        for d, block in enumerate(blocks, start=1)
-    ]
+    def to_next(block, d):
+        return lax.ppermute(block, "tp", [(i, (i + d) % parts) for i in range(parts)])
+
+    blocks = [to_next(blocks[0], 1), to_next(blocks[1], 2), blocks[2]]
     states, late, top = call(
         lambda *refs: join_body(rows, *refs),
         [VMEM] * 5,
@@ -302,12 +308,15 @@
         [pltpu.VMEM((3, 2 * HEAD, channels), F32)],
     )(rims, heads, taps_here, rate, states)
     states = lax.all_to_all(states, ("y", "core"), 0, 0, tiled=True)
-    before, totals = call(
+    before, totals, blocks[2] = call(
         lambda *refs: plane_body(rows, *refs),
-        [VMEM] * 2,
-        (shape((modes, channels), F32), shape((planes, modes, channels), BF16)),
+        [VMEM] * 2 + [ANY],
+        (shape((modes, channels), F32), shape((planes, modes, channels), BF16), shape((channels, width), BF16)),
         "plane",
-    )(states, rate)
+        out_spec=(VMEM, VMEM, ANY),
+        aliases={2: 2},
+    )(states, rate, blocks[2])
+    blocks[2] = to_next(blocks[2], 3)
     totals = lax.all_to_all(totals, "z", 0, 0, tiled=True)
     hyena, own = call(
         lambda *refs: mix_body(taps, rows * plane, *refs),
@@ -321,10 +330,19 @@
         ],
     )(queries, gated, begin, late, top, before, totals, rate, amplitude, skip, out_weight)
     hyena = lax.all_to_all(hyena, "tp", 0, 0, tiled=True)
+    hyena, *blocks[:2] = call(
+        order_body,
+        [VMEM] + [ANY] * 2,
+        (shape((rows, parts * channels), BF16), *[shape((channels, width), BF16)] * 2),
+        "order",
+        out_spec=(VMEM, ANY, ANY),
+        aliases={1: 1, 2: 2},
+        us=2,
+    )(hyena, *blocks[:2])
     block = 256
     return call(
         project_body,
-        [VMEM] * (2 + len(blocks)),
+        [VMEM] * 5,
         shape((rows, width), BF16),
         "project",
         [pltpu.VMEM((width // block, rows, block), BF16), pltpu.SemaphoreType.DMA((width // block,))],

time: 58.9 us -> 57 us (0.968)
  the two profiles are of different devices: /device:TPU:8 before, /device:TPU:1 now
where the time goes in v8:
time: 57 us; the launch traced here: 56.3 us
  starting transfers between devices  36.7 us (64%)
  waiting for transfers between devices  11.8 us (21%)
  Pallas kernels  7.76 us (14%)
    ppermute x3, starting transfers between devices, to_next(): lax.ppermute(block, 'tp', [(i, (i + d) % parts) for i in range(parts)])  11.9 us
    all_to_all x1, starting transfers between devices, local(): totals = lax.all_to_all(totals, 'z', 0, 0, tiled=True)  10 us
    all_to_all x1, starting transfers between devices, local(): states = lax.all_to_all(states, ('y', 'core'), 0, 0, tiled=True)  6.13 us
    all_to_all x1, waiting for transfers between devices, local(): hyena = lax.all_to_all(hyena, 'tp', 0, 0, tiled=True)  5.52 us
    ppermute x1, starting transfers between devices, local(): rims = lax.ppermute(rims, order, [(i, i + 1) for i in range(devices - 1)])  4.59 us
    all_to_all x1, starting transfers between devices, local(): hyena = lax.all_to_all(hyena, 'tp', 0, 0, tiled=True)  4.03 us
    all_to_all x1, waiting for transfers between devices, local(): totals = lax.all_to_all(totals, 'z', 0, 0, tiled=True)  3.05 us
    pallas_call x1, Pallas kernels, local(): call(gate_body, [HBM] * 8, (shape(by_half, F32), shape(by_half, F32), sha...  2.66 us
  transfers between devices with their start and end apart: 7, of which 4 were waited for; matrix products, arithmetic and copies ran while one was open for 0% of the time, Pallas kernels for 9%

profile of v8, /device:TPU:1, one launch (start us, length us, event | category | flops | bytes accessed | tf_op | source)
XLA Modules:
  0.0 56.3 jit_solution(11634222700259405671)
XLA Ops:
  0.0 0.8 %rims.1 = bf16[48,256]{1,0:T(8,128)(2,1)S(1)} custom-call(bf16[128,256]{1,0:T(8,128)(2,1)} %q_ref.1, bf16[128,256]{1,0:T(8,128)(2,1)} %k_ref.1, bf16[128,256]{1,0:T(8,128)(2,1)} %v_ref.1), custom_call_target="tpu_custom_call" | custom-call | tf_op jit(solution)/shard_map/rims/pallas_call | solution.py:268
  0.8 4.6 %collective-permute-start = (bf16[48,256]{1,0:T(8,128)(2,1)S(1)}, bf16[48,256]{1,0:T(8,128)(2,1)S(1)}, u32[]{:S(2)}, u32[]{:S(2)}) collective-permute-start(bf16[48,256]{1,0:T(8,128)(2,1)S(1)} %rims.1), channel_id=1, source_target_pairs={{0,4},{4,8},{8,12},{12,16},{16,20},{20,24},{24,28},{28,32},{32,36}... | collective-permute-start | bytes 73736 | tf_op jit(solution)/shard_map/ppermute | solution.py:271
  5.4 2.7 %gate.1 = (f32[2,128,128]{2,1,0:T(8,128)S(1)}, f32[2,128,128]{2,1,0:T(8,128)S(1)}, f32[16,8,256]{2,1,0:T(8,128)S(1)}, f32[16,256]{1,0:T(8,128)S(1)}, f32[3,8,256...) custom-call(bf16[128,256]{1,0:T(8,128)(2,1)} %q_ref.1, ...), custom_call_target="tpu_custom_call" | custom-call | tf_op jit(solution)/shard_map/gate/pallas_call | solution.py:272
  8.0 1.6 %collective-permute-done.refs_0_ = bf16[48,256]{1,0:T(8,128)(2,1)S(1)} collective-permute-done((bf16[48,256]{1,0:T(8,128)(2,1)S(1)}, bf16[48,256]{1,0:T(8,128)(2,1)S(1)}, u32[]{:S(2)}, u32[]{:S(2)}) %collective-permute-start) | collective-permute-done | bytes 24608 | tf_op jit(solution)/shard_map/ppermute | solution.py:271
  9.6 0.7 %join.1 = (bf16[16,16,256]{2,1,0:T(8,128)(2,1)}, f32[16,256]{1,0:T(8,128)S(1)}, f32[2,8,256]{2,1,0:T(8,128)S(1)}) custom-call(bf16[48,256]{1,0:T(8,128)(2,1)S(1)} %collective-permute-done.refs_0_, f32[3,8,256]{2,1,0:T(8,128)S(1)} %get-tuple-element.31.refs_1_, f32[3,7,256]{2,1,0:T(8,128)S(1)} %get-tuple-element.32.refs_2_, ...), custom_call_target="tpu_custom_call" | custom-call | tf_op jit(solution)/shard_map/join/pallas_call | solution.py:299
  10.3 6.1 %all-to-all-start = ((bf16[16,16,256]{2,1,0:T(8,128)(2,1)}), bf16[16,16,256]{2,1,0:T(8,128)(2,1)S(1)}, u32[]{:S(2)}, u32[]{:S(2)}) async-start(bf16[16,16,256]{2,1,0:T(8,128)(2,1)} %get-tuple-element.37), calls=%async_computation | async-start | bytes 262144 | tf_op jit(solution)/shard_map/all_to_all | solution.py:310
  16.5 3.1 %collective-permute-start.1 = (bf16[256,1024]{1,0:T(8,128)(2,1)}, bf16[256,1024]{1,0:T(8,128)(2,1)S(1)}, u32[]{:S(2)}, u32[]{:S(2)}) collective-permute-start(bf16[256,1024]{1,0:T(8,128)(2,1)} %get-tuple-element.44), channel_id=1, source_target_pairs={{0,1},{1,2},{2,3},{3,0},{4,5},{5,6},{6,7},{7,4},{8,9},{9,10},{10,1... | collective-permute-start | bytes 1572872 | tf_op jit(solution)/shard_map/ppermute | solution.py:296
  19.6 4.4 %collective-permute-start.2 = (bf16[256,1024]{1,0:T(8,128)(2,1)}, bf16[256,1024]{1,0:T(8,128)(2,1)S(1)}, u32[]{:S(2)}, u32[]{:S(2)}) collective-permute-start(bf16[256,1024]{1,0:T(8,128)(2,1)} %get-tuple-element.45), channel_id=1, source_target_pairs={{0,2},{1,3},{2,0},{3,1},{4,6},{5,7},{6,4},{7,5},{8,10},{9,11},{10,... | collective-permute-start | bytes 1572872 | tf_op jit(solution)/shard_map/ppermute | solution.py:296
  24.0 1.7 %all-to-all-done.refs_0_ = bf16[16,16,256]{2,1,0:T(8,128)(2,1)S(1)} async-done(((bf16[16,16,256]{2,1,0:T(8,128)(2,1)}), bf16[16,16,256]{2,1,0:T(8,128)(2,1)S(1)}, u32[]{:S(2)}, u32[]{:S(2)}) %all-to-all-start) | async-done | bytes 131104 | tf_op jit(solution)/shard_map/all_to_all | solution.py:310
  25.6 0.7 %plane.1 = (f32[16,256]{1,0:T(8,128)S(1)}, bf16[8,16,256]{2,1,0:T(8,128)(2,1)}, bf16[256,1024]{1,0:T(8,128)(2,1)S(1)}) custom-call(bf16[16,16,256]{2,1,0:T(8,128)(2,1)S(1)} %all-to-all-done.refs_0_, f32[16,256]{1,0:T(8,128)S(1)} %get-tuple-element.33.refs_3_.refs_1_.refs_7_, ...), custom_call_target="tpu_custom_call", output_to_operand_aliasing={{2}: (2, {})} | custom-call | tf_op jit(solution)/shard_map/plane/pallas_call | solution.py:311
  26.3 10.0 %all-to-all-start.1 = ((bf16[8,16,256]{2,1,0:T(8,128)(2,1)}), bf16[8,16,256]{2,1,0:T(8,128)(2,1)S(1)}, u32[]{:S(2)}, u32[]{:S(2)}) async-start(bf16[8,16,256]{2,1,0:T(8,128)(2,1)} %get-tuple-element.40), calls=%async_computation.1 | async-start | bytes 131072 | tf_op jit(solution)/shard_map/all_to_all | solution.py:320
  36.4 4.4 %collective-permute-start.3 = (bf16[256,1024]{1,0:T(8,128)(2,1)S(1)}, bf16[256,1024]{1,0:T(8,128)(2,1)S(1)}, u32[]{:S(2)}, u32[]{:S(2)}) collective-permute-start(bf16[256,1024]{1,0:T(8,128)(2,1)S(1)} %get-tuple-element.50), channel_id=1, source_target_pairs={{0,3},{1,0},{2,1},{3,2},{4,7},{5,4},{6,5},{7,6},{8,11},{9,8},{10,9... | collective-permute-start | bytes 1572872 | tf_op jit(solution)/shard_map/ppermute | solution.py:296
  40.7 3.0 %all-to-all-done.1.refs_6_ = bf16[8,16,256]{2,1,0:T(8,128)(2,1)S(1)} async-done(((bf16[8,16,256]{2,1,0:T(8,128)(2,1)}), bf16[8,16,256]{2,1,0:T(8,128)(2,1)S(1)}, u32[]{:S(2)}, u32[]{:S(2)}) %all-to-all-start.1) | async-done | bytes 65568 | tf_op jit(solution)/shard_map/all_to_all | solution.py:320
  43.8 1.8 %mix.1 = (bf16[4,128,256]{2,1,0:T(8,128)(2,1)}, bf16[256,1024]{1,0:T(8,128)(2,1)S(1)}) custom-call(f32[2,128,128]{2,1,0:T(8,128)S(1)} %get-tuple-element.28.refs_0_, f32[2,128,128]{2,1,0:T(8,128)S(1)} %get-tuple-element.29.refs_1_, f32[16,8,256]{2,1,0:T(8,128)S(1)} %get-tuple-element.30.refs_2_, f32[16,256]{1,0:T(8,128)S(1)} %get-tuple-element.35.refs_3_, ...), custom_call_target="tpu_custom_call" | custom-call | tf_op jit(solution)/shard_map/mix/pallas_call | solution.py:321
  45.6 4.0 %all-to-all-start.2 = ((bf16[4,128,256]{2,1,0:T(8,128)(2,1)}), bf16[4,128,256]{2,1,0:T(8,128)(2,1)S(1)}, u32[]{:S(2)}, u32[]{:S(2)}) async-start(bf16[4,128,256]{2,1,0:T(8,128)(2,1)} %get-tuple-element.43), calls=%async_computation.2 | async-start | bytes 524288 | tf_op jit(solution)/shard_map/all_to_all | solution.py:332
  49.6 0.0 collective-permute-done.1._side
  49.6 0.0 collective-permute-done.2._across
  49.6 5.5 %all-to-all-done.2.left_ref = bf16[4,128,256]{2,1,0:T(8,128)(2,1)S(1)} async-done(((bf16[4,128,256]{2,1,0:T(8,128)(2,1)}), bf16[4,128,256]{2,1,0:T(8,128)(2,1)S(1)}, u32[]{:S(2)}, u32[]{:S(2)}) %all-to-all-start.2) | async-done | bytes 262176 | tf_op jit(solution)/shard_map/all_to_all | solution.py:332
  55.1 0.0 collective-permute-done.3.rest_3_
  55.1 1.2 %project.1 = bf16[128,1024]{1,0:T(8,128)(2,1)} custom-call(bf16[128,1024]{1,0:T(8,128)(2,1)S(1)} %get-tuple-element.46.left_ref, bf16[256,1024]{1,0:T(8,128)(2,1)S(1)} %get-tuple-element.47.rest_0_, bf16[256,1024]{1,0:T(8,128)(2,1)S(1)} %get-tuple-element.48.rest_1_, bf16[256,1024]{1,0:T(8,128)(2,1)S(1)} %get-tuple-element.49.rest_2_, ...), custom_call_target="tpu_custom_call" | custom-call | tf_op jit(solution)/shard_map/project/pallas_call | solution.py:343
  (1 shorter events, 0.0 us)
Async XLA Ops:
  0.8 8.8 %collective-permute-start = (bf16[48,256]{1,0:T(8,128)(2,1)S(1)}, bf16[48,256]{1,0:T(8,128)(2,1)S(1)}, u32[]{:S(2)}, u32[]{:S(2)}) collective-permute-start(bf16[48,256]{1,0:T(8,128)(2,1)S(1)} %rims.1), channel_id=1, source_target_pairs={{0,4},{4,8},{8,12},{12,16},{16,20},{20,24},{24,28},{28,32},{32,36}... | collective-permute-start | bytes 73736 | tf_op jit(solution)/shard_map/ppermute | solution.py:271
  10.3 15.3 %all-to-all-start = ((bf16[16,16,256]{2,1,0:T(8,128)(2,1)}), bf16[16,16,256]{2,1,0:T(8,128)(2,1)S(1)}, u32[]{:S(2)}, u32[]{:S(2)}) async-start(bf16[16,16,256]{2,1,0:T(8,128)(2,1)} %get-tuple-element.37), calls=%async_computation | async-start | bytes 262144 | tf_op jit(solution)/shard_map/all_to_all | solution.py:310
  16.5 33.1 %collective-permute-start.1 = (bf16[256,1024]{1,0:T(8,128)(2,1)}, bf16[256,1024]{1,0:T(8,128)(2,1)S(1)}, u32[]{:S(2)}, u32[]{:S(2)}) collective-permute-start(bf16[256,1024]{1,0:T(8,128)(2,1)} %get-tuple-element.44), channel_id=1, source_target_pairs={{0,1},{1,2},{2,3},{3,0},{4,5},{5,6},{6,7},{7,4},{8,9},{9,10},{10,1... | collective-permute-start | bytes 1572872 | tf_op jit(solution)/shard_map/ppermute | solution.py:296
  19.6 30.0 %collective-permute-start.2 = (bf16[256,1024]{1,0:T(8,128)(2,1)}, bf16[256,1024]{1,0:T(8,128)(2,1)S(1)}, u32[]{:S(2)}, u32[]{:S(2)}) collective-permute-start(bf16[256,1024]{1,0:T(8,128)(2,1)} %get-tuple-element.45), channel_id=1, source_target_pairs={{0,2},{1,3},{2,0},{3,1},{4,6},{5,7},{6,4},{7,5},{8,10},{9,11},{10,... | collective-permute-start | bytes 1572872 | tf_op jit(solution)/shard_map/ppermute | solution.py:296
  26.3 17.5 %all-to-all-start.1 = ((bf16[8,16,256]{2,1,0:T(8,128)(2,1)}), bf16[8,16,256]{2,1,0:T(8,128)(2,1)S(1)}, u32[]{:S(2)}, u32[]{:S(2)}) async-start(bf16[8,16,256]{2,1,0:T(8,128)(2,1)} %get-tuple-element.40), calls=%async_computation.1 | async-start | bytes 131072 | tf_op jit(solution)/shard_map/all_to_all | solution.py:320
  36.4 18.8 %collective-permute-start.3 = (bf16[256,1024]{1,0:T(8,128)(2,1)S(1)}, bf16[256,1024]{1,0:T(8,128)(2,1)S(1)}, u32[]{:S(2)}, u32[]{:S(2)}) collective-permute-start(bf16[256,1024]{1,0:T(8,128)(2,1)S(1)} %get-tuple-element.50), channel_id=1, source_target_pairs={{0,3},{1,0},{2,1},{3,2},{4,7},{5,4},{6,5},{7,6},{8,11},{9,8},{10,9... | collective-permute-start | bytes 1572872 | tf_op jit(solution)/shard_map/ppermute | solution.py:296
  45.6 9.6 %all-to-all-start.2 = ((bf16[4,128,256]{2,1,0:T(8,128)(2,1)}), bf16[4,128,256]{2,1,0:T(8,128)(2,1)S(1)}, u32[]{:S(2)}, u32[]{:S(2)}) async-start(bf16[4,128,256]{2,1,0:T(8,128)(2,1)} %get-tuple-element.43), calls=%async_computation.2 | async-start | bytes 524288 | tf_op jit(solution)/shard_map/all_to_all | solution.py:332

commit v9 on v8

--- a/solution.py
+++ b/solution.py
@@ -76,9 +76,9 @@
     q_hbm, k_hbm, v_hbm, taps_hbm, rate_hbm, residue_hbm, skip_hbm, weight_hbm,
     query_ref, gated_ref, begin_ref, state_ref, head_ref, taps_ref, rate_ref, amp_ref, skip_ref, *rest,
 ):
-    *blocks, streams, residue_ref, pad, sems = rest
+    *blocks, streams, residue_ref, pad, held, sems = rest
     here, parts = lax.axis_index("tp"), lax.axis_size("tp")
-    width = blocks[0].shape[1]
+    width = held.shape[2]
     _, rows, channels = streams.shape
     modes = rate_ref.shape[0]
     taps = taps_ref.shape[1]
@@ -90,7 +90,7 @@
     )
     sent = fetch(
         [weight_hbm.at[:, pl.ds(lax.rem(here + d, parts) * width, width)] for d in range(1, parts)],
-        blocks,
+        [held.at[d] for d in range(parts - 1)],
         sems.at[pl.ds(7, parts - 1)],
     )
     for copy in copies:
@@ -113,6 +113,9 @@
                     head_ref[i, :, lanes] = total[:HEAD]
             query_ref[half, pl.ds(r, block), :] = sums[0]
             gated_ref[half, pl.ds(r, block), :] = sums[1] * sums[2]
+    for copy in sent:
+        copy.wait()
+    sent = fetch([held.at[d] for d in range(parts - 1)], blocks, sems.at[pl.ds(7, parts - 1)])
     sub = lax.broadcasted_iota(jnp.int32, (SUBS, LANES), 0)
     for half in range(channels // LANES):
         lanes = pl.ds(half * LANES, LANES)
@@ -159,7 +162,7 @@
         out_ref[i] = whole
 
 
-def plane_body(rows, parts_ref, rate_ref, _block, before_ref, total_ref, _same_block):
+def plane_body(rows, parts_ref, rate_ref, _a, _b, before_ref, total_ref, _same_a, _same_b):
     me = lax.axis_index("y") * lax.axis_size("core") + lax.axis_index("core")
     drop = jnp.exp(-rows * rate_ref[...])
     before = jnp.zeros(rate_ref.shape, F32)
@@ -225,7 +228,7 @@
     own.wait()
 
 
-def order_body(left_ref, _side, _across, out_ref, _same_side, _same_across):
+def order_body(left_ref, _across, out_ref, _same_across):
     parts, _, channels = left_ref.shape
     here = lax.axis_index("tp")
     for d in range(parts):
@@ -282,20 +285,22 @@
             shape((modes, channels), F32),
             shape((modes, channels), F32),
             shape((1, channels), F32),
-            *[shape((channels, width), BF16)] * (parts - 1),
+            *[pltpu.HBM((channels, width), BF16)] * (parts - 1),
         ),
         "gate",
         [
             pltpu.VMEM((3, rows, channels), BF16),
             pltpu.VMEM((modes, channels), F32),
             pltpu.VMEM((3, HEAD + rows, channels), F32),
+            pltpu.VMEM((parts - 1, channels, width), BF16),
             pltpu.SemaphoreType.DMA((7 + parts - 1,)),
         ],
+        out_spec=(*[VMEM] * 9, *[HBM] * (parts - 1)),
     )(query_in, key_in, value_in, short_weight, rate, residue, skip, out_weight)
     def to_next(block, d):
         return lax.ppermute(block, "tp", [(i, (i + d) % parts) for i in range(parts)])
 
-    blocks = [to_next(blocks[0], 1), to_next(blocks[1], 2), blocks[2]]
+    blocks[1] = to_next(blocks[1], 2)
     states, late, top = call(
         lambda *refs: join_body(rows, *refs),
         [VMEM] * 5,
@@ -308,15 +313,19 @@
         [pltpu.VMEM((3, 2 * HEAD, channels), F32)],
     )(rims, heads, taps_here, rate, states)
     states = lax.all_to_all(states, ("y", "core"), 0, 0, tiled=True)
-    before, totals, blocks[2] = call(
+    before, totals, *blocks[::2] = call(
         lambda *refs: plane_body(rows, *refs),
-        [VMEM] * 2 + [ANY],
-        (shape((modes, channels), F32), shape((planes, modes, channels), BF16), shape((channels, width), BF16)),
+        [VMEM] * 2 + [ANY] * 2,
+        (
+            shape((modes, channels), F32),
+            shape((planes, modes, channels), BF16),
+            *[pltpu.HBM((channels, width), BF16)] * 2,
+        ),
         "plane",
-        out_spec=(VMEM, VMEM, ANY),
-        aliases={2: 2},
-    )(states, rate, blocks[2])
-    blocks[2] = to_next(blocks[2], 3)
+        out_spec=(VMEM, VMEM, ANY, ANY),
+        aliases={2: 2, 3: 3},
+    )(states, rate, *blocks[::2])
+    blocks[0], blocks[2] = to_next(blocks[0], 1), to_next(blocks[2], 3)
     totals = lax.all_to_all(totals, "z", 0, 0, tiled=True)
     hyena, own = call(
         lambda *refs: mix_body(taps, rows * plane, *refs),
@@ -330,15 +339,15 @@
         ],
     )(queries, gated, begin, late, top, before, totals, rate, amplitude, skip, out_weight)
     hyena = lax.all_to_all(hyena, "tp", 0, 0, tiled=True)
-    hyena, *blocks[:2] = call(
+    hyena, blocks[1] = call(
         order_body,
-        [VMEM] + [ANY] * 2,
-        (shape((rows, parts * channels), BF16), *[shape((channels, width), BF16)] * 2),
+        [VMEM, ANY],
+        (shape((rows, parts * channels), BF16), shape((channels, width), BF16)),
         "order",
-        out_spec=(VMEM, ANY, ANY),
-        aliases={1: 1, 2: 2},
+        out_spec=(VMEM, ANY),
+        aliases={1: 1},
         us=2,
-    )(hyena, *blocks[:2])
+    )(hyena, blocks[1])
     block = 256
     return call(
         project_body,

time: 57 us -> 59.6 us (1.046)
  the two profiles are of different devices: /device:TPU:1 before, /device:TPU:2 now
where the time goes in v9:
time: 59.6 us; the launch traced here: 59 us
  starting transfers between devices  35.7 us (60%)
  waiting for transfers between devices  15.3 us (26%)
  Pallas kernels  7.9 us (13%)
    all_to_all x1, starting transfers between devices, local(): totals = lax.all_to_all(totals, 'z', 0, 0, tiled=True)  10.3 us
    ppermute x3, starting transfers between devices, to_next(): lax.ppermute(block, 'tp', [(i, (i + d) % parts) for i in range(parts)])  9.86 us
    all_to_all x1, starting transfers between devices, local(): states = lax.all_to_all(states, ('y', 'core'), 0, 0, tiled=True)  8.98 us
    all_to_all x1, waiting for transfers between devices, local(): hyena = lax.all_to_all(hyena, 'tp', 0, 0, tiled=True)  7.77 us
    all_to_all x1, starting transfers between devices, local(): hyena = lax.all_to_all(hyena, 'tp', 0, 0, tiled=True)  4.84 us
    all_to_all x1, waiting for transfers between devices, local(): states = lax.all_to_all(states, ('y', 'core'), 0, 0, tiled=True)  4.7 us
    all_to_all x1, waiting for transfers between devices, local(): totals = lax.all_to_all(totals, 'z', 0, 0, tiled=True)  2.82 us
    pallas_call x1, Pallas kernels, local(): call(gate_body, [HBM] * 8, (shape(by_half, F32), shape(by_half, F32), sha...  2.81 us
  transfers between devices with their start and end apart: 7, of which 3 were waited for; matrix products, arithmetic and copies ran while one was open for 0% of the time, Pallas kernels for 9%

profile of v9, /device:TPU:2, one launch (start us, length us, event | category | flops | bytes accessed | tf_op | source)
XLA Modules:
  0.0 59.0 jit_solution(12590390152144108834)
XLA Ops:
  0.0 0.8 %rims.1 = bf16[48,256]{1,0:T(8,128)(2,1)S(1)} custom-call(bf16[128,256]{1,0:T(8,128)(2,1)} %q_ref.1, bf16[128,256]{1,0:T(8,128)(2,1)} %k_ref.1, bf16[128,256]{1,0:T(8,128)(2,1)} %v_ref.1), custom_call_target="tpu_custom_call" | custom-call | tf_op jit(solution)/shard_map/rims/pallas_call | solution.py:271
  0.8 1.7 %collective-permute-start = (bf16[48,256]{1,0:T(8,128)(2,1)S(1)}, bf16[48,256]{1,0:T(8,128)(2,1)S(1)}, u32[]{:S(2)}, u32[]{:S(2)}) collective-permute-start(bf16[48,256]{1,0:T(8,128)(2,1)S(1)} %rims.1), channel_id=1, source_target_pairs={{0,4},{4,8},{8,12},{12,16},{16,20},{20,24},{24,28},{28,32},{32,36}... | collective-permute-start | bytes 73736 | tf_op jit(solution)/shard_map/ppermute | solution.py:274
  2.5 2.8 %gate.1 = (f32[2,128,128]{2,1,0:T(8,128)S(1)}, f32[2,128,128]{2,1,0:T(8,128)S(1)}, f32[16,8,256]{2,1,0:T(8,128)S(1)}, f32[16,256]{1,0:T(8,128)S(1)}, f32[3,8,256...) custom-call(bf16[128,256]{1,0:T(8,128)(2,1)} %q_ref.1, ...), custom_call_target="tpu_custom_call" | custom-call | tf_op jit(solution)/shard_map/gate/pallas_call | solution.py:275
  5.3 0.0 collective-permute-done.refs_0_
  5.3 0.7 %join.1 = (bf16[16,16,256]{2,1,0:T(8,128)(2,1)}, f32[16,256]{1,0:T(8,128)S(1)}, f32[2,8,256]{2,1,0:T(8,128)S(1)}) custom-call(bf16[48,256]{1,0:T(8,128)(2,1)S(1)} %collective-permute-done.refs_0_, f32[3,8,256]{2,1,0:T(8,128)S(1)} %get-tuple-element.31.refs_1_, f32[3,7,256]{2,1,0:T(8,128)S(1)} %get-tuple-element.32.refs_2_, ...), custom_call_target="tpu_custom_call" | custom-call | tf_op jit(solution)/shard_map/join/pallas_call | solution.py:304
  6.1 9.0 %all-to-all-start = ((bf16[16,16,256]{2,1,0:T(8,128)(2,1)}), bf16[16,16,256]{2,1,0:T(8,128)(2,1)S(1)}, u32[]{:S(2)}, u32[]{:S(2)}) async-start(bf16[16,16,256]{2,1,0:T(8,128)(2,1)} %get-tuple-element.37), calls=%async_computation | async-start | bytes 262144 | tf_op jit(solution)/shard_map/all_to_all | solution.py:315
  15.1 4.0 %collective-permute-start.1 = (bf16[256,1024]{1,0:T(8,128)(2,1)}, bf16[256,1024]{1,0:T(8,128)(2,1)S(1)}, u32[]{:S(2)}, u32[]{:S(2)}) collective-permute-start(bf16[256,1024]{1,0:T(8,128)(2,1)} %get-tuple-element.45), channel_id=1, source_target_pairs={{0,2},{1,3},{2,0},{3,1},{4,6},{5,7},{6,4},{7,5},{8,10},{9,11},{10,... | collective-permute-start | bytes 1572872 | tf_op jit(solution)/shard_map/ppermute | solution.py:301
  19.1 4.7 %all-to-all-done.refs_0_ = bf16[16,16,256]{2,1,0:T(8,128)(2,1)S(1)} async-done(((bf16[16,16,256]{2,1,0:T(8,128)(2,1)}), bf16[16,16,256]{2,1,0:T(8,128)(2,1)S(1)}, u32[]{:S(2)}, u32[]{:S(2)}) %all-to-all-start) | async-done | bytes 131104 | tf_op jit(solution)/shard_map/all_to_all | solution.py:315
  23.8 0.7 %plane.1 = (f32[16,256]{1,0:T(8,128)S(1)}, bf16[8,16,256]{2,1,0:T(8,128)(2,1)}, bf16[256,1024]{1,0:T(8,128)(2,1)}, bf16[256,1024]{1,0:T(8,128)(2,1)}) custom-call(bf16[16,16,256]{2,1,0:T(8,128)(2,1)S(1)} %all-to-all-done.refs_0_, f32[16,256]{1,0:T(8,128)S(1)} %get-tuple-element.33.refs_3_.refs_1_.refs_7_, ...), custom_call_target="tpu_custom_call", output_to_operand_aliasing={{2}: (2, {}), {3}: (3, {})} | custom-call | tf_op jit(solution)/shard_map/plane/pallas_call | solution.py:316
  24.5 10.3 %all-to-all-start.1 = ((bf16[8,16,256]{2,1,0:T(8,128)(2,1)}), bf16[8,16,256]{2,1,0:T(8,128)(2,1)S(1)}, u32[]{:S(2)}, u32[]{:S(2)}) async-start(bf16[8,16,256]{2,1,0:T(8,128)(2,1)} %get-tuple-element.41), calls=%async_computation.1 | async-start | bytes 131072 | tf_op jit(solution)/shard_map/all_to_all | solution.py:329
  34.8 3.4 %collective-permute-start.2 = (bf16[256,1024]{1,0:T(8,128)(2,1)}, bf16[256,1024]{1,0:T(8,128)(2,1)S(1)}, u32[]{:S(2)}, u32[]{:S(2)}) collective-permute-start(bf16[256,1024]{1,0:T(8,128)(2,1)} %get-tuple-element.48), channel_id=1, source_target_pairs={{0,1},{1,2},{2,3},{3,0},{4,5},{5,6},{6,7},{7,4},{8,9},{9,10},{10,1... | collective-permute-start | bytes 1572872 | tf_op jit(solution)/shard_map/ppermute | solution.py:301
  38.2 2.4 %collective-permute-start.3 = (bf16[256,1024]{1,0:T(8,128)(2,1)}, bf16[256,1024]{1,0:T(8,128)(2,1)S(1)}, u32[]{:S(2)}, u32[]{:S(2)}) collective-permute-start(bf16[256,1024]{1,0:T(8,128)(2,1)} %get-tuple-element.50), channel_id=1, source_target_pairs={{0,3},{1,0},{2,1},{3,2},{4,7},{5,4},{6,5},{7,6},{8,11},{9,8},{10,9... | collective-permute-start | bytes 1572872 | tf_op jit(solution)/shard_map/ppermute | solution.py:301
  40.6 2.8 %all-to-all-done.1.refs_6_ = bf16[8,16,256]{2,1,0:T(8,128)(2,1)S(1)} async-done(((bf16[8,16,256]{2,1,0:T(8,128)(2,1)}), bf16[8,16,256]{2,1,0:T(8,128)(2,1)S(1)}, u32[]{:S(2)}, u32[]{:S(2)}) %all-to-all-start.1) | async-done | bytes 65568 | tf_op jit(solution)/shard_map/all_to_all | solution.py:329
  43.5 1.8 %mix.1 = (bf16[4,128,256]{2,1,0:T(8,128)(2,1)}, bf16[256,1024]{1,0:T(8,128)(2,1)S(1)}) custom-call(f32[2,128,128]{2,1,0:T(8,128)S(1)} %get-tuple-element.28.refs_0_, f32[2,128,128]{2,1,0:T(8,128)S(1)} %get-tuple-element.29.refs_1_, f32[16,8,256]{2,1,0:T(8,128)S(1)} %get-tuple-element.30.refs_2_, f32[16,256]{1,0:T(8,128)S(1)} %get-tuple-element.35.refs_3_, ...), custom_call_target="tpu_custom_call" | custom-call | tf_op jit(solution)/shard_map/mix/pallas_call | solution.py:330
  45.2 4.8 %all-to-all-start.2 = ((bf16[4,128,256]{2,1,0:T(8,128)(2,1)}), bf16[4,128,256]{2,1,0:T(8,128)(2,1)S(1)}, u32[]{:S(2)}, u32[]{:S(2)}) async-start(bf16[4,128,256]{2,1,0:T(8,128)(2,1)} %get-tuple-element.44), calls=%async_computation.2 | async-start | bytes 524288 | tf_op jit(solution)/shard_map/all_to_all | solution.py:341
  50.1 0.0 collective-permute-done.1._across
  50.1 7.8 %all-to-all-done.2.left_ref = bf16[4,128,256]{2,1,0:T(8,128)(2,1)S(1)} async-done(((bf16[4,128,256]{2,1,0:T(8,128)(2,1)}), bf16[4,128,256]{2,1,0:T(8,128)(2,1)S(1)}, u32[]{:S(2)}, u32[]{:S(2)}) %all-to-all-start.2) | async-done | bytes 262176 | tf_op jit(solution)/shard_map/all_to_all | solution.py:341
  57.9 0.0 collective-permute-done.2.rest_1_
  57.9 0.0 collective-permute-done.3.rest_3_
  57.9 1.1 %project.1 = bf16[128,1024]{1,0:T(8,128)(2,1)} custom-call(bf16[128,1024]{1,0:T(8,128)(2,1)S(1)} %get-tuple-element.46.left_ref, bf16[256,1024]{1,0:T(8,128)(2,1)S(1)} %get-tuple-element.47.rest_0_, bf16[256,1024]{1,0:T(8,128)(2,1)S(1)} %collective-permute-done.2.rest_1_, bf16[256,1024]{1,0:T(8,128)(2,1)S(1)} %get-tuple-element.49.rest_2_, ...), custom_call_target="tpu_custom_call" | custom-call | tf_op jit(solution)/shard_map/project/pallas_call | solution.py:352
  (1 shorter events, 0.0 us)
Async XLA Ops:
  0.8 4.6 %collective-permute-start = (bf16[48,256]{1,0:T(8,128)(2,1)S(1)}, bf16[48,256]{1,0:T(8,128)(2,1)S(1)}, u32[]{:S(2)}, u32[]{:S(2)}) collective-permute-start(bf16[48,256]{1,0:T(8,128)(2,1)S(1)} %rims.1), channel_id=1, source_target_pairs={{0,4},{4,8},{8,12},{12,16},{16,20},{20,24},{24,28},{28,32},{32,36}... | collective-permute-start | bytes 73736 | tf_op jit(solution)/shard_map/ppermute | solution.py:274
  6.1 17.7 %all-to-all-start = ((bf16[16,16,256]{2,1,0:T(8,128)(2,1)}), bf16[16,16,256]{2,1,0:T(8,128)(2,1)S(1)}, u32[]{:S(2)}, u32[]{:S(2)}) async-start(bf16[16,16,256]{2,1,0:T(8,128)(2,1)} %get-tuple-element.37), calls=%async_computation | async-start | bytes 262144 | tf_op jit(solution)/shard_map/all_to_all | solution.py:315
  15.1 35.0 %collective-permute-start.1 = (bf16[256,1024]{1,0:T(8,128)(2,1)}, bf16[256,1024]{1,0:T(8,128)(2,1)S(1)}, u32[]{:S(2)}, u32[]{:S(2)}) collective-permute-start(bf16[256,1024]{1,0:T(8,128)(2,1)} %get-tuple-element.45), channel_id=1, source_target_pairs={{0,2},{1,3},{2,0},{3,1},{4,6},{5,7},{6,4},{7,5},{8,10},{9,11},{10,... | collective-permute-start | bytes 1572872 | tf_op jit(solution)/shard_map/ppermute | solution.py:301
  24.5 19.0 %all-to-all-start.1 = ((bf16[8,16,256]{2,1,0:T(8,128)(2,1)}), bf16[8,16,256]{2,1,0:T(8,128)(2,1)S(1)}, u32[]{:S(2)}, u32[]{:S(2)}) async-start(bf16[8,16,256]{2,1,0:T(8,128)(2,1)} %get-tuple-element.41), calls=%async_computation.1 | async-start | bytes 131072 | tf_op jit(solution)/shard_map/all_to_all | solution.py:329
  34.8 23.1 %collective-permute-start.2 = (bf16[256,1024]{1,0:T(8,128)(2,1)}, bf16[256,1024]{1,0:T(8,128)(2,1)S(1)}, u32[]{:S(2)}, u32[]{:S(2)}) collective-permute-start(bf16[256,1024]{1,0:T(8,128)(2,1)} %get-tuple-element.48), channel_id=1, source_target_pairs={{0,1},{1,2},{2,3},{3,0},{4,5},{5,6},{6,7},{7,4},{8,9},{9,10},{10,1... | collective-permute-start | bytes 1572872 | tf_op jit(solution)/shard_map/ppermute | solution.py:301
  38.2 19.7 %collective-permute-start.3 = (bf16[256,1024]{1,0:T(8,128)(2,1)}, bf16[256,1024]{1,0:T(8,128)(2,1)S(1)}, u32[]{:S(2)}, u32[]{:S(2)}) collective-permute-start(bf16[256,1024]{1,0:T(8,128)(2,1)} %get-tuple-element.50), channel_id=1, source_target_pairs={{0,3},{1,0},{2,1},{3,2},{4,7},{5,4},{6,5},{7,6},{8,11},{9,8},{10,9... | collective-permute-start | bytes 1572872 | tf_op jit(solution)/shard_map/ppermute | solution.py:301
  45.2 12.6 %all-to-all-start.2 = ((bf16[4,128,256]{2,1,0:T(8,128)(2,1)}), bf16[4,128,256]{2,1,0:T(8,128)(2,1)S(1)}, u32[]{:S(2)}, u32[]{:S(2)}) async-start(bf16[4,128,256]{2,1,0:T(8,128)(2,1)} %get-tuple-element.44), calls=%async_computation.2 | async-start | bytes 524288 | tf_op jit(solution)/shard_map/all_to_all | solution.py:341

commit v10 on v8

--- a/solution.py
+++ b/solution.py
@@ -133,7 +133,7 @@
         copy.wait()
 
 
-def join_body(rows, rim_ref, head_ref, taps_ref, rate_ref, state_ref, out_ref, late_ref, top_ref, pad):
+def join_body(rows, rim_ref, head_ref, taps_ref, rate_ref, state_ref, out_hbm, late_ref, top_ref, pad, whole, sems):
     modes, channels = rate_ref.shape
     taps = taps_ref.shape[1]
     sums = []
@@ -145,37 +145,42 @@
             total = total + taps_ref[i, pl.ds(t, 1), :] * pad[i, pl.ds(HEAD - t, HEAD), :]
         sums.append(total)
     gated = sums[1] * sums[2]
-    top_ref[0] = sums[0]
-    top_ref[1] = gated
     more = gated - head_ref[1] * head_ref[2]
     rate = rate_ref[...]
     retain = jnp.exp(-rate)
     late = jnp.broadcast_to(more[:1], rate.shape)
     for i in range(1, taps - 1):
         late = retain * late + more[i : i + 1]
+    whole[...] = (state_ref[...] + jnp.exp(-(rows - taps + 1) * rate) * late).astype(BF16)
+    peers = out_hbm.shape[0]
+    copies = fetch([whole] * peers, [out_hbm.at[i] for i in range(peers)], sems)
+    top_ref[0] = sums[0]
+    top_ref[1] = gated
     late_ref[...] = late
-    whole = (state_ref[...] + jnp.exp(-(rows - taps + 1) * rate) * late).astype(BF16)
-    for i in range(out_ref.shape[0]):
-        out_ref[i] = whole
-
-
-def plane_body(rows, parts_ref, rate_ref, _block, before_ref, total_ref, _same_block):
+    for copy in copies:
+        copy.wait()
+
+
+def plane_body(rows, parts_ref, rate_ref, _block, before_ref, total_hbm, _same_block, held, sems):
     me = lax.axis_index("y") * lax.axis_size("core") + lax.axis_index("core")
     drop = jnp.exp(-rows * rate_ref[...])
-    before = jnp.zeros(rate_ref.shape, F32)
     total = jnp.zeros(rate_ref.shape, F32)
     for i in range(parts_ref.shape[0]):
-        part = parts_ref[i].astype(F32)
-        before = jnp.where(i < me, before * drop + part, before)
-        total = total * drop + part
+        total = total * drop + parts_ref[i].astype(F32)
+    held[...] = total.astype(BF16)
+    planes = total_hbm.shape[0]
+    copies = fetch([held] * planes, [total_hbm.at[i] for i in range(planes)], sems)
+    before = jnp.zeros(rate_ref.shape, F32)
+    for i in range(parts_ref.shape[0]):
+        before = jnp.where(i < me, before * drop + parts_ref[i].astype(F32), before)
     before_ref[...] = before
-    for i in range(total_ref.shape[0]):
-        total_ref[i] = total.astype(BF16)
+    for copy in copies:
+        copy.wait()
 
 
 def mix_body(
     taps, plane_rows, query_ref, gated_ref, begin_ref, late_ref, top_ref, before_ref, planes_ref, rate_ref, amp_ref,
-    skip_ref, weight_hbm, out_ref, own_ref, hyena, carry, sem,
+    skip_ref, weight_hbm, out_hbm, own_ref, hyena, left, carry, sem, sems,
 ):
     halves, rows, _ = query_ref.shape
     modes = rate_ref.shape[0]
@@ -193,6 +198,7 @@
     carried = before_ref[...] + jnp.exp(-(rows * me).astype(F32) * rate) * behind
     carry[0] = carried
     carry[1] = carried + jnp.exp((taps - 1) * rate) * late_ref[...]
+    parts, copies = out_hbm.shape[0], []
     sub = lax.broadcasted_iota(jnp.int32, (SUBS, LANES), 0)
     ahead = sub.astype(F32) * float(steps)
     for half in range(halves):
@@ -219,9 +225,10 @@
             while len(terms) > 1:
                 terms = [x + y for x, y in zip(terms[::2], terms[1::2])] + terms[len(terms) // 2 * 2 :]
             hyena[half, at, :] = query * terms[0]
-    left = jnp.concatenate([hyena[half].astype(BF16) for half in range(halves)], axis=1)
-    for i in range(out_ref.shape[0]):
-        out_ref[i] = left
+        left[:, lanes] = hyena[half].astype(BF16)
+        copies += fetch([left.at[:, lanes]] * parts, [out_hbm.at[i, :, lanes] for i in range(parts)], sems.at[half])
+    for copy in copies:
+        copy.wait()
     own.wait()
 
 
@@ -305,7 +312,12 @@
             shape((2, HEAD, channels), F32),
         ),
         "join",
-        [pltpu.VMEM((3, 2 * HEAD, channels), F32)],
+        [
+            pltpu.VMEM((3, 2 * HEAD, channels), F32),
+            pltpu.VMEM((modes, channels), BF16),
+            pltpu.SemaphoreType.DMA((plane,)),
+        ],
+        out_spec=(HBM, VMEM, VMEM),
     )(rims, heads, taps_here, rate, states)
     states = lax.all_to_all(states, ("y", "core"), 0, 0, tiled=True)
     before, totals, blocks[2] = call(
@@ -313,7 +325,8 @@
         [VMEM] * 2 + [ANY],
         (shape((modes, channels), F32), shape((planes, modes, channels), BF16), shape((channels, width), BF16)),
         "plane",
-        out_spec=(VMEM, VMEM, ANY),
+        [pltpu.VMEM((modes, channels), BF16), pltpu.SemaphoreType.DMA((planes,))],
+        out_spec=(VMEM, HBM, ANY),
         aliases={2: 2},
     )(states, rate, blocks[2])
     blocks[2] = to_next(blocks[2], 3)
@@ -325,9 +338,12 @@
         "mix",
         [
             pltpu.VMEM(by_half, F32),
+            pltpu.VMEM((rows, channels), BF16),
             pltpu.VMEM((2, modes, channels), F32),
             pltpu.SemaphoreType.DMA,
+            pltpu.SemaphoreType.DMA((channels // LANES, parts)),
         ],
+        out_spec=(HBM, VMEM),
     )(queries, gated, begin, late, top, before, totals, rate, amplitude, skip, out_weight)
     hyena = lax.all_to_all(hyena, "tp", 0, 0, tiled=True)
     hyena, *blocks[:2] = call(

time: 57 us -> 57.1 us (level)
  no operation moved by 1% of the time
where the time goes in v10:
time: 57.1 us; the launch traced here: 56.2 us
  starting transfers between devices  36.7 us (64%)
  waiting for transfers between devices  11.8 us (21%)
  Pallas kernels  7.63 us (13%)
    ppermute x3, starting transfers between devices, to_next(): lax.ppermute(block, 'tp', [(i, (i + d) % parts) for i in range(parts)])  11.9 us
    all_to_all x1, starting transfers between devices, local(): totals = lax.all_to_all(totals, 'z', 0, 0, tiled=True)  10 us
    all_to_all x1, starting transfers between devices, local(): states = lax.all_to_all(states, ('y', 'core'), 0, 0, tiled=True)  6.14 us
    all_to_all x1, waiting for transfers between devices, local(): hyena = lax.all_to_all(hyena, 'tp', 0, 0, tiled=True)  5.52 us
    ppermute x1, starting transfers between devices, local(): rims = lax.ppermute(rims, order, [(i, i + 1) for i in range(devices - 1)])  4.59 us
    all_to_all x1, starting transfers between devices, local(): hyena = lax.all_to_all(hyena, 'tp', 0, 0, tiled=True)  4.03 us
    all_to_all x1, waiting for transfers between devices, local(): totals = lax.all_to_all(totals, 'z', 0, 0, tiled=True)  3.05 us
    pallas_call x1, Pallas kernels, local(): call(gate_body, [HBM] * 8, (shape(by_half, F32), shape(by_half, F32), sha...  2.66 us
  transfers between devices with their start and end apart: 7, of which 4 were waited for; matrix products, arithmetic and copies ran while one was open for 0% of the time, Pallas kernels for 9%

profile of v10, /device:TPU:1, one launch (start us, length us, event | category | flops | bytes accessed | tf_op | source)
XLA Modules:
  0.0 56.2 jit_solution(14557185919420760117)
XLA Ops:
  0.0 0.8 %rims.1 = bf16[48,256]{1,0:T(8,128)(2,1)S(1)} custom-call(bf16[128,256]{1,0:T(8,128)(2,1)} %q_ref.1, bf16[128,256]{1,0:T(8,128)(2,1)} %k_ref.1, bf16[128,256]{1,0:T(8,128)(2,1)} %v_ref.1), custom_call_target="tpu_custom_call" | custom-call | tf_op jit(solution)/shard_map/rims/pallas_call | solution.py:275
  0.8 4.6 %collective-permute-start = (bf16[48,256]{1,0:T(8,128)(2,1)S(1)}, bf16[48,256]{1,0:T(8,128)(2,1)S(1)}, u32[]{:S(2)}, u32[]{:S(2)}) collective-permute-start(bf16[48,256]{1,0:T(8,128)(2,1)S(1)} %rims.1), channel_id=1, source_target_pairs={{0,4},{4,8},{8,12},{12,16},{16,20},{20,24},{24,28},{28,32},{32,36}... | collective-permute-start | bytes 73736 | tf_op jit(solution)/shard_map/ppermute | solution.py:278
  5.4 2.7 %gate.1 = (f32[2,128,128]{2,1,0:T(8,128)S(1)}, f32[2,128,128]{2,1,0:T(8,128)S(1)}, f32[16,8,256]{2,1,0:T(8,128)S(1)}, f32[16,256]{1,0:T(8,128)S(1)}, f32[3,8,256...) custom-call(bf16[128,256]{1,0:T(8,128)(2,1)} %q_ref.1, ...), custom_call_target="tpu_custom_call" | custom-call | tf_op jit(solution)/shard_map/gate/pallas_call | solution.py:279
  8.0 1.6 %collective-permute-done.refs_0_ = bf16[48,256]{1,0:T(8,128)(2,1)S(1)} collective-permute-done((bf16[48,256]{1,0:T(8,128)(2,1)S(1)}, bf16[48,256]{1,0:T(8,128)(2,1)S(1)}, u32[]{:S(2)}, u32[]{:S(2)}) %collective-permute-start) | collective-permute-done | bytes 24608 | tf_op jit(solution)/shard_map/ppermute | solution.py:278
  9.6 0.9 %join.1 = (bf16[16,16,256]{2,1,0:T(8,128)(2,1)}, f32[16,256]{1,0:T(8,128)S(1)}, f32[2,8,256]{2,1,0:T(8,128)S(1)}) custom-call(bf16[48,256]{1,0:T(8,128)(2,1)S(1)} %collective-permute-done.refs_0_, f32[3,8,256]{2,1,0:T(8,128)S(1)} %get-tuple-element.31.refs_1_, f32[3,7,256]{2,1,0:T(8,128)S(1)} %get-tuple-element.32.refs_2_, ...), custom_call_target="tpu_custom_call" | custom-call | tf_op jit(solution)/shard_map/join/pallas_call | solution.py:306
  10.5 6.1 %all-to-all-start = ((bf16[16,16,256]{2,1,0:T(8,128)(2,1)}), bf16[16,16,256]{2,1,0:T(8,128)(2,1)S(1)}, u32[]{:S(2)}, u32[]{:S(2)}) async-start(bf16[16,16,256]{2,1,0:T(8,128)(2,1)} %get-tuple-element.37), calls=%async_computation | async-start | bytes 262144 | tf_op jit(solution)/shard_map/all_to_all | solution.py:322
  16.6 3.1 %collective-permute-start.1 = (bf16[256,1024]{1,0:T(8,128)(2,1)}, bf16[256,1024]{1,0:T(8,128)(2,1)S(1)}, u32[]{:S(2)}, u32[]{:S(2)}) collective-permute-start(bf16[256,1024]{1,0:T(8,128)(2,1)} %get-tuple-element.44), channel_id=1, source_target_pairs={{0,1},{1,2},{2,3},{3,0},{4,5},{5,6},{6,7},{7,4},{8,9},{9,10},{10,1... | collective-permute-start | bytes 1572872 | tf_op jit(solution)/shard_map/ppermute | solution.py:303
  19.8 4.4 %collective-permute-start.2 = (bf16[256,1024]{1,0:T(8,128)(2,1)}, bf16[256,1024]{1,0:T(8,128)(2,1)S(1)}, u32[]{:S(2)}, u32[]{:S(2)}) collective-permute-start(bf16[256,1024]{1,0:T(8,128)(2,1)} %get-tuple-element.45), channel_id=1, source_target_pairs={{0,2},{1,3},{2,0},{3,1},{4,6},{5,7},{6,4},{7,5},{8,10},{9,11},{10,... | collective-permute-start | bytes 1572872 | tf_op jit(solution)/shard_map/ppermute | solution.py:303
  24.1 1.7 %all-to-all-done.refs_0_ = bf16[16,16,256]{2,1,0:T(8,128)(2,1)S(1)} async-done(((bf16[16,16,256]{2,1,0:T(8,128)(2,1)}), bf16[16,16,256]{2,1,0:T(8,128)(2,1)S(1)}, u32[]{:S(2)}, u32[]{:S(2)}) %all-to-all-start) | async-done | bytes 131104 | tf_op jit(solution)/shard_map/all_to_all | solution.py:322
  25.8 0.8 %plane.1 = (f32[16,256]{1,0:T(8,128)S(1)}, bf16[8,16,256]{2,1,0:T(8,128)(2,1)}, bf16[256,1024]{1,0:T(8,128)(2,1)S(1)}) custom-call(bf16[16,16,256]{2,1,0:T(8,128)(2,1)S(1)} %all-to-all-done.refs_0_, f32[16,256]{1,0:T(8,128)S(1)} %get-tuple-element.33.refs_3_.refs_1_.refs_7_, ...), custom_call_target="tpu_custom_call", output_to_operand_aliasing={{2}: (2, {})} | custom-call | tf_op jit(solution)/shard_map/plane/pallas_call | solution.py:323
  26.5 10.0 %all-to-all-start.1 = ((bf16[8,16,256]{2,1,0:T(8,128)(2,1)}), bf16[8,16,256]{2,1,0:T(8,128)(2,1)S(1)}, u32[]{:S(2)}, u32[]{:S(2)}) async-start(bf16[8,16,256]{2,1,0:T(8,128)(2,1)} %get-tuple-element.40), calls=%async_computation.1 | async-start | bytes 131072 | tf_op jit(solution)/shard_map/all_to_all | solution.py:333
  36.6 4.4 %collective-permute-start.3 = (bf16[256,1024]{1,0:T(8,128)(2,1)S(1)}, bf16[256,1024]{1,0:T(8,128)(2,1)S(1)}, u32[]{:S(2)}, u32[]{:S(2)}) collective-permute-start(bf16[256,1024]{1,0:T(8,128)(2,1)S(1)} %get-tuple-element.50), channel_id=1, source_target_pairs={{0,3},{1,0},{2,1},{3,2},{4,7},{5,4},{6,5},{7,6},{8,11},{9,8},{10,9... | collective-permute-start | bytes 1572872 | tf_op jit(solution)/shard_map/ppermute | solution.py:303
  41.0 3.0 %all-to-all-done.1.refs_6_ = bf16[8,16,256]{2,1,0:T(8,128)(2,1)S(1)} async-done(((bf16[8,16,256]{2,1,0:T(8,128)(2,1)}), bf16[8,16,256]{2,1,0:T(8,128)(2,1)S(1)}, u32[]{:S(2)}, u32[]{:S(2)}) %all-to-all-start.1) | async-done | bytes 65568 | tf_op jit(solution)/shard_map/all_to_all | solution.py:333
  44.0 1.4 %mix.1 = (bf16[4,128,256]{2,1,0:T(8,128)(2,1)}, bf16[256,1024]{1,0:T(8,128)(2,1)S(1)}) custom-call(f32[2,128,128]{2,1,0:T(8,128)S(1)} %get-tuple-element.28.refs_0_, f32[2,128,128]{2,1,0:T(8,128)S(1)} %get-tuple-element.29.refs_1_, f32[16,8,256]{2,1,0:T(8,128)S(1)} %get-tuple-element.30.refs_2_, f32[16,256]{1,0:T(8,128)S(1)} %get-tuple-element.35.refs_3_, ...), custom_call_target="tpu_custom_call" | custom-call | tf_op jit(solution)/shard_map/mix/pallas_call | solution.py:334
  45.5 4.0 %all-to-all-start.2 = ((bf16[4,128,256]{2,1,0:T(8,128)(2,1)}), bf16[4,128,256]{2,1,0:T(8,128)(2,1)S(1)}, u32[]{:S(2)}, u32[]{:S(2)}) async-start(bf16[4,128,256]{2,1,0:T(8,128)(2,1)} %get-tuple-element.43), calls=%async_computation.2 | async-start | bytes 524288 | tf_op jit(solution)/shard_map/all_to_all | solution.py:348
  49.5 0.0 collective-permute-done.1._side
  49.5 0.0 collective-permute-done.2._across
  49.5 5.5 %all-to-all-done.2.left_ref = bf16[4,128,256]{2,1,0:T(8,128)(2,1)S(1)} async-done(((bf16[4,128,256]{2,1,0:T(8,128)(2,1)}), bf16[4,128,256]{2,1,0:T(8,128)(2,1)S(1)}, u32[]{:S(2)}, u32[]{:S(2)}) %all-to-all-start.2) | async-done | bytes 262176 | tf_op jit(solution)/shard_map/all_to_all | solution.py:348
  55.1 0.0 collective-permute-done.3.rest_3_
  55.1 1.1 %project.1 = bf16[128,1024]{1,0:T(8,128)(2,1)} custom-call(bf16[128,1024]{1,0:T(8,128)(2,1)S(1)} %get-tuple-element.46.left_ref, bf16[256,1024]{1,0:T(8,128)(2,1)S(1)} %get-tuple-element.47.rest_0_, bf16[256,1024]{1,0:T(8,128)(2,1)S(1)} %get-tuple-element.48.rest_1_, bf16[256,1024]{1,0:T(8,128)(2,1)S(1)} %get-tuple-element.49.rest_2_, ...), custom_call_target="tpu_custom_call" | custom-call | tf_op jit(solution)/shard_map/project/pallas_call | solution.py:359
  (1 shorter events, 0.0 us)
Async XLA Ops:
  0.8 8.8 %collective-permute-start = (bf16[48,256]{1,0:T(8,128)(2,1)S(1)}, bf16[48,256]{1,0:T(8,128)(2,1)S(1)}, u32[]{:S(2)}, u32[]{:S(2)}) collective-permute-start(bf16[48,256]{1,0:T(8,128)(2,1)S(1)} %rims.1), channel_id=1, source_target_pairs={{0,4},{4,8},{8,12},{12,16},{16,20},{20,24},{24,28},{28,32},{32,36}... | collective-permute-start | bytes 73736 | tf_op jit(solution)/shard_map/ppermute | solution.py:278
  10.5 15.3 %all-to-all-start = ((bf16[16,16,256]{2,1,0:T(8,128)(2,1)}), bf16[16,16,256]{2,1,0:T(8,128)(2,1)S(1)}, u32[]{:S(2)}, u32[]{:S(2)}) async-start(bf16[16,16,256]{2,1,0:T(8,128)(2,1)} %get-tuple-element.37), calls=%async_computation | async-start | bytes 262144 | tf_op jit(solution)/shard_map/all_to_all | solution.py:322
  16.6 32.9 %collective-permute-start.1 = (bf16[256,1024]{1,0:T(8,128)(2,1)}, bf16[256,1024]{1,0:T(8,128)(2,1)S(1)}, u32[]{:S(2)}, u32[]{:S(2)}) collective-permute-start(bf16[256,1024]{1,0:T(8,128)(2,1)} %get-tuple-element.44), channel_id=1, source_target_pairs={{0,1},{1,2},{2,3},{3,0},{4,5},{5,6},{6,7},{7,4},{8,9},{9,10},{10,1... | collective-permute-start | bytes 1572872 | tf_op jit(solution)/shard_map/ppermute | solution.py:303
  19.8 29.7 %collective-permute-start.2 = (bf16[256,1024]{1,0:T(8,128)(2,1)}, bf16[256,1024]{1,0:T(8,128)(2,1)S(1)}, u32[]{:S(2)}, u32[]{:S(2)}) collective-permute-start(bf16[256,1024]{1,0:T(8,128)(2,1)} %get-tuple-element.45), channel_id=1, source_target_pairs={{0,2},{1,3},{2,0},{3,1},{4,6},{5,7},{6,4},{7,5},{8,10},{9,11},{10,... | collective-permute-start | bytes 1572872 | tf_op jit(solution)/shard_map/ppermute | solution.py:303
  26.5 17.5 %all-to-all-start.1 = ((bf16[8,16,256]{2,1,0:T(8,128)(2,1)}), bf16[8,16,256]{2,1,0:T(8,128)(2,1)S(1)}, u32[]{:S(2)}, u32[]{:S(2)}) async-start(bf16[8,16,256]{2,1,0:T(8,128)(2,1)} %get-tuple-element.40), calls=%async_computation.1 | async-start | bytes 131072 | tf_op jit(solution)/shard_map/all_to_all | solution.py:333
  36.6 18.5 %collective-permute-start.3 = (bf16[256,1024]{1,0:T(8,128)(2,1)S(1)}, bf16[256,1024]{1,0:T(8,128)(2,1)S(1)}, u32[]{:S(2)}, u32[]{:S(2)}) collective-permute-start(bf16[256,1024]{1,0:T(8,128)(2,1)S(1)} %get-tuple-element.50), channel_id=1, source_target_pairs={{0,3},{1,0},{2,1},{3,2},{4,7},{5,4},{6,5},{7,6},{8,11},{9,8},{10,9... | collective-permute-start | bytes 1572872 | tf_op jit(solution)/shard_map/ppermute | solution.py:303
  45.5 9.6 %all-to-all-start.2 = ((bf16[4,128,256]{2,1,0:T(8,128)(2,1)}), bf16[4,128,256]{2,1,0:T(8,128)(2,1)S(1)}, u32[]{:S(2)}, u32[]{:S(2)}) async-start(bf16[4,128,256]{2,1,0:T(8,128)(2,1)} %get-tuple-element.43), calls=%async_computation.2 | async-start | bytes 524288 | tf_op jit(solution)/shard_map/all_to_all | solution.py:348

commit v11 on v8

--- a/solution.py
+++ b/solution.py
@@ -76,7 +76,7 @@
     q_hbm, k_hbm, v_hbm, taps_hbm, rate_hbm, residue_hbm, skip_hbm, weight_hbm,
     query_ref, gated_ref, begin_ref, state_ref, head_ref, taps_ref, rate_ref, amp_ref, skip_ref, *rest,
 ):
-    *blocks, streams, residue_ref, pad, sems = rest
+    *blocks, own_ref, streams, residue_ref, pad, sems = rest
     here, parts = lax.axis_index("tp"), lax.axis_size("tp")
     width = blocks[0].shape[1]
     _, rows, channels = streams.shape
@@ -93,6 +93,7 @@
         blocks,
         sems.at[pl.ds(7, parts - 1)],
     )
+    sent += fetch([weight_hbm.at[:, pl.ds(here * width, width)]], [own_ref], sems.at[pl.ds(6 + parts, 1)])
     for copy in copies:
         copy.wait()
     amp_ref[...] = residue_ref[...] * jnp.sqrt(one_minus_exp(2.0 * rate_ref[...]))
@@ -173,26 +174,14 @@
         total_ref[i] = total.astype(BF16)
 
 
-def mix_body(
-    taps, plane_rows, query_ref, gated_ref, begin_ref, late_ref, top_ref, before_ref, planes_ref, rate_ref, amp_ref,
-    skip_ref, weight_hbm, out_ref, own_ref, hyena, carry, sem,
-):
+def mix(taps, carried, refs, out_hbm, hyena, left, carry, sems):
+    query_ref, gated_ref, begin_ref, late_ref, top_ref, rate_ref, amp_ref, skip_ref = refs
     halves, rows, _ = query_ref.shape
     modes = rate_ref.shape[0]
     steps = rows // SUBS
-    width = own_ref.shape[1]
-    own = pltpu.make_async_copy(weight_hbm.at[:, pl.ds(lax.axis_index("tp") * width, width)], own_ref, sem)
-    own.start()
-    z = lax.axis_index("z")
-    me = lax.axis_index("y") * lax.axis_size("core") + lax.axis_index("core")
-    rate = rate_ref[...]
-    drop = jnp.exp(-plane_rows * rate)
-    behind = jnp.zeros(rate.shape, F32)
-    for i in range(planes_ref.shape[0]):
-        behind = jnp.where(i < z, behind * drop + planes_ref[i].astype(F32), behind)
-    carried = before_ref[...] + jnp.exp(-(rows * me).astype(F32) * rate) * behind
     carry[0] = carried
-    carry[1] = carried + jnp.exp((taps - 1) * rate) * late_ref[...]
+    carry[1] = carried + jnp.exp((taps - 1) * rate_ref[...]) * late_ref[...]
+    parts, copies = out_hbm.shape[0], []
     sub = lax.broadcasted_iota(jnp.int32, (SUBS, LANES), 0)
     ahead = sub.astype(F32) * float(steps)
     for half in range(halves):
@@ -219,10 +208,48 @@
             while len(terms) > 1:
                 terms = [x + y for x, y in zip(terms[::2], terms[1::2])] + terms[len(terms) // 2 * 2 :]
             hyena[half, at, :] = query * terms[0]
-    left = jnp.concatenate([hyena[half].astype(BF16) for half in range(halves)], axis=1)
-    for i in range(out_ref.shape[0]):
-        out_ref[i] = left
-    own.wait()
+        left[:, lanes] = hyena[half].astype(BF16)
+        copies += fetch([left.at[:, lanes]] * parts, [out_hbm.at[i, :, lanes] for i in range(parts)], sems.at[half])
+    for copy in copies:
+        copy.wait()
+
+
+def plane_body(taps, rows, parts_ref, _block, *refs):
+    *refs, before_ref, total_ref, _same_block, out_hbm, hyena, left, carry, sems = refs
+    rate_ref = refs[5]
+    me = lax.axis_index("y") * lax.axis_size("core") + lax.axis_index("core")
+    drop = jnp.exp(-rows * rate_ref[...])
+    before = jnp.zeros(rate_ref.shape, F32)
+    total = jnp.zeros(rate_ref.shape, F32)
+    for i in range(parts_ref.shape[0]):
+        part = parts_ref[i].astype(F32)
+        before = jnp.where(i < me, before * drop + part, before)
+        total = total * drop + part
+    before_ref[...] = before
+    for i in range(total_ref.shape[0]):
+        total_ref[i] = total.astype(BF16)
+
+    @pl.when(lax.axis_index("z") == 0)
+    def _():
+        mix(taps, before, refs, out_hbm, hyena, left, carry, sems)
+
+
+def mix_body(taps, plane_rows, before_ref, planes_ref, _hyena, *refs):
+    *refs, out_hbm, hyena, left, carry, sems = refs
+    query_ref, rate_ref = refs[0], refs[5]
+    rows = query_ref.shape[1]
+    z = lax.axis_index("z")
+
+    @pl.when(z > 0)
+    def _():
+        me = lax.axis_index("y") * lax.axis_size("core") + lax.axis_index("core")
+        rate = rate_ref[...]
+        drop = jnp.exp(-plane_rows * rate)
+        behind = jnp.zeros(rate.shape, F32)
+        for i in range(planes_ref.shape[0]):
+            behind = jnp.where(i < z, behind * drop + planes_ref[i].astype(F32), behind)
+        carried = before_ref[...] + jnp.exp(-(rows * me).astype(F32) * rate) * behind
+        mix(taps, carried, refs, out_hbm, hyena, left, carry, sems)
 
 
 def order_body(left_ref, _side, _across, out_ref, _same_side, _same_across):
@@ -269,7 +296,7 @@
         rim_body, [HBM] * 3, shape((3 * RIM, channels), BF16), "rims", [pltpu.SemaphoreType.DMA((3,))]
     )(query_in, key_in, value_in)
     rims = lax.ppermute(rims, order, [(i, i + 1) for i in range(devices - 1)])
-    queries, gated, begin, states, heads, taps_here, rate, amplitude, skip, *blocks = call(
+    queries, gated, begin, states, heads, taps_here, rate, amplitude, skip, *blocks, own = call(
         gate_body,
         [HBM] * 8,
         (
@@ -283,13 +310,14 @@
             shape((modes, channels), F32),
             shape((1, channels), F32),
             *[shape((channels, width), BF16)] * (parts - 1),
+            pltpu.VMEM((channels, width), BF16),
         ),
         "gate",
         [
             pltpu.VMEM((3, rows, channels), BF16),
             pltpu.VMEM((modes, channels), F32),
             pltpu.VMEM((3, HEAD + rows, channels), F32),
-            pltpu.SemaphoreType.DMA((7 + parts - 1,)),
+            pltpu.SemaphoreType.DMA((7 + parts,)),
         ],
     )(query_in, key_in, value_in, short_weight, rate, residue, skip, out_weight)
     def to_next(block, d):
@@ -308,27 +336,38 @@
         [pltpu.VMEM((3, 2 * HEAD, channels), F32)],
     )(rims, heads, taps_here, rate, states)
     states = lax.all_to_all(states, ("y", "core"), 0, 0, tiled=True)
-    before, totals, blocks[2] = call(
-        lambda *refs: plane_body(rows, *refs),
-        [VMEM] * 2 + [ANY],
-        (shape((modes, channels), F32), shape((planes, modes, channels), BF16), shape((channels, width), BF16)),
+    shared = (queries, gated, begin, late, top, rate, amplitude, skip)
+    scratch = [
+        pltpu.VMEM(by_half, F32),
+        pltpu.VMEM((rows, channels), BF16),
+        pltpu.VMEM((2, modes, channels), F32),
+        pltpu.SemaphoreType.DMA((channels // LANES, parts)),
+    ]
+    before, totals, blocks[2], hyena = call(
+        lambda *refs: plane_body(taps, rows, *refs),
+        [VMEM, ANY] + [VMEM] * len(shared),
+        (
+            shape((modes, channels), F32),
+            shape((planes, modes, channels), BF16),
+            shape((channels, width), BF16),
+            pltpu.HBM((parts, rows, channels), BF16),
+        ),
         "plane",
-        out_spec=(VMEM, VMEM, ANY),
-        aliases={2: 2},
-    )(states, rate, blocks[2])
+        scratch,
+        out_spec=(VMEM, VMEM, ANY, HBM),
+        aliases={1: 2},
+    )(states, blocks[2], *shared)
     blocks[2] = to_next(blocks[2], 3)
     totals = lax.all_to_all(totals, "z", 0, 0, tiled=True)
-    hyena, own = call(
+    hyena = call(
         lambda *refs: mix_body(taps, rows * plane, *refs),
-        [VMEM] * 10 + [HBM],
-        (shape((parts, rows, channels), BF16), shape((channels, width), BF16)),
+        [VMEM] * 2 + [HBM] + [VMEM] * len(shared),
+        pltpu.HBM((parts, rows, channels), BF16),
         "mix",
-        [
-            pltpu.VMEM(by_half, F32),
-            pltpu.VMEM((2, modes, channels), F32),
-            pltpu.SemaphoreType.DMA,
-        ],
-    )(queries, gated, begin, late, top, before, totals, rate, amplitude, skip, out_weight)
+        scratch,
+        out_spec=HBM,
+        aliases={2: 0},
+    )(before, totals, hyena, *shared)
     hyena = lax.all_to_all(hyena, "tp", 0, 0, tiled=True)
     hyena, *blocks[:2] = call(
         order_body,

time: 57 us -> 56.9 us (level)
  waiting for transfers between devices: 11.8 us -> 13.1 us
  starting transfers between devices: 36.7 us -> 35.6 us
    all_to_all x1, waiting for transfers between devices: 5.52 us -> 6.99 us  [local(): hyena = lax.all_to_all(hyena, 'tp', 0, 0, tiled=True)]
    all_to_all x1, starting transfers between devices: 10 us -> 8.98 us  [local(): totals = lax.all_to_all(totals, 'z', 0, 0, tiled=True)]
  transfers between devices with their start and end apart: 7 -> 7, of which waited for: 4 -> 4; matrix products, arithmetic and copies ran while one was open for 0% -> 0% of each run, Pallas kernels for 9% -> 8%
where the time goes in v11:
time: 56.9 us; the launch traced here: 56.2 us
  starting transfers between devices  35.6 us (63%)
  waiting for transfers between devices  13.1 us (23%)
  Pallas kernels  7.35 us (13%)
    ppermute x3, starting transfers between devices, to_next(): lax.ppermute(block, 'tp', [(i, (i + d) % parts) for i in range(parts)])  11.9 us
    all_to_all x1, starting transfers between devices, local(): totals = lax.all_to_all(totals, 'z', 0, 0, tiled=True)  8.98 us
    all_to_all x1, waiting for transfers between devices, local(): hyena = lax.all_to_all(hyena, 'tp', 0, 0, tiled=True)  6.99 us
    all_to_all x1, starting transfers between devices, local(): states = lax.all_to_all(states, ('y', 'core'), 0, 0, tiled=True)  6.13 us
    ppermute x1, starting transfers between devices, local(): rims = lax.ppermute(rims, order, [(i, i + 1) for i in range(devices - 1)])  4.59 us
    all_to_all x1, starting transfers between devices, local(): hyena = lax.all_to_all(hyena, 'tp', 0, 0, tiled=True)  4.03 us
    all_to_all x1, waiting for transfers between devices, local(): totals = lax.all_to_all(totals, 'z', 0, 0, tiled=True)  3.05 us
    pallas_call x1, Pallas kernels, local(): call(gate_body, [HBM] * 8, (shape(by_half, F32), shape(by_half, F32), sha...  2.79 us
  transfers between devices with their start and end apart: 7, of which 4 were waited for; matrix products, arithmetic and copies ran while one was open for 0% of the time, Pallas kernels for 8%

profile of v11, /device:TPU:1, one launch (start us, length us, event | category | flops | bytes accessed | tf_op | source)
XLA Modules:
  0.0 56.2 jit_solution(5409103719942485661)
XLA Ops:
  0.0 0.8 %rims.1 = bf16[48,256]{1,0:T(8,128)(2,1)S(1)} custom-call(bf16[128,256]{1,0:T(8,128)(2,1)} %q_hbm.1, bf16[128,256]{1,0:T(8,128)(2,1)} %k_hbm.1, bf16[128,256]{1,0:T(8,128)(2,1)} %v_hbm.1), custom_call_target="tpu_custom_call" | custom-call | tf_op jit(solution)/shard_map/rims/pallas_call | solution.py:295
  0.8 4.6 %collective-permute-start = (bf16[48,256]{1,0:T(8,128)(2,1)S(1)}, bf16[48,256]{1,0:T(8,128)(2,1)S(1)}, u32[]{:S(2)}, u32[]{:S(2)}) collective-permute-start(bf16[48,256]{1,0:T(8,128)(2,1)S(1)} %rims.1), channel_id=1, source_target_pairs={{0,4},{4,8},{8,12},{12,16},{16,20},{20,24},{24,28},{28,32},{32,36}... | collective-permute-start | bytes 73736 | tf_op jit(solution)/shard_map/ppermute | solution.py:298
  5.4 2.8 %gate.1 = (f32[2,128,128]{2,1,0:T(8,128)S(1)}, f32[2,128,128]{2,1,0:T(8,128)S(1)}, f32[16,8,256]{2,1,0:T(8,128)S(1)}, f32[16,256]{1,0:T(8,128)S(1)}, f32[3,8,256...) custom-call(bf16[128,256]{1,0:T(8,128)(2,1)} %q_hbm.1, ...), custom_call_target="tpu_custom_call" | custom-call | tf_op jit(solution)/shard_map/gate/pallas_call | solution.py:299
  8.2 1.4 %collective-permute-done.refs_0_ = bf16[48,256]{1,0:T(8,128)(2,1)S(1)} collective-permute-done((bf16[48,256]{1,0:T(8,128)(2,1)S(1)}, bf16[48,256]{1,0:T(8,128)(2,1)S(1)}, u32[]{:S(2)}, u32[]{:S(2)}) %collective-permute-start) | collective-permute-done | bytes 24608 | tf_op jit(solution)/shard_map/ppermute | solution.py:298
  9.6 0.7 %join.1 = (bf16[16,16,256]{2,1,0:T(8,128)(2,1)}, f32[16,256]{1,0:T(8,128)S(1)}, f32[2,8,256]{2,1,0:T(8,128)S(1)}) custom-call(bf16[48,256]{1,0:T(8,128)(2,1)S(1)} %collective-permute-done.refs_0_, f32[3,8,256]{2,1,0:T(8,128)S(1)} %get-tuple-element.28.refs_1_, f32[3,7,256]{2,1,0:T(8,128)S(1)} %get-tuple-element.29.refs_2_, ...), custom_call_target="tpu_custom_call" | custom-call | tf_op jit(solution)/shard_map/join/pallas_call | solution.py:327
  10.3 6.1 %all-to-all-start = ((bf16[16,16,256]{2,1,0:T(8,128)(2,1)}), bf16[16,16,256]{2,1,0:T(8,128)(2,1)S(1)}, u32[]{:S(2)}, u32[]{:S(2)}) async-start(bf16[16,16,256]{2,1,0:T(8,128)(2,1)} %get-tuple-element.32), calls=%async_computation | async-start | bytes 262144 | tf_op jit(solution)/shard_map/all_to_all | solution.py:338
  16.5 3.1 %collective-permute-start.1 = (bf16[256,1024]{1,0:T(8,128)(2,1)}, bf16[256,1024]{1,0:T(8,128)(2,1)S(1)}, u32[]{:S(2)}, u32[]{:S(2)}) collective-permute-start(bf16[256,1024]{1,0:T(8,128)(2,1)} %get-tuple-element.44), channel_id=1, source_target_pairs={{0,1},{1,2},{2,3},{3,0},{4,5},{5,6},{6,7},{7,4},{8,9},{9,10},{10,1... | collective-permute-start | bytes 1572872 | tf_op jit(solution)/shard_map/ppermute | solution.py:324
  19.6 4.4 %collective-permute-start.2 = (bf16[256,1024]{1,0:T(8,128)(2,1)}, bf16[256,1024]{1,0:T(8,128)(2,1)S(1)}, u32[]{:S(2)}, u32[]{:S(2)}) collective-permute-start(bf16[256,1024]{1,0:T(8,128)(2,1)} %get-tuple-element.45), channel_id=1, source_target_pairs={{0,2},{1,3},{2,0},{3,1},{4,6},{5,7},{6,4},{7,5},{8,10},{9,11},{10,... | collective-permute-start | bytes 1572872 | tf_op jit(solution)/shard_map/ppermute | solution.py:324
  24.0 1.7 %all-to-all-done.refs_0_ = bf16[16,16,256]{2,1,0:T(8,128)(2,1)S(1)} async-done(((bf16[16,16,256]{2,1,0:T(8,128)(2,1)}), bf16[16,16,256]{2,1,0:T(8,128)(2,1)S(1)}, u32[]{:S(2)}, u32[]{:S(2)}) %all-to-all-start) | async-done | bytes 131104 | tf_op jit(solution)/shard_map/all_to_all | solution.py:338
  25.6 1.8 %plane.1 = (f32[16,256]{1,0:T(8,128)S(1)}, bf16[8,16,256]{2,1,0:T(8,128)(2,1)}, bf16[256,1024]{1,0:T(8,128)(2,1)S(1)}, bf16[4,128,256]{2,1,0:T(8,128)(2,1)}) custom-call(bf16[16,16,256]{2,1,0:T(8,128)(2,1)S(1)} %all-to-all-done.refs_0_, bf16[256,1024]{1,0:T(8,128)(2,1)S(1)} %get-tuple-element.33.refs_1_, ...), custom_call_target="tpu_custom_call", output_to_operand_aliasing={{2}: (1, {})} | custom-call | tf_op jit(solution)/shard_map/plane/pallas_call | solution.py:346
  27.5 9.0 %all-to-all-start.1 = ((bf16[8,16,256]{2,1,0:T(8,128)(2,1)}), bf16[8,16,256]{2,1,0:T(8,128)(2,1)S(1)}, u32[]{:S(2)}, u32[]{:S(2)}) async-start(bf16[8,16,256]{2,1,0:T(8,128)(2,1)} %get-tuple-element.42), calls=%async_computation.1 | async-start | bytes 131072 | tf_op jit(solution)/shard_map/all_to_all | solution.py:361
  36.5 4.4 %collective-permute-start.3 = (bf16[256,1024]{1,0:T(8,128)(2,1)S(1)}, bf16[256,1024]{1,0:T(8,128)(2,1)S(1)}, u32[]{:S(2)}, u32[]{:S(2)}) collective-permute-start(bf16[256,1024]{1,0:T(8,128)(2,1)S(1)} %get-tuple-element.50), channel_id=1, source_target_pairs={{0,3},{1,0},{2,1},{3,2},{4,7},{5,4},{6,5},{7,6},{8,11},{9,8},{10,9... | collective-permute-start | bytes 1572872 | tf_op jit(solution)/shard_map/ppermute | solution.py:324
  40.9 3.0 %all-to-all-done.1.refs_1_ = bf16[8,16,256]{2,1,0:T(8,128)(2,1)S(1)} async-done(((bf16[8,16,256]{2,1,0:T(8,128)(2,1)}), bf16[8,16,256]{2,1,0:T(8,128)(2,1)S(1)}, u32[]{:S(2)}, u32[]{:S(2)}) %all-to-all-start.1) | async-done | bytes 65568 | tf_op jit(solution)/shard_map/all_to_all | solution.py:361
  43.9 0.1 mix.1
  44.0 4.0 %all-to-all-start.2 = ((bf16[4,128,256]{2,1,0:T(8,128)(2,1)}), bf16[4,128,256]{2,1,0:T(8,128)(2,1)S(1)}, u32[]{:S(2)}, u32[]{:S(2)}) async-start(bf16[4,128,256]{2,1,0:T(8,128)(2,1)} %mix.1), calls=%async_computation.2 | async-start | bytes 524288 | tf_op jit(solution)/shard_map/all_to_all | solution.py:371
  48.0 0.0 collective-permute-done.1._side
  48.0 0.0 collective-permute-done.2._across
  48.0 7.0 %all-to-all-done.2.left_ref = bf16[4,128,256]{2,1,0:T(8,128)(2,1)S(1)} async-done(((bf16[4,128,256]{2,1,0:T(8,128)(2,1)}), bf16[4,128,256]{2,1,0:T(8,128)(2,1)S(1)}, u32[]{:S(2)}, u32[]{:S(2)}) %all-to-all-start.2) | async-done | bytes 262176 | tf_op jit(solution)/shard_map/all_to_all | solution.py:371
  55.0 0.0 collective-permute-done.3.rest_3_
  55.0 1.1 %project.1 = bf16[128,1024]{1,0:T(8,128)(2,1)} custom-call(bf16[128,1024]{1,0:T(8,128)(2,1)S(1)} %get-tuple-element.46.left_ref, bf16[256,1024]{1,0:T(8,128)(2,1)S(1)} %get-tuple-element.47.rest_0_, bf16[256,1024]{1,0:T(8,128)(2,1)S(1)} %get-tuple-element.48.rest_1_, bf16[256,1024]{1,0:T(8,128)(2,1)S(1)} %get-tuple-element.49.rest_2_, ...), custom_call_target="tpu_custom_call" | custom-call | tf_op jit(solution)/shard_map/project/pallas_call | solution.py:382
  (1 shorter events, 0.0 us)
Async XLA Ops:
  0.8 8.8 %collective-permute-start = (bf16[48,256]{1,0:T(8,128)(2,1)S(1)}, bf16[48,256]{1,0:T(8,128)(2,1)S(1)}, u32[]{:S(2)}, u32[]{:S(2)}) collective-permute-start(bf16[48,256]{1,0:T(8,128)(2,1)S(1)} %rims.1), channel_id=1, source_target_pairs={{0,4},{4,8},{8,12},{12,16},{16,20},{20,24},{24,28},{28,32},{32,36}... | collective-permute-start | bytes 73736 | tf_op jit(solution)/shard_map/ppermute | solution.py:298
  10.3 15.3 %all-to-all-start = ((bf16[16,16,256]{2,1,0:T(8,128)(2,1)}), bf16[16,16,256]{2,1,0:T(8,128)(2,1)S(1)}, u32[]{:S(2)}, u32[]{:S(2)}) async-start(bf16[16,16,256]{2,1,0:T(8,128)(2,1)} %get-tuple-element.32), calls=%async_computation | async-start | bytes 262144 | tf_op jit(solution)/shard_map/all_to_all | solution.py:338
  16.5 31.5 %collective-permute-start.1 = (bf16[256,1024]{1,0:T(8,128)(2,1)}, bf16[256,1024]{1,0:T(8,128)(2,1)S(1)}, u32[]{:S(2)}, u32[]{:S(2)}) collective-permute-start(bf16[256,1024]{1,0:T(8,128)(2,1)} %get-tuple-element.44), channel_id=1, source_target_pairs={{0,1},{1,2},{2,3},{3,0},{4,5},{5,6},{6,7},{7,4},{8,9},{9,10},{10,1... | collective-permute-start | bytes 1572872 | tf_op jit(solution)/shard_map/ppermute | solution.py:324
  19.6 28.4 %collective-permute-start.2 = (bf16[256,1024]{1,0:T(8,128)(2,1)}, bf16[256,1024]{1,0:T(8,128)(2,1)S(1)}, u32[]{:S(2)}, u32[]{:S(2)}) collective-permute-start(bf16[256,1024]{1,0:T(8,128)(2,1)} %get-tuple-element.45), channel_id=1, source_target_pairs={{0,2},{1,3},{2,0},{3,1},{4,6},{5,7},{6,4},{7,5},{8,10},{9,11},{10,... | collective-permute-start | bytes 1572872 | tf_op jit(solution)/shard_map/ppermute | solution.py:324
  27.5 16.4 %all-to-all-start.1 = ((bf16[8,16,256]{2,1,0:T(8,128)(2,1)}), bf16[8,16,256]{2,1,0:T(8,128)(2,1)S(1)}, u32[]{:S(2)}, u32[]{:S(2)}) async-start(bf16[8,16,256]{2,1,0:T(8,128)(2,1)} %get-tuple-element.42), calls=%async_computation.1 | async-start | bytes 131072 | tf_op jit(solution)/shard_map/all_to_all | solution.py:361
  36.5 18.6 %collective-permute-start.3 = (bf16[256,1024]{1,0:T(8,128)(2,1)S(1)}, bf16[256,1024]{1,0:T(8,128)(2,1)S(1)}, u32[]{:S(2)}, u32[]{:S(2)}) collective-permute-start(bf16[256,1024]{1,0:T(8,128)(2,1)S(1)} %get-tuple-element.50), channel_id=1, source_target_pairs={{0,3},{1,0},{2,1},{3,2},{4,7},{5,4},{6,5},{7,6},{8,11},{9,8},{10,9... | collective-permute-start | bytes 1572872 | tf_op jit(solution)/shard_map/ppermute | solution.py:324
  44.0 11.0 %all-to-all-start.2 = ((bf16[4,128,256]{2,1,0:T(8,128)(2,1)}), bf16[4,128,256]{2,1,0:T(8,128)(2,1)S(1)}, u32[]{:S(2)}, u32[]{:S(2)}) async-start(bf16[4,128,256]{2,1,0:T(8,128)(2,1)} %mix.1), calls=%async_computation.2 | async-start | bytes 524288 | tf_op jit(solution)/shard_map/all_to_all | solution.py:371

commit v12 on v11

--- a/solution.py
+++ b/solution.py
@@ -88,12 +88,21 @@
         (streams.at[0], streams.at[1], streams.at[2], taps_ref, rate_ref, residue_ref, skip_ref),
         sems,
     )
+    core = lax.axis_index("core")
+    height = blocks[1].shape[0]
+    side = lax.rem(here + jnp.where(core == 0, 1, parts - 1), parts)
     sent = fetch(
-        [weight_hbm.at[:, pl.ds(lax.rem(here + d, parts) * width, width)] for d in range(1, parts)],
+        (
+            weight_hbm.at[:, pl.ds(pl.multiple_of(side * width, LANES), width)],
+            weight_hbm.at[
+                pl.ds(pl.multiple_of(core * height, height), height),
+                pl.ds(pl.multiple_of(lax.rem(here + 2, parts) * width, LANES), width),
+            ],
+        ),
         blocks,
-        sems.at[pl.ds(7, parts - 1)],
-    )
-    sent += fetch([weight_hbm.at[:, pl.ds(here * width, width)]], [own_ref], sems.at[pl.ds(6 + parts, 1)])
+        sems.at[pl.ds(7, 2)],
+    )
+    sent += fetch([weight_hbm.at[:, pl.ds(here * width, width)]], [own_ref], sems.at[pl.ds(9, 1)])
     for copy in copies:
         copy.wait()
     amp_ref[...] = residue_ref[...] * jnp.sqrt(one_minus_exp(2.0 * rate_ref[...]))
@@ -214,8 +223,8 @@
         copy.wait()
 
 
-def plane_body(taps, rows, parts_ref, _block, *refs):
-    *refs, before_ref, total_ref, _same_block, out_hbm, hyena, left, carry, sems = refs
+def plane_body(taps, rows, parts_ref, *refs):
+    *refs, before_ref, total_ref, out_hbm, hyena, left, carry, sems = refs
     rate_ref = refs[5]
     me = lax.axis_index("y") * lax.axis_size("core") + lax.axis_index("core")
     drop = jnp.exp(-rows * rate_ref[...])
@@ -234,8 +243,8 @@
         mix(taps, before, refs, out_hbm, hyena, left, carry, sems)
 
 
-def mix_body(taps, plane_rows, before_ref, planes_ref, _hyena, *refs):
-    *refs, out_hbm, hyena, left, carry, sems = refs
+def mix_body(taps, plane_rows, before_ref, planes_ref, _hyena, _side, _half, *refs):
+    *refs, out_hbm, _same_side, _same_half, hyena, left, carry, sems = refs
     query_ref, rate_ref = refs[0], refs[5]
     rows = query_ref.shape[1]
     z = lax.axis_index("z")
@@ -252,23 +261,32 @@
         mix(taps, carried, refs, out_hbm, hyena, left, carry, sems)
 
 
-def order_body(left_ref, _side, _across, out_ref, _same_side, _same_across):
+def order_body(left_ref, out_ref):
     parts, _, channels = left_ref.shape
-    here = lax.axis_index("tp")
-    for d in range(parts):
-        out_ref[:, pl.ds(d * channels, channels)] = left_ref[lax.rem(here + parts - d, parts)]
+    here, core = lax.axis_index("tp"), lax.axis_index("core")
+    ahead, behind = lax.rem(here + 1, parts), lax.rem(here + parts - 1, parts)
+    across = lax.rem(here + 2, parts)
+    height = channels // 2
+    out_ref[:, :channels] = left_ref[here]
+    out_ref[:, channels : 2 * channels] = left_ref[jnp.where(core == 0, behind, ahead)]
+    out_ref[:, 2 * channels : 3 * channels] = left_ref[jnp.where(core == 0, ahead, behind)]
+    for i, half in enumerate((core, 1 - core)):
+        columns = pl.ds(pl.multiple_of(half * height, height), height)
+        out_ref[:, pl.ds(3 * channels + i * height, height)] = left_ref[across, :, columns]
 
 
 def project_body(left_ref, *rest):
     *rights, out_hbm, done, sems = rest
     blocks, _, block = done.shape
-    channels = rights[0].shape[0]
     copies = []
     for b in range(blocks):
         at = pl.ds(b * block, block)
         total = jnp.zeros(done.shape[1:], F32)
-        for d, right in enumerate(rights):
-            total += jnp.dot(left_ref[:, pl.ds(d * channels, channels)], right[:, at], preferred_element_type=F32)
+        begin = 0
+        for right in rights:
+            depth = right.shape[0]
+            total += jnp.dot(left_ref[:, pl.ds(begin, depth)], right[:, at], preferred_element_type=F32)
+            begin += depth
         done[b] = total.astype(BF16)
         copies.append(pltpu.make_async_copy(done.at[b], out_hbm.at[:, at], sems.at[b]))
         copies[-1].start()
@@ -309,7 +327,8 @@
             shape((modes, channels), F32),
             shape((modes, channels), F32),
             shape((1, channels), F32),
-            *[shape((channels, width), BF16)] * (parts - 1),
+            shape((channels, width), BF16),
+            shape((channels // 2, width), BF16),
             pltpu.VMEM((channels, width), BF16),
         ),
         "gate",
@@ -317,13 +336,16 @@
             pltpu.VMEM((3, rows, channels), BF16),
             pltpu.VMEM((modes, channels), F32),
             pltpu.VMEM((3, HEAD + rows, channels), F32),
-            pltpu.SemaphoreType.DMA((7 + parts,)),
+            pltpu.SemaphoreType.DMA((10,)),
         ],
     )(query_in, key_in, value_in, short_weight, rate, residue, skip, out_weight)
-    def to_next(block, d):
-        return lax.ppermute(block, "tp", [(i, (i + d) % parts) for i in range(parts)])
-
-    blocks = [to_next(blocks[0], 1), to_next(blocks[1], 2), blocks[2]]
+    side, half = blocks
+    side = lax.ppermute(
+        side,
+        ("core", "tp"),
+        [(c * parts + t, c * parts + (t + 1 - 2 * c) % parts) for c in range(2) for t in range(parts)],
+    )
+    half = lax.ppermute(half, "tp", [(t, (t + 2) % parts) for t in range(parts)])
     states, late, top = call(
         lambda *refs: join_body(rows, *refs),
         [VMEM] * 5,
@@ -343,50 +365,41 @@
         pltpu.VMEM((2, modes, channels), F32),
         pltpu.SemaphoreType.DMA((channels // LANES, parts)),
     ]
-    before, totals, blocks[2], hyena = call(
+    before, totals, hyena = call(
         lambda *refs: plane_body(taps, rows, *refs),
-        [VMEM, ANY] + [VMEM] * len(shared),
+        [VMEM] * (1 + len(shared)),
         (
             shape((modes, channels), F32),
             shape((planes, modes, channels), BF16),
-            shape((channels, width), BF16),
             pltpu.HBM((parts, rows, channels), BF16),
         ),
         "plane",
         scratch,
-        out_spec=(VMEM, VMEM, ANY, HBM),
-        aliases={1: 2},
-    )(states, blocks[2], *shared)
-    blocks[2] = to_next(blocks[2], 3)
+        out_spec=(VMEM, VMEM, HBM),
+        us=2,
+    )(states, *shared)
     totals = lax.all_to_all(totals, "z", 0, 0, tiled=True)
-    hyena = call(
+    hyena, side, half = call(
         lambda *refs: mix_body(taps, rows * plane, *refs),
-        [VMEM] * 2 + [HBM] + [VMEM] * len(shared),
-        pltpu.HBM((parts, rows, channels), BF16),
+        [VMEM] * 2 + [HBM] + [ANY] * 2 + [VMEM] * len(shared),
+        (pltpu.HBM((parts, rows, channels), BF16), shape(side.shape, BF16), shape(half.shape, BF16)),
         "mix",
         scratch,
-        out_spec=HBM,
-        aliases={2: 0},
-    )(before, totals, hyena, *shared)
+        out_spec=(HBM, ANY, ANY),
+        aliases={2: 0, 3: 1, 4: 2},
+    )(before, totals, hyena, side, half, *shared)
+    swapped = [lax.ppermute(x, "core", [(0, 1), (1, 0)]) for x in (side, half)]
     hyena = lax.all_to_all(hyena, "tp", 0, 0, tiled=True)
-    hyena, *blocks[:2] = call(
-        order_body,
-        [VMEM] + [ANY] * 2,
-        (shape((rows, parts * channels), BF16), *[shape((channels, width), BF16)] * 2),
-        "order",
-        out_spec=(VMEM, ANY, ANY),
-        aliases={1: 1, 2: 2},
-        us=2,
-    )(hyena, *blocks[:2])
+    hyena = call(order_body, [VMEM], shape((rows, parts * channels), BF16), "order", us=4)(hyena)
     block = 256
     return call(
         project_body,
-        [VMEM] * 5,
+        [VMEM] * 6,
         shape((rows, width), BF16),
         "project",
         [pltpu.VMEM((width // block, rows, block), BF16), pltpu.SemaphoreType.DMA((width // block,))],
         out_spec=HBM,
-    )(hyena, own, *blocks)
+    )(hyena, own, side, swapped[0], half, swapped[1])
 
 
 def solution(mesh):

time: 56.9 us -> 56.6 us (level)
  Pallas kernels: 7.35 us -> 6.3 us
  waiting for transfers between devices: 13.1 us -> 13.8 us
    all_to_all x1, waiting for transfers between devices: 6.99 us -> 0.23 us  [local(): hyena = lax.all_to_all(hyena, 'tp', 0, 0, tiled=True)]
    all_to_all x1, waiting for transfers between devices: 3.05 us -> 7.42 us  [local(): totals = lax.all_to_all(totals, 'z', 0, 0, tiled=True)]
    ppermute x3 -> x4, waiting for transfers between devices: 0.01 us -> 1.24 us  [the longest x2 1.24 us: local(): swapped = [lax.ppermute(x, 'core', [(0, 1), (1, 0)]) for x in (side, half)]]
    ppermute x1, waiting for transfers between devices: 1.44 us -> 2.56 us  [local(): rims = lax.ppermute(rims, order, [(i, i + 1) for i in range(devices - 1)])]
    pallas_call x1, Pallas kernels: 2.79 us -> 1.67 us  [local(): call(gate_body, [HBM] * 8, (shape(by_half, F32), shape(by_half, F32), sha...]
    all_to_all x1, waiting for transfers between devices: 1.66 us -> 2.35 us  [local(): states = lax.all_to_all(states, ('y', 'core'), 0, 0, tiled=True)]
    ppermute x3 -> x4, starting transfers between devices: 11.9 us -> 12.1 us  [the longest x2 5.29 us: local(): swapped = [lax.ppermute(x, 'core', [(0, 1), (1, 0)]) for x in (side, half)]]
  transfers between devices with their start and end apart: 7 -> 8, of which waited for: 4 -> 5; matrix products, arithmetic and copies ran while one was open for 0% -> 0% of each run, Pallas kernels for 8% -> 6%
where the time goes in v12:
time: 56.6 us; the launch traced here: 56 us
  starting transfers between devices  35.8 us (63%)
  waiting for transfers between devices  13.8 us (24%)
  Pallas kernels  6.3 us (11%)
    all_to_all x1, starting transfers between devices, local(): totals = lax.all_to_all(totals, 'z', 0, 0, tiled=True)  8.98 us
    all_to_all x1, waiting for transfers between devices, local(): totals = lax.all_to_all(totals, 'z', 0, 0, tiled=True)  7.42 us
    all_to_all x1, starting transfers between devices, local(): states = lax.all_to_all(states, ('y', 'core'), 0, 0, tiled=True)  6.13 us
    ppermute x2, starting transfers between devices, local(): swapped = [lax.ppermute(x, 'core', [(0, 1), (1, 0)]) for x in (side, half)]  5.29 us
    ppermute x1, starting transfers between devices, local(): rims = lax.ppermute(rims, order, [(i, i + 1) for i in range(devices - 1)])  4.59 us
    ppermute x1, starting transfers between devices, local(): lax.ppermute(side, ('core', 'tp'), [(c * parts + t, c * parts + (t + 1 -...  4.37 us
    all_to_all x1, starting transfers between devices, local(): hyena = lax.all_to_all(hyena, 'tp', 0, 0, tiled=True)  4.03 us
    ppermute x1, waiting for transfers between devices, local(): rims = lax.ppermute(rims, order, [(i, i + 1) for i in range(devices - 1)])  2.56 us
  transfers between devices with their start and end apart: 8, of which 5 were waited for; matrix products, arithmetic and copies ran while one was open for 0% of the time, Pallas kernels for 6%

profile of v12, /device:TPU:1, one launch (start us, length us, event | category | flops | bytes accessed | tf_op | source)
XLA Modules:
  0.0 56.0 jit_solution(2390340231317726177)
XLA Ops:
  0.0 0.8 %rims.1 = bf16[48,256]{1,0:T(8,128)(2,1)S(1)} custom-call(bf16[128,256]{1,0:T(8,128)(2,1)} %q_hbm.1, bf16[128,256]{1,0:T(8,128)(2,1)} %k_hbm.1, bf16[128,256]{1,0:T(8,128)(2,1)} %v_hbm.1), custom_call_target="tpu_custom_call" | custom-call | tf_op jit(solution)/shard_map/rims/pallas_call | solution.py:313
  0.8 4.6 %collective-permute-start = (bf16[48,256]{1,0:T(8,128)(2,1)S(1)}, bf16[48,256]{1,0:T(8,128)(2,1)S(1)}, u32[]{:S(2)}, u32[]{:S(2)}) collective-permute-start(bf16[48,256]{1,0:T(8,128)(2,1)S(1)} %rims.1), channel_id=1, source_target_pairs={{0,4},{4,8},{8,12},{12,16},{16,20},{20,24},{24,28},{28,32},{32,36}... | collective-permute-start | bytes 73736 | tf_op jit(solution)/shard_map/ppermute | solution.py:316
  5.4 1.7 %gate.1 = (f32[2,128,128]{2,1,0:T(8,128)S(1)}, f32[2,128,128]{2,1,0:T(8,128)S(1)}, f32[16,8,256]{2,1,0:T(8,128)S(1)}, f32[16,256]{1,0:T(8,128)S(1)}, f32[3,8,256...) custom-call(bf16[128,256]{1,0:T(8,128)(2,1)} %q_hbm.1, ...), custom_call_target="tpu_custom_call" | custom-call | tf_op jit(solution)/shard_map/gate/pallas_call | solution.py:317
  7.0 2.6 %collective-permute-done.refs_0_ = bf16[48,256]{1,0:T(8,128)(2,1)S(1)} collective-permute-done((bf16[48,256]{1,0:T(8,128)(2,1)S(1)}, bf16[48,256]{1,0:T(8,128)(2,1)S(1)}, u32[]{:S(2)}, u32[]{:S(2)}) %collective-permute-start) | collective-permute-done | bytes 24608 | tf_op jit(solution)/shard_map/ppermute | solution.py:316
  9.6 0.7 %join.1 = (bf16[16,16,256]{2,1,0:T(8,128)(2,1)}, f32[16,256]{1,0:T(8,128)S(1)}, f32[2,8,256]{2,1,0:T(8,128)S(1)}) custom-call(bf16[48,256]{1,0:T(8,128)(2,1)S(1)} %collective-permute-done.refs_0_, f32[3,8,256]{2,1,0:T(8,128)S(1)} %get-tuple-element.26.refs_1_, f32[3,7,256]{2,1,0:T(8,128)S(1)} %get-tuple-element.27.refs_2_, ...), custom_call_target="tpu_custom_call" | custom-call | tf_op jit(solution)/shard_map/join/pallas_call | solution.py:349
  10.3 6.1 %all-to-all-start = ((bf16[16,16,256]{2,1,0:T(8,128)(2,1)}), bf16[16,16,256]{2,1,0:T(8,128)(2,1)S(1)}, u32[]{:S(2)}, u32[]{:S(2)}) async-start(bf16[16,16,256]{2,1,0:T(8,128)(2,1)} %get-tuple-element.30), calls=%async_computation | async-start | bytes 262144 | tf_op jit(solution)/shard_map/all_to_all | solution.py:360
  16.5 4.4 %collective-permute-start.1 = (bf16[256,1024]{1,0:T(8,128)(2,1)S(1)}, bf16[256,1024]{1,0:T(8,128)(2,1)S(1)}, u32[]{:S(2)}, u32[]{:S(2)}) collective-permute-start(bf16[256,1024]{1,0:T(8,128)(2,1)S(1)} %get-tuple-element.41), channel_id=1, source_target_pairs={{0,1},{1,2},{2,3},{3,0},{4,7},{5,4},{6,5},{7,6},{8,9},{9,10},{10,1... | collective-permute-start | bytes 1572872 | tf_op jit(solution)/shard_map/ppermute | solution.py:343
  20.8 2.4 %collective-permute-start.2 = (bf16[128,1024]{1,0:T(8,128)(2,1)S(1)}, bf16[128,1024]{1,0:T(8,128)(2,1)S(1)}, u32[]{:S(2)}, u32[]{:S(2)}) collective-permute-start(bf16[128,1024]{1,0:T(8,128)(2,1)S(1)} %get-tuple-element.42), channel_id=1, source_target_pairs={{0,2},{1,3},{2,0},{3,1},{4,6},{5,7},{6,4},{7,5},{8,10},{9,11},{10,... | collective-permute-start | bytes 786440 | tf_op jit(solution)/shard_map/ppermute | solution.py:348
  23.3 2.3 %all-to-all-done.refs_0_ = bf16[16,16,256]{2,1,0:T(8,128)(2,1)S(1)} async-done(((bf16[16,16,256]{2,1,0:T(8,128)(2,1)}), bf16[16,16,256]{2,1,0:T(8,128)(2,1)S(1)}, u32[]{:S(2)}, u32[]{:S(2)}) %all-to-all-start) | async-done | bytes 131104 | tf_op jit(solution)/shard_map/all_to_all | solution.py:360
  25.6 1.8 %plane.1 = (f32[16,256]{1,0:T(8,128)S(1)}, bf16[8,16,256]{2,1,0:T(8,128)(2,1)}, bf16[4,128,256]{2,1,0:T(8,128)(2,1)}) custom-call(bf16[16,16,256]{2,1,0:T(8,128)(2,1)S(1)} %all-to-all-done.refs_0_, f32[2,128,128]{2,1,0:T(8,128)S(1)} %get-tuple-element.31.refs_1_.refs_5_, f32[2,128,128]{2,1,0:T(8,128)S(1)} %get-tuple-element.32.refs_2_.refs_6_, ...), custom_call_target="tpu_custom_call" | custom-call | flops 2300000000 | tf_op jit(solution)/shard_map/plane/pallas_call | solution.py:368
  27.5 9.0 %all-to-all-start.1 = ((bf16[8,16,256]{2,1,0:T(8,128)(2,1)}), bf16[8,16,256]{2,1,0:T(8,128)(2,1)S(1)}, u32[]{:S(2)}, u32[]{:S(2)}) async-start(bf16[8,16,256]{2,1,0:T(8,128)(2,1)} %get-tuple-element.39), calls=%async_computation.1 | async-start | bytes 131072 | tf_op jit(solution)/shard_map/all_to_all | solution.py:381
  36.5 0.0 collective-permute-done.2.refs_4_
  36.5 7.4 %all-to-all-done.1.refs_1_ = bf16[8,16,256]{2,1,0:T(8,128)(2,1)S(1)} async-done(((bf16[8,16,256]{2,1,0:T(8,128)(2,1)}), bf16[8,16,256]{2,1,0:T(8,128)(2,1)S(1)}, u32[]{:S(2)}, u32[]{:S(2)}) %all-to-all-start.1) | async-done | bytes 65568 | tf_op jit(solution)/shard_map/all_to_all | solution.py:381
  43.9 0.0 collective-permute-done.1.refs_3_
  43.9 0.1 mix.1
  44.0 4.0 %all-to-all-start.2 = ((bf16[4,128,256]{2,1,0:T(8,128)(2,1)}), bf16[4,128,256]{2,1,0:T(8,128)(2,1)S(1)}, u32[]{:S(2)}, u32[]{:S(2)}) async-start(bf16[4,128,256]{2,1,0:T(8,128)(2,1)} %get-tuple-element.43), calls=%async_computation.2 | async-start | bytes 524288 | tf_op jit(solution)/shard_map/all_to_all | solution.py:392
  48.0 3.4 %collective-permute-start.3 = (bf16[256,1024]{1,0:T(8,128)(2,1)S(1)}, bf16[256,1024]{1,0:T(8,128)(2,1)S(1)}, u32[]{:S(2)}, u32[]{:S(2)}) collective-permute-start(bf16[256,1024]{1,0:T(8,128)(2,1)S(1)} %get-tuple-element.45.rest_1_), channel_id=1, source_target_pairs={{0,4},{4,0},{1,5},{5,1},{2,6},{6,2},{3,7},{7,3},{8,12},{12,8},{9,1... | collective-permute-start | bytes 1572872 | tf_op jit(solution)/shard_map/ppermute | solution.py:391
  51.4 1.9 %collective-permute-start.4 = (bf16[128,1024]{1,0:T(8,128)(2,1)S(1)}, bf16[128,1024]{1,0:T(8,128)(2,1)S(1)}, u32[]{:S(2)}, u32[]{:S(2)}) collective-permute-start(bf16[128,1024]{1,0:T(8,128)(2,1)S(1)} %get-tuple-element.46.rest_3_), channel_id=1, source_target_pairs={{0,4},{4,0},{1,5},{5,1},{2,6},{6,2},{3,7},{7,3},{8,12},{12,8},{9,1... | collective-permute-start | bytes 786440 | tf_op jit(solution)/shard_map/ppermute | solution.py:391
  53.3 0.2 all-to-all-done.2.left_ref
  53.6 1.2 %collective-permute-done.4.rest_4_ = bf16[128,1024]{1,0:T(8,128)(2,1)S(1)} collective-permute-done((bf16[128,1024]{1,0:T(8,128)(2,1)S(1)}, bf16[128,1024]{1,0:T(8,128)(2,1)S(1)}, u32[]{:S(2)}, u32[]{:S(2)}) %collective-permute-start.4) | collective-permute-done | bytes 262176 | tf_op jit(solution)/shard_map/ppermute | solution.py:391
  54.8 0.0 collective-permute-done.3.rest_2_
  54.8 1.2 %project.1 = bf16[128,1024]{1,0:T(8,128)(2,1)} custom-call(bf16[128,1024]{1,0:T(8,128)(2,1)S(1)} %order.1.left_ref, bf16[256,1024]{1,0:T(8,128)(2,1)S(1)} %get-tuple-element.44.rest_0_, bf16[256,1024]{1,0:T(8,128)(2,1)S(1)} %get-tuple-element.45.rest_1_, bf16[256,1024]{1,0:T(8,128)(2,1)S(1)} %collective-permute-done.3.rest_2_, ...), custom_call_target="tpu_custom_call" | custom-call | tf_op jit(solution)/shard_map/project/pallas_call | solution.py:395
  (1 shorter events, 0.0 us)
Async XLA Ops:
  0.8 8.8 %collective-permute-start = (bf16[48,256]{1,0:T(8,128)(2,1)S(1)}, bf16[48,256]{1,0:T(8,128)(2,1)S(1)}, u32[]{:S(2)}, u32[]{:S(2)}) collective-permute-start(bf16[48,256]{1,0:T(8,128)(2,1)S(1)} %rims.1), channel_id=1, source_target_pairs={{0,4},{4,8},{8,12},{12,16},{16,20},{20,24},{24,28},{28,32},{32,36}... | collective-permute-start | bytes 73736 | tf_op jit(solution)/shard_map/ppermute | solution.py:316
  10.3 15.3 %all-to-all-start = ((bf16[16,16,256]{2,1,0:T(8,128)(2,1)}), bf16[16,16,256]{2,1,0:T(8,128)(2,1)S(1)}, u32[]{:S(2)}, u32[]{:S(2)}) async-start(bf16[16,16,256]{2,1,0:T(8,128)(2,1)} %get-tuple-element.30), calls=%async_computation | async-start | bytes 262144 | tf_op jit(solution)/shard_map/all_to_all | solution.py:360
  16.5 27.4 %collective-permute-start.1 = (bf16[256,1024]{1,0:T(8,128)(2,1)S(1)}, bf16[256,1024]{1,0:T(8,128)(2,1)S(1)}, u32[]{:S(2)}, u32[]{:S(2)}) collective-permute-start(bf16[256,1024]{1,0:T(8,128)(2,1)S(1)} %get-tuple-element.41), channel_id=1, source_target_pairs={{0,1},{1,2},{2,3},{3,0},{4,7},{5,4},{6,5},{7,6},{8,9},{9,10},{10,1... | collective-permute-start | bytes 1572872 | tf_op jit(solution)/shard_map/ppermute | solution.py:343
  20.8 15.6 %collective-permute-start.2 = (bf16[128,1024]{1,0:T(8,128)(2,1)S(1)}, bf16[128,1024]{1,0:T(8,128)(2,1)S(1)}, u32[]{:S(2)}, u32[]{:S(2)}) collective-permute-start(bf16[128,1024]{1,0:T(8,128)(2,1)S(1)} %get-tuple-element.42), channel_id=1, source_target_pairs={{0,2},{1,3},{2,0},{3,1},{4,6},{5,7},{6,4},{7,5},{8,10},{9,11},{10,... | collective-permute-start | bytes 786440 | tf_op jit(solution)/shard_map/ppermute | solution.py:348
  27.5 16.4 %all-to-all-start.1 = ((bf16[8,16,256]{2,1,0:T(8,128)(2,1)}), bf16[8,16,256]{2,1,0:T(8,128)(2,1)S(1)}, u32[]{:S(2)}, u32[]{:S(2)}) async-start(bf16[8,16,256]{2,1,0:T(8,128)(2,1)} %get-tuple-element.39), calls=%async_computation.1 | async-start | bytes 131072 | tf_op jit(solution)/shard_map/all_to_all | solution.py:381
  44.0 9.6 %all-to-all-start.2 = ((bf16[4,128,256]{2,1,0:T(8,128)(2,1)}), bf16[4,128,256]{2,1,0:T(8,128)(2,1)S(1)}, u32[]{:S(2)}, u32[]{:S(2)}) async-start(bf16[4,128,256]{2,1,0:T(8,128)(2,1)} %get-tuple-element.43), calls=%async_computation.2 | async-start | bytes 524288 | tf_op jit(solution)/shard_map/all_to_all | solution.py:392
  48.0 6.8 %collective-permute-start.3 = (bf16[256,1024]{1,0:T(8,128)(2,1)S(1)}, bf16[256,1024]{1,0:T(8,128)(2,1)S(1)}, u32[]{:S(2)}, u32[]{:S(2)}) collective-permute-start(bf16[256,1024]{1,0:T(8,128)(2,1)S(1)} %get-tuple-element.45.rest_1_), channel_id=1, source_target_pairs={{0,4},{4,0},{1,5},{5,1},{2,6},{6,2},{3,7},{7,3},{8,12},{12,8},{9,1... | collective-permute-start | bytes 1572872 | tf_op jit(solution)/shard_map/ppermute | solution.py:391
  51.4 3.4 %collective-permute-start.4 = (bf16[128,1024]{1,0:T(8,128)(2,1)S(1)}, bf16[128,1024]{1,0:T(8,128)(2,1)S(1)}, u32[]{:S(2)}, u32[]{:S(2)}) collective-permute-start(bf16[128,1024]{1,0:T(8,128)(2,1)S(1)} %get-tuple-element.46.rest_3_), channel_id=1, source_target_pairs={{0,4},{4,0},{1,5},{5,1},{2,6},{6,2},{3,7},{7,3},{8,12},{12,8},{9,1... | collective-permute-start | bytes 786440 | tf_op jit(solution)/shard_map/ppermute | solution.py:391

commit v13 on v12

--- a/solution.py
+++ b/solution.py
@@ -243,8 +243,8 @@
         mix(taps, before, refs, out_hbm, hyena, left, carry, sems)
 
 
-def mix_body(taps, plane_rows, before_ref, planes_ref, _hyena, _side, _half, *refs):
-    *refs, out_hbm, _same_side, _same_half, hyena, left, carry, sems = refs
+def mix_body(taps, plane_rows, before_ref, planes_ref, _hyena, _half, *refs):
+    *refs, out_hbm, _same_half, hyena, left, carry, sems = refs
     query_ref, rate_ref = refs[0], refs[5]
     rows = query_ref.shape[1]
     z = lax.axis_index("z")
@@ -379,18 +379,19 @@
         us=2,
     )(states, *shared)
     totals = lax.all_to_all(totals, "z", 0, 0, tiled=True)
-    hyena, side, half = call(
+    swapped = [lax.ppermute(side, "core", [(0, 1), (1, 0)])]
+    hyena, half = call(
         lambda *refs: mix_body(taps, rows * plane, *refs),
-        [VMEM] * 2 + [HBM] + [ANY] * 2 + [VMEM] * len(shared),
-        (pltpu.HBM((parts, rows, channels), BF16), shape(side.shape, BF16), shape(half.shape, BF16)),
+        [VMEM] * 2 + [HBM, ANY] + [VMEM] * len(shared),
+        (pltpu.HBM((parts, rows, channels), BF16), shape(half.shape, BF16)),
         "mix",
         scratch,
-        out_spec=(HBM, ANY, ANY),
-        aliases={2: 0, 3: 1, 4: 2},
-    )(before, totals, hyena, side, half, *shared)
-    swapped = [lax.ppermute(x, "core", [(0, 1), (1, 0)]) for x in (side, half)]
+        out_spec=(HBM, ANY),
+        aliases={2: 0, 3: 1},
+    )(before, totals, hyena, half, *shared)
+    swapped.append(lax.ppermute(half, "core", [(0, 1), (1, 0)]))
     hyena = lax.all_to_all(hyena, "tp", 0, 0, tiled=True)
-    hyena = call(order_body, [VMEM], shape((rows, parts * channels), BF16), "order", us=4)(hyena)
+    hyena = call(order_body, [VMEM], shape((rows, parts * channels), BF16), "order", us=3)(hyena)
     block = 256
     return call(
         project_body,

time: 56.6 us -> 55.8 us (0.986)
  waiting for transfers between devices: 13.8 us -> 12.5 us
    all_to_all x1, waiting for transfers between devices: 7.42 us -> 5.49 us  [local(): totals = lax.all_to_all(totals, 'z', 0, 0, tiled=True)]
    all_to_all x1, waiting for transfers between devices: 0.23 us -> 2.16 us  [local(): hyena = lax.all_to_all(hyena, 'tp', 0, 0, tiled=True)]
    ppermute x2, waiting for transfers between devices: 1.24 us -> 0.01 us  [the longest x1 0.01 us: local(): swapped = [lax.ppermute(side, 'core', [(0, 1), (1, 0)])]]
  transfers between devices with their start and end apart: 8 -> 8, of which waited for: 5 -> 4; matrix products, arithmetic and copies ran while one was open for 0% -> 0% of each run, Pallas kernels for 6% -> 7%
where the time goes in v13:
time: 55.8 us; the launch traced here: 54.8 us
  starting transfers between devices  35.8 us (64%)
  waiting for transfers between devices  12.5 us (22%)
  Pallas kernels  6.32 us (11%)
    all_to_all x1, starting transfers between devices, local(): totals = lax.all_to_all(totals, 'z', 0, 0, tiled=True)  8.98 us
    all_to_all x1, starting transfers between devices, local(): states = lax.all_to_all(states, ('y', 'core'), 0, 0, tiled=True)  6.13 us
    all_to_all x1, waiting for transfers between devices, local(): totals = lax.all_to_all(totals, 'z', 0, 0, tiled=True)  5.49 us
    ppermute x1, starting transfers between devices, local(): rims = lax.ppermute(rims, order, [(i, i + 1) for i in range(devices - 1)])  4.59 us
    ppermute x1, starting transfers between devices, local(): lax.ppermute(side, ('core', 'tp'), [(c * parts + t, c * parts + (t + 1 -...  4.37 us
    all_to_all x1, starting transfers between devices, local(): hyena = lax.all_to_all(hyena, 'tp', 0, 0, tiled=True)  4.03 us
    ppermute x1, starting transfers between devices, local(): swapped.append(lax.ppermute(half, 'core', [(0, 1), (1, 0)]))  3.37 us
    ppermute x1, waiting for transfers between devices, local(): rims = lax.ppermute(rims, order, [(i, i + 1) for i in range(devices - 1)])  2.55 us
  transfers between devices with their start and end apart: 8, of which 4 were waited for; matrix products, arithmetic and copies ran while one was open for 0% of the time, Pallas kernels for 7%

profile of v13, /device:TPU:1, one launch (start us, length us, event | category | flops | bytes accessed | tf_op | source)
XLA Modules:
  0.0 54.8 jit_solution(6406758764642568030)
XLA Ops:
  0.0 0.8 %rims.1 = bf16[48,256]{1,0:T(8,128)(2,1)S(1)} custom-call(bf16[128,256]{1,0:T(8,128)(2,1)} %q_hbm.1, bf16[128,256]{1,0:T(8,128)(2,1)} %k_hbm.1, bf16[128,256]{1,0:T(8,128)(2,1)} %v_hbm.1), custom_call_target="tpu_custom_call" | custom-call | tf_op jit(solution)/shard_map/rims/pallas_call | solution.py:313
  0.8 4.6 %collective-permute-start = (bf16[48,256]{1,0:T(8,128)(2,1)S(1)}, bf16[48,256]{1,0:T(8,128)(2,1)S(1)}, u32[]{:S(2)}, u32[]{:S(2)}) collective-permute-start(bf16[48,256]{1,0:T(8,128)(2,1)S(1)} %rims.1), channel_id=1, source_target_pairs={{0,4},{4,8},{8,12},{12,16},{16,20},{20,24},{24,28},{28,32},{32,36}... | collective-permute-start | bytes 73736 | tf_op jit(solution)/shard_map/ppermute | solution.py:316
  5.4 1.7 %gate.1 = (f32[2,128,128]{2,1,0:T(8,128)S(1)}, f32[2,128,128]{2,1,0:T(8,128)S(1)}, f32[16,8,256]{2,1,0:T(8,128)S(1)}, f32[16,256]{1,0:T(8,128)S(1)}, f32[3,8,256...) custom-call(bf16[128,256]{1,0:T(8,128)(2,1)} %q_hbm.1, ...), custom_call_target="tpu_custom_call" | custom-call | tf_op jit(solution)/shard_map/gate/pallas_call | solution.py:317
  7.1 2.5 %collective-permute-done.refs_0_ = bf16[48,256]{1,0:T(8,128)(2,1)S(1)} collective-permute-done((bf16[48,256]{1,0:T(8,128)(2,1)S(1)}, bf16[48,256]{1,0:T(8,128)(2,1)S(1)}, u32[]{:S(2)}, u32[]{:S(2)}) %collective-permute-start) | collective-permute-done | bytes 24608 | tf_op jit(solution)/shard_map/ppermute | solution.py:316
  9.6 0.7 %join.1 = (bf16[16,16,256]{2,1,0:T(8,128)(2,1)}, f32[16,256]{1,0:T(8,128)S(1)}, f32[2,8,256]{2,1,0:T(8,128)S(1)}) custom-call(bf16[48,256]{1,0:T(8,128)(2,1)S(1)} %collective-permute-done.refs_0_, f32[3,8,256]{2,1,0:T(8,128)S(1)} %get-tuple-element.25.refs_1_, f32[3,7,256]{2,1,0:T(8,128)S(1)} %get-tuple-element.26.refs_2_, ...), custom_call_target="tpu_custom_call" | custom-call | tf_op jit(solution)/shard_map/join/pallas_call | solution.py:349
  10.3 6.1 %all-to-all-start = ((bf16[16,16,256]{2,1,0:T(8,128)(2,1)}), bf16[16,16,256]{2,1,0:T(8,128)(2,1)S(1)}, u32[]{:S(2)}, u32[]{:S(2)}) async-start(bf16[16,16,256]{2,1,0:T(8,128)(2,1)} %get-tuple-element.29), calls=%async_computation | async-start | bytes 262144 | tf_op jit(solution)/shard_map/all_to_all | solution.py:360
  16.5 4.4 %collective-permute-start.2 = (bf16[256,1024]{1,0:T(8,128)(2,1)S(1)}, bf16[256,1024]{1,0:T(8,128)(2,1)S(1)}, u32[]{:S(2)}, u32[]{:S(2)}) collective-permute-start(bf16[256,1024]{1,0:T(8,128)(2,1)S(1)} %get-tuple-element.43), channel_id=1, source_target_pairs={{0,1},{1,2},{2,3},{3,0},{4,7},{5,4},{6,5},{7,6},{8,9},{9,10},{10,1... | collective-permute-start | bytes 1572872 | tf_op jit(solution)/shard_map/ppermute | solution.py:343
  20.8 2.4 %collective-permute-start.1 = (bf16[128,1024]{1,0:T(8,128)(2,1)S(1)}, bf16[128,1024]{1,0:T(8,128)(2,1)S(1)}, u32[]{:S(2)}, u32[]{:S(2)}) collective-permute-start(bf16[128,1024]{1,0:T(8,128)(2,1)S(1)} %get-tuple-element.40), channel_id=1, source_target_pairs={{0,2},{1,3},{2,0},{3,1},{4,6},{5,7},{6,4},{7,5},{8,10},{9,11},{10,... | collective-permute-start | bytes 786440 | tf_op jit(solution)/shard_map/ppermute | solution.py:348
  23.3 2.3 %all-to-all-done.refs_0_ = bf16[16,16,256]{2,1,0:T(8,128)(2,1)S(1)} async-done(((bf16[16,16,256]{2,1,0:T(8,128)(2,1)}), bf16[16,16,256]{2,1,0:T(8,128)(2,1)S(1)}, u32[]{:S(2)}, u32[]{:S(2)}) %all-to-all-start) | async-done | bytes 131104 | tf_op jit(solution)/shard_map/all_to_all | solution.py:360
  25.6 1.8 %plane.1 = (f32[16,256]{1,0:T(8,128)S(1)}, bf16[8,16,256]{2,1,0:T(8,128)(2,1)}, bf16[4,128,256]{2,1,0:T(8,128)(2,1)}) custom-call(bf16[16,16,256]{2,1,0:T(8,128)(2,1)S(1)} %all-to-all-done.refs_0_, f32[2,128,128]{2,1,0:T(8,128)S(1)} %get-tuple-element.30.refs_1_.refs_4_, f32[2,128,128]{2,1,0:T(8,128)S(1)} %get-tuple-element.31.refs_2_.refs_5_, ...), custom_call_target="tpu_custom_call" | custom-call | flops 2300000000 | tf_op jit(solution)/shard_map/plane/pallas_call | solution.py:368
  27.5 9.0 %all-to-all-start.1 = ((bf16[8,16,256]{2,1,0:T(8,128)(2,1)}), bf16[8,16,256]{2,1,0:T(8,128)(2,1)S(1)}, u32[]{:S(2)}, u32[]{:S(2)}) async-start(bf16[8,16,256]{2,1,0:T(8,128)(2,1)} %get-tuple-element.38), calls=%async_computation.1 | async-start | bytes 131072 | tf_op jit(solution)/shard_map/all_to_all | solution.py:381
  36.5 0.0 collective-permute-done.2.rest_1_
  36.5 1.9 %collective-permute-start.3 = (bf16[256,1024]{1,0:T(8,128)(2,1)S(1)}, bf16[256,1024]{1,0:T(8,128)(2,1)S(1)}, u32[]{:S(2)}, u32[]{:S(2)}) collective-permute-start(bf16[256,1024]{1,0:T(8,128)(2,1)S(1)} %collective-permute-done.2.rest_1_), channel_id=1, source_target_pairs={{0,4},{4,0},{1,5},{5,1},{2,6},{6,2},{3,7},{7,3},{8,12},{12,8},{9,1... | collective-permute-start | bytes 1572872 | tf_op jit(solution)/shard_map/ppermute | solution.py:382
  38.4 0.0 collective-permute-done.1.refs_3_
  38.4 5.5 %all-to-all-done.1.refs_1_ = bf16[8,16,256]{2,1,0:T(8,128)(2,1)S(1)} async-done(((bf16[8,16,256]{2,1,0:T(8,128)(2,1)}), bf16[8,16,256]{2,1,0:T(8,128)(2,1)S(1)}, u32[]{:S(2)}, u32[]{:S(2)}) %all-to-all-start.1) | async-done | bytes 65568 | tf_op jit(solution)/shard_map/all_to_all | solution.py:381
  43.9 0.1 mix.1
  44.0 4.0 %all-to-all-start.2 = ((bf16[4,128,256]{2,1,0:T(8,128)(2,1)}), bf16[4,128,256]{2,1,0:T(8,128)(2,1)S(1)}, u32[]{:S(2)}, u32[]{:S(2)}) async-start(bf16[4,128,256]{2,1,0:T(8,128)(2,1)} %get-tuple-element.41), calls=%async_computation.2 | async-start | bytes 524288 | tf_op jit(solution)/shard_map/all_to_all | solution.py:393
  48.0 3.4 %collective-permute-start.4 = (bf16[128,1024]{1,0:T(8,128)(2,1)S(1)}, bf16[128,1024]{1,0:T(8,128)(2,1)S(1)}, u32[]{:S(2)}, u32[]{:S(2)}) collective-permute-start(bf16[128,1024]{1,0:T(8,128)(2,1)S(1)} %get-tuple-element.44.rest_3_), channel_id=1, source_target_pairs={{0,4},{4,0},{1,5},{5,1},{2,6},{6,2},{3,7},{7,3},{8,12},{12,8},{9,1... | collective-permute-start | bytes 786440 | tf_op jit(solution)/shard_map/ppermute | solution.py:392
  51.4 2.2 %all-to-all-done.2.left_ref = bf16[4,128,256]{2,1,0:T(8,128)(2,1)S(1)} async-done(((bf16[4,128,256]{2,1,0:T(8,128)(2,1)}), bf16[4,128,256]{2,1,0:T(8,128)(2,1)S(1)}, u32[]{:S(2)}, u32[]{:S(2)}) %all-to-all-start.2) | async-done | bytes 262176 | tf_op jit(solution)/shard_map/all_to_all | solution.py:393
  53.6 0.0 collective-permute-done.4.rest_4_
  53.6 0.0 collective-permute-done.3.rest_2_
  53.6 1.2 %project.1 = bf16[128,1024]{1,0:T(8,128)(2,1)} custom-call(bf16[128,1024]{1,0:T(8,128)(2,1)S(1)} %order.1.left_ref, bf16[256,1024]{1,0:T(8,128)(2,1)S(1)} %get-tuple-element.42.rest_0_, bf16[256,1024]{1,0:T(8,128)(2,1)S(1)} %collective-permute-done.2.rest_1_, bf16[256,1024]{1,0:T(8,128)(2,1)S(1)} %collective-permute-done.3.rest_2_, ...), custom_call_target="tpu_custom_call" | custom-call | tf_op jit(solution)/shard_map/project/pallas_call | solution.py:396
  (1 shorter events, 0.0 us)
Async XLA Ops:
  0.8 8.8 %collective-permute-start = (bf16[48,256]{1,0:T(8,128)(2,1)S(1)}, bf16[48,256]{1,0:T(8,128)(2,1)S(1)}, u32[]{:S(2)}, u32[]{:S(2)}) collective-permute-start(bf16[48,256]{1,0:T(8,128)(2,1)S(1)} %rims.1), channel_id=1, source_target_pairs={{0,4},{4,8},{8,12},{12,16},{16,20},{20,24},{24,28},{28,32},{32,36}... | collective-permute-start | bytes 73736 | tf_op jit(solution)/shard_map/ppermute | solution.py:316
  10.3 15.3 %all-to-all-start = ((bf16[16,16,256]{2,1,0:T(8,128)(2,1)}), bf16[16,16,256]{2,1,0:T(8,128)(2,1)S(1)}, u32[]{:S(2)}, u32[]{:S(2)}) async-start(bf16[16,16,256]{2,1,0:T(8,128)(2,1)} %get-tuple-element.29), calls=%async_computation | async-start | bytes 262144 | tf_op jit(solution)/shard_map/all_to_all | solution.py:360
  16.5 20.0 %collective-permute-start.2 = (bf16[256,1024]{1,0:T(8,128)(2,1)S(1)}, bf16[256,1024]{1,0:T(8,128)(2,1)S(1)}, u32[]{:S(2)}, u32[]{:S(2)}) collective-permute-start(bf16[256,1024]{1,0:T(8,128)(2,1)S(1)} %get-tuple-element.43), channel_id=1, source_target_pairs={{0,1},{1,2},{2,3},{3,0},{4,7},{5,4},{6,5},{7,6},{8,9},{9,10},{10,1... | collective-permute-start | bytes 1572872 | tf_op jit(solution)/shard_map/ppermute | solution.py:343
  20.8 17.5 %collective-permute-start.1 = (bf16[128,1024]{1,0:T(8,128)(2,1)S(1)}, bf16[128,1024]{1,0:T(8,128)(2,1)S(1)}, u32[]{:S(2)}, u32[]{:S(2)}) collective-permute-start(bf16[128,1024]{1,0:T(8,128)(2,1)S(1)} %get-tuple-element.40), channel_id=1, source_target_pairs={{0,2},{1,3},{2,0},{3,1},{4,6},{5,7},{6,4},{7,5},{8,10},{9,11},{10,... | collective-permute-start | bytes 786440 | tf_op jit(solution)/shard_map/ppermute | solution.py:348
  27.5 16.4 %all-to-all-start.1 = ((bf16[8,16,256]{2,1,0:T(8,128)(2,1)}), bf16[8,16,256]{2,1,0:T(8,128)(2,1)S(1)}, u32[]{:S(2)}, u32[]{:S(2)}) async-start(bf16[8,16,256]{2,1,0:T(8,128)(2,1)} %get-tuple-element.38), calls=%async_computation.1 | async-start | bytes 131072 | tf_op jit(solution)/shard_map/all_to_all | solution.py:381
  36.5 17.1 %collective-permute-start.3 = (bf16[256,1024]{1,0:T(8,128)(2,1)S(1)}, bf16[256,1024]{1,0:T(8,128)(2,1)S(1)}, u32[]{:S(2)}, u32[]{:S(2)}) collective-permute-start(bf16[256,1024]{1,0:T(8,128)(2,1)S(1)} %collective-permute-done.2.rest_1_), channel_id=1, source_target_pairs={{0,4},{4,0},{1,5},{5,1},{2,6},{6,2},{3,7},{7,3},{8,12},{12,8},{9,1... | collective-permute-start | bytes 1572872 | tf_op jit(solution)/shard_map/ppermute | solution.py:382
  44.0 9.6 %all-to-all-start.2 = ((bf16[4,128,256]{2,1,0:T(8,128)(2,1)}), bf16[4,128,256]{2,1,0:T(8,128)(2,1)S(1)}, u32[]{:S(2)}, u32[]{:S(2)}) async-start(bf16[4,128,256]{2,1,0:T(8,128)(2,1)} %get-tuple-element.41), calls=%async_computation.2 | async-start | bytes 524288 | tf_op jit(solution)/shard_map/all_to_all | solution.py:393
  48.0 5.6 %collective-permute-start.4 = (bf16[128,1024]{1,0:T(8,128)(2,1)S(1)}, bf16[128,1024]{1,0:T(8,128)(2,1)S(1)}, u32[]{:S(2)}, u32[]{:S(2)}) collective-permute-start(bf16[128,1024]{1,0:T(8,128)(2,1)S(1)} %get-tuple-element.44.rest_3_), channel_id=1, source_target_pairs={{0,4},{4,0},{1,5},{5,1},{2,6},{6,2},{3,7},{7,3},{8,12},{12,8},{9,1... | collective-permute-start | bytes 786440 | tf_op jit(solution)/shard_map/ppermute | solution.py:392

commit v14 on v12

--- a/solution.py
+++ b/solution.py
@@ -243,8 +243,8 @@
         mix(taps, before, refs, out_hbm, hyena, left, carry, sems)
 
 
-def mix_body(taps, plane_rows, before_ref, planes_ref, _hyena, _side, _half, *refs):
-    *refs, out_hbm, _same_side, _same_half, hyena, left, carry, sems = refs
+def mix_body(taps, plane_rows, before_ref, planes_ref, _hyena, *refs):
+    *refs, out_hbm, hyena, left, carry, sems = refs
     query_ref, rate_ref = refs[0], refs[5]
     rows = query_ref.shape[1]
     z = lax.axis_index("z")
@@ -371,26 +371,27 @@
         (
             shape((modes, channels), F32),
             shape((planes, modes, channels), BF16),
-            pltpu.HBM((parts, rows, channels), BF16),
+            shape((parts, rows, channels), BF16),
         ),
         "plane",
         scratch,
-        out_spec=(VMEM, VMEM, HBM),
-        us=2,
+        out_spec=(VMEM, VMEM, ANY),
+        us=4,
     )(states, *shared)
     totals = lax.all_to_all(totals, "z", 0, 0, tiled=True)
-    hyena, side, half = call(
+    swapped = [lax.ppermute(x, "core", [(0, 1), (1, 0)]) for x in (side, half)]
+    hyena = call(
         lambda *refs: mix_body(taps, rows * plane, *refs),
-        [VMEM] * 2 + [HBM] + [ANY] * 2 + [VMEM] * len(shared),
-        (pltpu.HBM((parts, rows, channels), BF16), shape(side.shape, BF16), shape(half.shape, BF16)),
+        [VMEM] * 2 + [ANY] + [VMEM] * len(shared),
+        shape((parts, rows, channels), BF16),
         "mix",
         scratch,
-        out_spec=(HBM, ANY, ANY),
-        aliases={2: 0, 3: 1, 4: 2},
-    )(before, totals, hyena, side, half, *shared)
-    swapped = [lax.ppermute(x, "core", [(0, 1), (1, 0)]) for x in (side, half)]
+        out_spec=ANY,
+        aliases={2: 0},
+        us=2,
+    )(before, totals, hyena, *shared)
     hyena = lax.all_to_all(hyena, "tp", 0, 0, tiled=True)
-    hyena = call(order_body, [VMEM], shape((rows, parts * channels), BF16), "order", us=4)(hyena)
+    hyena = call(order_body, [VMEM], shape((rows, parts * channels), BF16), "order", us=0)(hyena)
     block = 256
     return call(
         project_body,

time: 56.6 us -> 55.3 us (0.977)
  blocking collectives: 0 us -> 9.35 us
  waiting for transfers between devices: 13.8 us -> 7.99 us
  starting transfers between devices: 35.8 us -> 31.4 us
    all_to_all x0 -> x1, blocking collectives: none -> 9.35 us  [local(): hyena = lax.all_to_all(hyena, 'tp', 0, 0, tiled=True)]
    all_to_all x1, waiting for transfers between devices: 7.42 us -> 3.07 us  [local(): totals = lax.all_to_all(totals, 'z', 0, 0, tiled=True)]
    all_to_all x1 -> x0, starting transfers between devices: 4.03 us -> none  [local(): hyena = lax.all_to_all(hyena, 'tp', 0, 0, tiled=True)]
    ppermute x2, waiting for transfers between devices: 1.24 us -> 0.01 us  [local(): swapped = [lax.ppermute(x, 'core', [(0, 1), (1, 0)]) for x in (side, half)]]
    ppermute x2, starting transfers between devices: 5.29 us -> 4.33 us  [local(): swapped = [lax.ppermute(x, 'core', [(0, 1), (1, 0)]) for x in (side, half)]]
  transfers between devices with their start and end apart: 8 -> 7, of which waited for: 5 -> 3; matrix products, arithmetic and copies ran while one was open for 0% -> 0% of each run, Pallas kernels for 6% -> 6%
where the time goes in v14:
time: 55.3 us; the launch traced here: 54.6 us
  starting transfers between devices  31.4 us (57%)
  blocking collectives  9.35 us (17%)
  waiting for transfers between devices  7.99 us (14%)
  Pallas kernels  5.75 us (10%)
    all_to_all x1, starting transfers between devices, local(): totals = lax.all_to_all(totals, 'z', 0, 0, tiled=True)  9.54 us
    all_to_all x1, blocking collectives, local(): hyena = lax.all_to_all(hyena, 'tp', 0, 0, tiled=True)  9.35 us
    all_to_all x1, starting transfers between devices, local(): states = lax.all_to_all(states, ('y', 'core'), 0, 0, tiled=True)  6.13 us
    ppermute x1, starting transfers between devices, local(): rims = lax.ppermute(rims, order, [(i, i + 1) for i in range(devices - 1)])  4.59 us
    ppermute x1, starting transfers between devices, local(): lax.ppermute(side, ('core', 'tp'), [(c * parts + t, c * parts + (t + 1 -...  4.37 us
    ppermute x2, starting transfers between devices, local(): swapped = [lax.ppermute(x, 'core', [(0, 1), (1, 0)]) for x in (side, half)]  4.33 us
    all_to_all x1, waiting for transfers between devices, local(): totals = lax.all_to_all(totals, 'z', 0, 0, tiled=True)  3.07 us
    ppermute x1, waiting for transfers between devices, local(): rims = lax.ppermute(rims, order, [(i, i + 1) for i in range(devices - 1)])  2.56 us
  transfers between devices with their start and end apart: 7, of which 3 were waited for; matrix products, arithmetic and copies ran while one was open for 0% of the time, Pallas kernels for 6%

profile of v14, /device:TPU:1, one launch (start us, length us, event | category | flops | bytes accessed | tf_op | source)
XLA Modules:
  0.0 54.6 jit_solution(9311762775804201725)
XLA Ops:
  0.0 0.8 %rims.1 = bf16[48,256]{1,0:T(8,128)(2,1)S(1)} custom-call(bf16[128,256]{1,0:T(8,128)(2,1)} %q_hbm.1, bf16[128,256]{1,0:T(8,128)(2,1)} %k_hbm.1, bf16[128,256]{1,0:T(8,128)(2,1)} %v_hbm.1), custom_call_target="tpu_custom_call" | custom-call | tf_op jit(solution)/shard_map/rims/pallas_call | solution.py:313
  0.8 4.6 %collective-permute-start = (bf16[48,256]{1,0:T(8,128)(2,1)S(1)}, bf16[48,256]{1,0:T(8,128)(2,1)S(1)}, u32[]{:S(2)}, u32[]{:S(2)}) collective-permute-start(bf16[48,256]{1,0:T(8,128)(2,1)S(1)} %rims.1), channel_id=1, source_target_pairs={{0,4},{4,8},{8,12},{12,16},{16,20},{20,24},{24,28},{28,32},{32,36}... | collective-permute-start | bytes 73736 | tf_op jit(solution)/shard_map/ppermute | solution.py:316
  5.4 1.7 %gate.1 = (f32[2,128,128]{2,1,0:T(8,128)S(1)}, f32[2,128,128]{2,1,0:T(8,128)S(1)}, f32[16,8,256]{2,1,0:T(8,128)S(1)}, f32[16,256]{1,0:T(8,128)S(1)}, f32[3,8,256...) custom-call(bf16[128,256]{1,0:T(8,128)(2,1)} %q_hbm.1, ...), custom_call_target="tpu_custom_call" | custom-call | tf_op jit(solution)/shard_map/gate/pallas_call | solution.py:317
  7.0 2.6 %collective-permute-done.refs_0_ = bf16[48,256]{1,0:T(8,128)(2,1)S(1)} collective-permute-done((bf16[48,256]{1,0:T(8,128)(2,1)S(1)}, bf16[48,256]{1,0:T(8,128)(2,1)S(1)}, u32[]{:S(2)}, u32[]{:S(2)}) %collective-permute-start) | collective-permute-done | bytes 24608 | tf_op jit(solution)/shard_map/ppermute | solution.py:316
  9.6 0.7 %join.1 = (bf16[16,16,256]{2,1,0:T(8,128)(2,1)}, f32[16,256]{1,0:T(8,128)S(1)}, f32[2,8,256]{2,1,0:T(8,128)S(1)}) custom-call(bf16[48,256]{1,0:T(8,128)(2,1)S(1)} %collective-permute-done.refs_0_, f32[3,8,256]{2,1,0:T(8,128)S(1)} %get-tuple-element.23.refs_1_, f32[3,7,256]{2,1,0:T(8,128)S(1)} %get-tuple-element.24.refs_2_, ...), custom_call_target="tpu_custom_call" | custom-call | tf_op jit(solution)/shard_map/join/pallas_call | solution.py:349
  10.3 6.1 %all-to-all-start = ((bf16[16,16,256]{2,1,0:T(8,128)(2,1)}), bf16[16,16,256]{2,1,0:T(8,128)(2,1)S(1)}, u32[]{:S(2)}, u32[]{:S(2)}) async-start(bf16[16,16,256]{2,1,0:T(8,128)(2,1)} %get-tuple-element.27), calls=%async_computation | async-start | bytes 262144 | tf_op jit(solution)/shard_map/all_to_all | solution.py:360
  16.5 4.4 %collective-permute-start.1 = (bf16[256,1024]{1,0:T(8,128)(2,1)S(1)}, bf16[256,1024]{1,0:T(8,128)(2,1)S(1)}, u32[]{:S(2)}, u32[]{:S(2)}) collective-permute-start(bf16[256,1024]{1,0:T(8,128)(2,1)S(1)} %get-tuple-element.39), channel_id=1, source_target_pairs={{0,1},{1,2},{2,3},{3,0},{4,7},{5,4},{6,5},{7,6},{8,9},{9,10},{10,1... | collective-permute-start | bytes 1572872 | tf_op jit(solution)/shard_map/ppermute | solution.py:343
  20.8 2.4 %collective-permute-start.3 = (bf16[128,1024]{1,0:T(8,128)(2,1)S(1)}, bf16[128,1024]{1,0:T(8,128)(2,1)S(1)}, u32[]{:S(2)}, u32[]{:S(2)}) collective-permute-start(bf16[128,1024]{1,0:T(8,128)(2,1)S(1)} %get-tuple-element.40), channel_id=1, source_target_pairs={{0,2},{1,3},{2,0},{3,1},{4,6},{5,7},{6,4},{7,5},{8,10},{9,11},{10,... | collective-permute-start | bytes 786440 | tf_op jit(solution)/shard_map/ppermute | solution.py:348
  23.3 2.3 %all-to-all-done.refs_0_ = bf16[16,16,256]{2,1,0:T(8,128)(2,1)S(1)} async-done(((bf16[16,16,256]{2,1,0:T(8,128)(2,1)}), bf16[16,16,256]{2,1,0:T(8,128)(2,1)S(1)}, u32[]{:S(2)}, u32[]{:S(2)}) %all-to-all-start) | async-done | bytes 131104 | tf_op jit(solution)/shard_map/all_to_all | solution.py:360
  25.6 1.3 %plane.1 = (f32[16,256]{1,0:T(8,128)S(1)}, bf16[8,16,256]{2,1,0:T(8,128)(2,1)}, bf16[4,128,256]{2,1,0:T(8,128)(2,1)S(1)}) custom-call(bf16[16,16,256]{2,1,0:T(8,128)(2,1)S(1)} %all-to-all-done.refs_0_, f32[2,128,128]{2,1,0:T(8,128)S(1)} %get-tuple-element.28.refs_1_.refs_3_, f32[2,128,128]{2,1,0:T(8,128)S(1)} %get-tuple-element.29.refs_2_.refs_4_, ...), custom_call_target="tpu_custom_call" | custom-call | flops 4600000000 | tf_op jit(solution)/shard_map/plane/pallas_call | solution.py:368
  26.9 9.5 %all-to-all-start.1 = ((bf16[8,16,256]{2,1,0:T(8,128)(2,1)}), bf16[8,16,256]{2,1,0:T(8,128)(2,1)S(1)}, u32[]{:S(2)}, u32[]{:S(2)}) async-start(bf16[8,16,256]{2,1,0:T(8,128)(2,1)} %get-tuple-element.36), calls=%async_computation.1 | async-start | bytes 131072 | tf_op jit(solution)/shard_map/all_to_all | solution.py:381
  36.5 0.0 collective-permute-done.1.rest_1_
  36.5 1.9 %collective-permute-start.2 = (bf16[256,1024]{1,0:T(8,128)(2,1)S(1)}, bf16[256,1024]{1,0:T(8,128)(2,1)S(1)}, u32[]{:S(2)}, u32[]{:S(2)}) collective-permute-start(bf16[256,1024]{1,0:T(8,128)(2,1)S(1)} %collective-permute-done.1.rest_1_), channel_id=1, source_target_pairs={{0,4},{4,0},{1,5},{5,1},{2,6},{6,2},{3,7},{7,3},{8,12},{12,8},{9,1... | collective-permute-start | bytes 1572872 | tf_op jit(solution)/shard_map/ppermute | solution.py:382
  38.4 0.0 collective-permute-done.3.rest_3_
  38.4 2.4 %collective-permute-start.4 = (bf16[128,1024]{1,0:T(8,128)(2,1)S(1)}, bf16[128,1024]{1,0:T(8,128)(2,1)S(1)}, u32[]{:S(2)}, u32[]{:S(2)}) collective-permute-start(bf16[128,1024]{1,0:T(8,128)(2,1)S(1)} %collective-permute-done.3.rest_3_), channel_id=1, source_target_pairs={{0,4},{4,0},{1,5},{5,1},{2,6},{6,2},{3,7},{7,3},{8,12},{12,8},{9,1... | collective-permute-start | bytes 786440 | tf_op jit(solution)/shard_map/ppermute | solution.py:382
  40.8 3.1 %all-to-all-done.1.refs_1_ = bf16[8,16,256]{2,1,0:T(8,128)(2,1)S(1)} async-done(((bf16[8,16,256]{2,1,0:T(8,128)(2,1)}), bf16[8,16,256]{2,1,0:T(8,128)(2,1)S(1)}, u32[]{:S(2)}, u32[]{:S(2)}) %all-to-all-start.1) | async-done | bytes 65568 | tf_op jit(solution)/shard_map/all_to_all | solution.py:381
  43.9 0.1 mix.1
  44.0 9.3 %all_to_all.15.left_ref = bf16[4,128,256]{2,1,0:T(8,128)(2,1)S(1)} all-to-all(bf16[4,128,256]{2,1,0:T(8,128)(2,1)S(1)} %mix.1), channel_id=1, replica_groups=mesh['z'=8,'y'=8,'core'=2,'tp'=4] {'tp'}, dimensions={0} | all-to-all | bytes 524288 | tf_op jit(solution)/shard_map/all_to_all | solution.py:393
  53.4 0.0 collective-permute-done.4.rest_4_
  53.4 0.0 collective-permute-done.2.rest_2_
  53.4 1.2 %project.1 = bf16[128,1024]{1,0:T(8,128)(2,1)} custom-call(bf16[128,1024]{1,0:T(8,128)(2,1)S(1)} %order.1.left_ref, bf16[256,1024]{1,0:T(8,128)(2,1)S(1)} %get-tuple-element.38.rest_0_, bf16[256,1024]{1,0:T(8,128)(2,1)S(1)} %collective-permute-done.1.rest_1_, bf16[256,1024]{1,0:T(8,128)(2,1)S(1)} %collective-permute-done.2.rest_2_, ...), custom_call_target="tpu_custom_call" | custom-call | tf_op jit(solution)/shard_map/project/pallas_call | solution.py:396
  (1 shorter events, 0.0 us)
Async XLA Ops:
  0.8 8.8 %collective-permute-start = (bf16[48,256]{1,0:T(8,128)(2,1)S(1)}, bf16[48,256]{1,0:T(8,128)(2,1)S(1)}, u32[]{:S(2)}, u32[]{:S(2)}) collective-permute-start(bf16[48,256]{1,0:T(8,128)(2,1)S(1)} %rims.1), channel_id=1, source_target_pairs={{0,4},{4,8},{8,12},{12,16},{16,20},{20,24},{24,28},{28,32},{32,36}... | collective-permute-start | bytes 73736 | tf_op jit(solution)/shard_map/ppermute | solution.py:316
  10.3 15.3 %all-to-all-start = ((bf16[16,16,256]{2,1,0:T(8,128)(2,1)}), bf16[16,16,256]{2,1,0:T(8,128)(2,1)S(1)}, u32[]{:S(2)}, u32[]{:S(2)}) async-start(bf16[16,16,256]{2,1,0:T(8,128)(2,1)} %get-tuple-element.27), calls=%async_computation | async-start | bytes 262144 | tf_op jit(solution)/shard_map/all_to_all | solution.py:360
  16.5 20.0 %collective-permute-start.1 = (bf16[256,1024]{1,0:T(8,128)(2,1)S(1)}, bf16[256,1024]{1,0:T(8,128)(2,1)S(1)}, u32[]{:S(2)}, u32[]{:S(2)}) collective-permute-start(bf16[256,1024]{1,0:T(8,128)(2,1)S(1)} %get-tuple-element.39), channel_id=1, source_target_pairs={{0,1},{1,2},{2,3},{3,0},{4,7},{5,4},{6,5},{7,6},{8,9},{9,10},{10,1... | collective-permute-start | bytes 1572872 | tf_op jit(solution)/shard_map/ppermute | solution.py:343
  20.8 17.6 %collective-permute-start.3 = (bf16[128,1024]{1,0:T(8,128)(2,1)S(1)}, bf16[128,1024]{1,0:T(8,128)(2,1)S(1)}, u32[]{:S(2)}, u32[]{:S(2)}) collective-permute-start(bf16[128,1024]{1,0:T(8,128)(2,1)S(1)} %get-tuple-element.40), channel_id=1, source_target_pairs={{0,2},{1,3},{2,0},{3,1},{4,6},{5,7},{6,4},{7,5},{8,10},{9,11},{10,... | collective-permute-start | bytes 786440 | tf_op jit(solution)/shard_map/ppermute | solution.py:348
  26.9 17.0 %all-to-all-start.1 = ((bf16[8,16,256]{2,1,0:T(8,128)(2,1)}), bf16[8,16,256]{2,1,0:T(8,128)(2,1)S(1)}, u32[]{:S(2)}, u32[]{:S(2)}) async-start(bf16[8,16,256]{2,1,0:T(8,128)(2,1)} %get-tuple-element.36), calls=%async_computation.1 | async-start | bytes 131072 | tf_op jit(solution)/shard_map/all_to_all | solution.py:381
  36.5 16.9 %collective-permute-start.2 = (bf16[256,1024]{1,0:T(8,128)(2,1)S(1)}, bf16[256,1024]{1,0:T(8,128)(2,1)S(1)}, u32[]{:S(2)}, u32[]{:S(2)}) collective-permute-start(bf16[256,1024]{1,0:T(8,128)(2,1)S(1)} %collective-permute-done.1.rest_1_), channel_id=1, source_target_pairs={{0,4},{4,0},{1,5},{5,1},{2,6},{6,2},{3,7},{7,3},{8,12},{12,8},{9,1... | collective-permute-start | bytes 1572872 | tf_op jit(solution)/shard_map/ppermute | solution.py:382
  38.4 15.0 %collective-permute-start.4 = (bf16[128,1024]{1,0:T(8,128)(2,1)S(1)}, bf16[128,1024]{1,0:T(8,128)(2,1)S(1)}, u32[]{:S(2)}, u32[]{:S(2)}) collective-permute-start(bf16[128,1024]{1,0:T(8,128)(2,1)S(1)} %collective-permute-done.3.rest_3_), channel_id=1, source_target_pairs={{0,4},{4,0},{1,5},{5,1},{2,6},{6,2},{3,7},{7,3},{8,12},{12,8},{9,1... | collective-permute-start | bytes 786440 | tf_op jit(solution)/shard_map/ppermute | solution.py:382

commit v15 on v14

--- a/solution.py
+++ b/solution.py
@@ -164,23 +164,7 @@
     for i in range(1, taps - 1):
         late = retain * late + more[i : i + 1]
     late_ref[...] = late
-    whole = (state_ref[...] + jnp.exp(-(rows - taps + 1) * rate) * late).astype(BF16)
-    for i in range(out_ref.shape[0]):
-        out_ref[i] = whole
-
-
-def plane_body(rows, parts_ref, rate_ref, _block, before_ref, total_ref, _same_block):
-    me = lax.axis_index("y") * lax.axis_size("core") + lax.axis_index("core")
-    drop = jnp.exp(-rows * rate_ref[...])
-    before = jnp.zeros(rate_ref.shape, F32)
-    total = jnp.zeros(rate_ref.shape, F32)
-    for i in range(parts_ref.shape[0]):
-        part = parts_ref[i].astype(F32)
-        before = jnp.where(i < me, before * drop + part, before)
-        total = total * drop + part
-    before_ref[...] = before
-    for i in range(total_ref.shape[0]):
-        total_ref[i] = total.astype(BF16)
+    out_ref[...] = (state_ref[...] + jnp.exp(-(rows - taps + 1) * rate) * late).astype(BF16)
 
 
 def mix(taps, carried, refs, out_hbm, hyena, left, carry, sems):
@@ -223,17 +207,26 @@
         copy.wait()
 
 
-def plane_body(taps, rows, parts_ref, *refs):
+def pair_body(rows, pair_ref, rate_ref, out_ref):
+    drop = jnp.exp(-rows * rate_ref[...])
+    whole = (pair_ref[0].astype(F32) * drop + pair_ref[1].astype(F32)).astype(BF16)
+    for i in range(out_ref.shape[0]):
+        out_ref[i] = whole
+
+
+def plane_body(taps, rows, parts_ref, pair_ref, *refs):
     *refs, before_ref, total_ref, out_hbm, hyena, left, carry, sems = refs
     rate_ref = refs[5]
-    me = lax.axis_index("y") * lax.axis_size("core") + lax.axis_index("core")
-    drop = jnp.exp(-rows * rate_ref[...])
+    y = lax.axis_index("y")
+    drop = jnp.exp(-2 * rows * rate_ref[...])
     before = jnp.zeros(rate_ref.shape, F32)
     total = jnp.zeros(rate_ref.shape, F32)
     for i in range(parts_ref.shape[0]):
         part = parts_ref[i].astype(F32)
-        before = jnp.where(i < me, before * drop + part, before)
+        before = jnp.where(i < y, before * drop + part, before)
         total = total * drop + part
+    second = before * jnp.exp(-rows * rate_ref[...]) + pair_ref[0].astype(F32)
+    before = jnp.where(lax.axis_index("core") == 0, before, second)
     before_ref[...] = before
     for i in range(total_ref.shape[0]):
         total_ref[i] = total.astype(BF16)
@@ -350,14 +343,18 @@
         lambda *refs: join_body(rows, *refs),
         [VMEM] * 5,
         (
-            shape((plane, modes, channels), BF16),
+            shape((modes, channels), BF16),
             shape((modes, channels), F32),
             shape((2, HEAD, channels), F32),
         ),
         "join",
         [pltpu.VMEM((3, 2 * HEAD, channels), F32)],
     )(rims, heads, taps_here, rate, states)
-    states = lax.all_to_all(states, ("y", "core"), 0, 0, tiled=True)
+    pair = lax.all_gather(states, "core")
+    states = call(
+        lambda *refs: pair_body(rows, *refs), [VMEM] * 2, shape((plane // 2, modes, channels), BF16), "pair"
+    )(pair, rate)
+    states = lax.all_to_all(states, "y", 0, 0, tiled=True)
     shared = (queries, gated, begin, late, top, rate, amplitude, skip)
     scratch = [
         pltpu.VMEM(by_half, F32),
@@ -367,7 +364,7 @@
     ]
     before, totals, hyena = call(
         lambda *refs: plane_body(taps, rows, *refs),
-        [VMEM] * (1 + len(shared)),
+        [VMEM] * (2 + len(shared)),
         (
             shape((modes, channels), F32),
             shape((planes, modes, channels), BF16),
@@ -377,7 +374,7 @@
         scratch,
         out_spec=(VMEM, VMEM, ANY),
         us=4,
-    )(states, *shared)
+    )(states, pair, *shared)
     totals = lax.all_to_all(totals, "z", 0, 0, tiled=True)
     swapped = [lax.ppermute(x, "core", [(0, 1), (1, 0)]) for x in (side, half)]
     hyena = call(

time: 55.3 us -> 56.4 us (1.020)
  the two profiles are of different devices: /device:TPU:1 before, /device:TPU:2 now
where the time goes in v15:
time: 56.4 us; the launch traced here: 55.8 us
  starting transfers between devices  30.8 us (55%)
  blocking collectives  13.2 us (23%)
  waiting for transfers between devices  5.99 us (11%)
  Pallas kernels  5.7 us (10%)
    all_to_all x1, blocking collectives, local(): hyena = lax.all_to_all(hyena, 'tp', 0, 0, tiled=True)  9.85 us
    all_to_all x1, starting transfers between devices, local(): totals = lax.all_to_all(totals, 'z', 0, 0, tiled=True)  9.82 us
    all_to_all x1, starting transfers between devices, local(): states = lax.all_to_all(states, 'y', 0, 0, tiled=True)  8.48 us
    ppermute x2, starting transfers between devices, local(): swapped = [lax.ppermute(x, 'core', [(0, 1), (1, 0)]) for x in (side, half)]  4.33 us
    all_to_all x1, waiting for transfers between devices, local(): totals = lax.all_to_all(totals, 'z', 0, 0, tiled=True)  4.02 us
    ppermute x1, starting transfers between devices, local(): lax.ppermute(side, ('core', 'tp'), [(c * parts + t, c * parts + (t + 1 -...  3.39 us
    all_gather x1, blocking collectives, local(): pair = lax.all_gather(states, 'core')  3.35 us
    ppermute x1, starting transfers between devices, local(): lax.ppermute(half, 'tp', [(t, (t + 2) % parts) for t in range(parts)])  3.02 us
  transfers between devices with their start and end apart: 7, of which 2 were waited for; matrix products, arithmetic and copies ran while one was open for 0% of the time, Pallas kernels for 5%

profile of v15, /device:TPU:2, one launch (start us, length us, event | category | flops | bytes accessed | tf_op | source)
XLA Modules:
  0.0 55.8 jit_solution(14486644716318051487)
XLA Ops:
  0.0 0.8 %rims.1 = bf16[48,256]{1,0:T(8,128)(2,1)S(1)} custom-call(bf16[128,256]{1,0:T(8,128)(2,1)} %q_hbm.1, bf16[128,256]{1,0:T(8,128)(2,1)} %k_hbm.1, bf16[128,256]{1,0:T(8,128)(2,1)} %v_hbm.1), custom_call_target="tpu_custom_call" | custom-call | tf_op jit(solution)/shard_map/rims/pallas_call | solution.py:306
  0.8 1.7 %collective-permute-start = (bf16[48,256]{1,0:T(8,128)(2,1)S(1)}, bf16[48,256]{1,0:T(8,128)(2,1)S(1)}, u32[]{:S(2)}, u32[]{:S(2)}) collective-permute-start(bf16[48,256]{1,0:T(8,128)(2,1)S(1)} %rims.1), channel_id=1, source_target_pairs={{0,4},{4,8},{8,12},{12,16},{16,20},{20,24},{24,28},{28,32},{32,36}... | collective-permute-start | bytes 73736 | tf_op jit(solution)/shard_map/ppermute | solution.py:309
  2.5 1.7 %gate.1 = (f32[2,128,128]{2,1,0:T(8,128)S(1)}, f32[2,128,128]{2,1,0:T(8,128)S(1)}, f32[16,8,256]{2,1,0:T(8,128)S(1)}, f32[16,256]{1,0:T(8,128)S(1)}, f32[3,8,256...) custom-call(bf16[128,256]{1,0:T(8,128)(2,1)} %q_hbm.1, ...), custom_call_target="tpu_custom_call" | custom-call | tf_op jit(solution)/shard_map/gate/pallas_call | solution.py:310
  4.2 0.0 collective-permute-done.refs_0_
  4.2 0.1 join.1
  4.3 3.4 %all-gather = bf16[32,256]{1,0:T(8,128)(2,1)S(1)} all-gather(bf16[16,256]{1,0:T(8,128)(2,1)S(1)} %get-tuple-element.27), channel_id=2, replica_groups=mesh['z'=8,'y'=8,'core'=2,'tp'=4] {'core'}, dimensions={0}, use_global_device_ids=true | all-gather | bytes 24576 | tf_op jit(solution)/shard_map/all_gather | solution.py:353
  7.6 0.6 %pair.1 = bf16[8,16,256]{2,1,0:T(8,128)(2,1)} custom-call(bf16[2,16,256]{2,1,0:T(8,128)(2,1)S(1)} %bitcast.2, f32[16,256]{1,0:T(8,128)S(1)} %get-tuple-element.25.refs_3_.refs_1_.refs_7_.refs_8_), custom_call_target="tpu_custom_call" | custom-call | tf_op jit(solution)/shard_map/pair/pallas_call | solution.py:354
  8.3 8.5 %all-to-all-start = ((bf16[8,16,256]{2,1,0:T(8,128)(2,1)}), bf16[8,16,256]{2,1,0:T(8,128)(2,1)S(1)}, u32[]{:S(2)}, u32[]{:S(2)}) async-start(bf16[8,16,256]{2,1,0:T(8,128)(2,1)} %pair.1), calls=%async_computation | async-start | bytes 131072 | tf_op jit(solution)/shard_map/all_to_all | solution.py:357
  16.7 3.4 %collective-permute-start.1 = (bf16[256,1024]{1,0:T(8,128)(2,1)S(1)}, bf16[256,1024]{1,0:T(8,128)(2,1)S(1)}, u32[]{:S(2)}, u32[]{:S(2)}) collective-permute-start(bf16[256,1024]{1,0:T(8,128)(2,1)S(1)} %get-tuple-element.39), channel_id=1, source_target_pairs={{0,1},{1,2},{2,3},{3,0},{4,7},{5,4},{6,5},{7,6},{8,9},{9,10},{10,1... | collective-permute-start | bytes 1572872 | tf_op jit(solution)/shard_map/ppermute | solution.py:336
  20.1 3.0 %collective-permute-start.3 = (bf16[128,1024]{1,0:T(8,128)(2,1)S(1)}, bf16[128,1024]{1,0:T(8,128)(2,1)S(1)}, u32[]{:S(2)}, u32[]{:S(2)}) collective-permute-start(bf16[128,1024]{1,0:T(8,128)(2,1)S(1)} %get-tuple-element.40), channel_id=1, source_target_pairs={{0,2},{1,3},{2,0},{3,1},{4,6},{5,7},{6,4},{7,5},{8,10},{9,11},{10,... | collective-permute-start | bytes 786440 | tf_op jit(solution)/shard_map/ppermute | solution.py:341
  23.2 2.0 %all-to-all-done.refs_0_ = bf16[8,16,256]{2,1,0:T(8,128)(2,1)S(1)} async-done(((bf16[8,16,256]{2,1,0:T(8,128)(2,1)}), bf16[8,16,256]{2,1,0:T(8,128)(2,1)S(1)}, u32[]{:S(2)}, u32[]{:S(2)}) %all-to-all-start) | async-done | bytes 65568 | tf_op jit(solution)/shard_map/all_to_all | solution.py:357
  25.1 1.3 %plane.1 = (f32[16,256]{1,0:T(8,128)S(1)}, bf16[8,16,256]{2,1,0:T(8,128)(2,1)}, bf16[4,128,256]{2,1,0:T(8,128)(2,1)S(1)}) custom-call(bf16[8,16,256]{2,1,0:T(8,128)(2,1)S(1)} %all-to-all-done.refs_0_, bf16[2,16,256]{2,1,0:T(8,128)(2,1)S(1)} %bitcast.3, f32[2,128,128]{2,1,0:T(8,128)S(1)} %get-tuple-element.28.refs_2_.refs_3_, ...), custom_call_target="tpu_custom_call" | custom-call | flops 4600000000 | tf_op jit(solution)/shard_map/plane/pallas_call | solution.py:365
  26.4 9.8 %all-to-all-start.1 = ((bf16[8,16,256]{2,1,0:T(8,128)(2,1)}), bf16[8,16,256]{2,1,0:T(8,128)(2,1)S(1)}, u32[]{:S(2)}, u32[]{:S(2)}) async-start(bf16[8,16,256]{2,1,0:T(8,128)(2,1)} %get-tuple-element.36), calls=%async_computation.1 | async-start | bytes 131072 | tf_op jit(solution)/shard_map/all_to_all | solution.py:378
  36.2 0.0 collective-permute-done.1.rest_1_
  36.2 1.9 %collective-permute-start.2 = (bf16[256,1024]{1,0:T(8,128)(2,1)S(1)}, bf16[256,1024]{1,0:T(8,128)(2,1)S(1)}, u32[]{:S(2)}, u32[]{:S(2)}) collective-permute-start(bf16[256,1024]{1,0:T(8,128)(2,1)S(1)} %collective-permute-done.1.rest_1_), channel_id=1, source_target_pairs={{0,4},{4,0},{1,5},{5,1},{2,6},{6,2},{3,7},{7,3},{8,12},{12,8},{9,1... | collective-permute-start | bytes 1572872 | tf_op jit(solution)/shard_map/ppermute | solution.py:379
  38.1 0.0 collective-permute-done.3.rest_3_
  38.1 2.4 %collective-permute-start.4 = (bf16[128,1024]{1,0:T(8,128)(2,1)S(1)}, bf16[128,1024]{1,0:T(8,128)(2,1)S(1)}, u32[]{:S(2)}, u32[]{:S(2)}) collective-permute-start(bf16[128,1024]{1,0:T(8,128)(2,1)S(1)} %collective-permute-done.3.rest_3_), channel_id=1, source_target_pairs={{0,4},{4,0},{1,5},{5,1},{2,6},{6,2},{3,7},{7,3},{8,12},{12,8},{9,1... | collective-permute-start | bytes 786440 | tf_op jit(solution)/shard_map/ppermute | solution.py:379
  40.6 4.0 %all-to-all-done.1.refs_1_ = bf16[8,16,256]{2,1,0:T(8,128)(2,1)S(1)} async-done(((bf16[8,16,256]{2,1,0:T(8,128)(2,1)}), bf16[8,16,256]{2,1,0:T(8,128)(2,1)S(1)}, u32[]{:S(2)}, u32[]{:S(2)}) %all-to-all-start.1) | async-done | bytes 65568 | tf_op jit(solution)/shard_map/all_to_all | solution.py:378
  44.6 0.1 mix.1
  44.7 9.8 %all_to_all.15.left_ref = bf16[4,128,256]{2,1,0:T(8,128)(2,1)S(1)} all-to-all(bf16[4,128,256]{2,1,0:T(8,128)(2,1)S(1)} %mix.1), channel_id=1, replica_groups=mesh['z'=8,'y'=8,'core'=2,'tp'=4] {'tp'}, dimensions={0} | all-to-all | bytes 524288 | tf_op jit(solution)/shard_map/all_to_all | solution.py:390
  54.5 0.0 collective-permute-done.4.rest_4_
  54.6 0.0 collective-permute-done.2.rest_2_
  54.6 1.2 %project.1 = bf16[128,1024]{1,0:T(8,128)(2,1)} custom-call(bf16[128,1024]{1,0:T(8,128)(2,1)S(1)} %order.1.left_ref, bf16[256,1024]{1,0:T(8,128)(2,1)S(1)} %get-tuple-element.38.rest_0_, bf16[256,1024]{1,0:T(8,128)(2,1)S(1)} %collective-permute-done.1.rest_1_, bf16[256,1024]{1,0:T(8,128)(2,1)S(1)} %collective-permute-done.2.rest_2_, ...), custom_call_target="tpu_custom_call" | custom-call | tf_op jit(solution)/shard_map/project/pallas_call | solution.py:393
  (1 shorter events, 0.0 us)
Async XLA Ops:
  0.8 3.4 %collective-permute-start = (bf16[48,256]{1,0:T(8,128)(2,1)S(1)}, bf16[48,256]{1,0:T(8,128)(2,1)S(1)}, u32[]{:S(2)}, u32[]{:S(2)}) collective-permute-start(bf16[48,256]{1,0:T(8,128)(2,1)S(1)} %rims.1), channel_id=1, source_target_pairs={{0,4},{4,8},{8,12},{12,16},{16,20},{20,24},{24,28},{28,32},{32,36}... | collective-permute-start | bytes 73736 | tf_op jit(solution)/shard_map/ppermute | solution.py:309
  8.3 16.9 %all-to-all-start = ((bf16[8,16,256]{2,1,0:T(8,128)(2,1)}), bf16[8,16,256]{2,1,0:T(8,128)(2,1)S(1)}, u32[]{:S(2)}, u32[]{:S(2)}) async-start(bf16[8,16,256]{2,1,0:T(8,128)(2,1)} %pair.1), calls=%async_computation | async-start | bytes 131072 | tf_op jit(solution)/shard_map/all_to_all | solution.py:357
  16.7 19.5 %collective-permute-start.1 = (bf16[256,1024]{1,0:T(8,128)(2,1)S(1)}, bf16[256,1024]{1,0:T(8,128)(2,1)S(1)}, u32[]{:S(2)}, u32[]{:S(2)}) collective-permute-start(bf16[256,1024]{1,0:T(8,128)(2,1)S(1)} %get-tuple-element.39), channel_id=1, source_target_pairs={{0,1},{1,2},{2,3},{3,0},{4,7},{5,4},{6,5},{7,6},{8,9},{9,10},{10,1... | collective-permute-start | bytes 1572872 | tf_op jit(solution)/shard_map/ppermute | solution.py:336
  20.1 18.0 %collective-permute-start.3 = (bf16[128,1024]{1,0:T(8,128)(2,1)S(1)}, bf16[128,1024]{1,0:T(8,128)(2,1)S(1)}, u32[]{:S(2)}, u32[]{:S(2)}) collective-permute-start(bf16[128,1024]{1,0:T(8,128)(2,1)S(1)} %get-tuple-element.40), channel_id=1, source_target_pairs={{0,2},{1,3},{2,0},{3,1},{4,6},{5,7},{6,4},{7,5},{8,10},{9,11},{10,... | collective-permute-start | bytes 786440 | tf_op jit(solution)/shard_map/ppermute | solution.py:341
  26.4 18.2 %all-to-all-start.1 = ((bf16[8,16,256]{2,1,0:T(8,128)(2,1)}), bf16[8,16,256]{2,1,0:T(8,128)(2,1)S(1)}, u32[]{:S(2)}, u32[]{:S(2)}) async-start(bf16[8,16,256]{2,1,0:T(8,128)(2,1)} %get-tuple-element.36), calls=%async_computation.1 | async-start | bytes 131072 | tf_op jit(solution)/shard_map/all_to_all | solution.py:378
  36.2 18.4 %collective-permute-start.2 = (bf16[256,1024]{1,0:T(8,128)(2,1)S(1)}, bf16[256,1024]{1,0:T(8,128)(2,1)S(1)}, u32[]{:S(2)}, u32[]{:S(2)}) collective-permute-start(bf16[256,1024]{1,0:T(8,128)(2,1)S(1)} %collective-permute-done.1.rest_1_), channel_id=1, source_target_pairs={{0,4},{4,0},{1,5},{5,1},{2,6},{6,2},{3,7},{7,3},{8,12},{12,8},{9,1... | collective-permute-start | bytes 1572872 | tf_op jit(solution)/shard_map/ppermute | solution.py:379
  38.1 16.4 %collective-permute-start.4 = (bf16[128,1024]{1,0:T(8,128)(2,1)S(1)}, bf16[128,1024]{1,0:T(8,128)(2,1)S(1)}, u32[]{:S(2)}, u32[]{:S(2)}) collective-permute-start(bf16[128,1024]{1,0:T(8,128)(2,1)S(1)} %collective-permute-done.3.rest_3_), channel_id=1, source_target_pairs={{0,4},{4,0},{1,5},{5,1},{2,6},{6,2},{3,7},{7,3},{8,12},{12,8},{9,1... | collective-permute-start | bytes 786440 | tf_op jit(solution)/shard_map/ppermute | solution.py:379

commit v16 on v14

--- a/solution.py
+++ b/solution.py
@@ -169,22 +169,8 @@
         out_ref[i] = whole
 
 
-def plane_body(rows, parts_ref, rate_ref, _block, before_ref, total_ref, _same_block):
-    me = lax.axis_index("y") * lax.axis_size("core") + lax.axis_index("core")
-    drop = jnp.exp(-rows * rate_ref[...])
-    before = jnp.zeros(rate_ref.shape, F32)
-    total = jnp.zeros(rate_ref.shape, F32)
-    for i in range(parts_ref.shape[0]):
-        part = parts_ref[i].astype(F32)
-        before = jnp.where(i < me, before * drop + part, before)
-        total = total * drop + part
-    before_ref[...] = before
-    for i in range(total_ref.shape[0]):
-        total_ref[i] = total.astype(BF16)
-
-
-def mix(taps, carried, refs, out_hbm, hyena, left, carry, sems):
-    query_ref, gated_ref, begin_ref, late_ref, top_ref, rate_ref, amp_ref, skip_ref = refs
+def mix(taps, carried, refs, out_hbm, own_part, hyena, left, carry, sems):
+    query_ref, gated_ref, begin_ref, late_ref, top_ref, rate_ref, amp_ref, skip_ref, own_ref = refs
     halves, rows, _ = query_ref.shape
     modes = rate_ref.shape[0]
     steps = rows // SUBS
@@ -219,12 +205,15 @@
             hyena[half, at, :] = query * terms[0]
         left[:, lanes] = hyena[half].astype(BF16)
         copies += fetch([left.at[:, lanes]] * parts, [out_hbm.at[i, :, lanes] for i in range(parts)], sems.at[half])
+    for c in range(0, own_part.shape[1], 256):
+        at = pl.ds(c, 256)
+        own_part[:, at] = jnp.dot(left[...], own_ref[:, at], preferred_element_type=F32).astype(BF16)
     for copy in copies:
         copy.wait()
 
 
 def plane_body(taps, rows, parts_ref, *refs):
-    *refs, before_ref, total_ref, out_hbm, hyena, left, carry, sems = refs
+    *refs, before_ref, total_ref, out_hbm, own_part, hyena, left, carry, sems = refs
     rate_ref = refs[5]
     me = lax.axis_index("y") * lax.axis_size("core") + lax.axis_index("core")
     drop = jnp.exp(-rows * rate_ref[...])
@@ -240,11 +229,11 @@
 
     @pl.when(lax.axis_index("z") == 0)
     def _():
-        mix(taps, before, refs, out_hbm, hyena, left, carry, sems)
-
-
-def mix_body(taps, plane_rows, before_ref, planes_ref, _hyena, *refs):
-    *refs, out_hbm, hyena, left, carry, sems = refs
+        mix(taps, before, refs, out_hbm, own_part, hyena, left, carry, sems)
+
+
+def mix_body(taps, plane_rows, before_ref, planes_ref, _hyena, _own_part, *refs):
+    *refs, out_hbm, own_part, hyena, left, carry, sems = refs
     query_ref, rate_ref = refs[0], refs[5]
     rows = query_ref.shape[1]
     z = lax.axis_index("z")
@@ -258,7 +247,7 @@
         for i in range(planes_ref.shape[0]):
             behind = jnp.where(i < z, behind * drop + planes_ref[i].astype(F32), behind)
         carried = before_ref[...] + jnp.exp(-(rows * me).astype(F32) * rate) * behind
-        mix(taps, carried, refs, out_hbm, hyena, left, carry, sems)
+        mix(taps, carried, refs, out_hbm, own_part, hyena, left, carry, sems)
 
 
 def order_body(left_ref, out_ref):
@@ -275,14 +264,14 @@
         out_ref[:, pl.ds(3 * channels + i * height, height)] = left_ref[across, :, columns]
 
 
-def project_body(left_ref, *rest):
+def project_body(left_ref, own_part, *rest):
     *rights, out_hbm, done, sems = rest
     blocks, _, block = done.shape
     copies = []
     for b in range(blocks):
         at = pl.ds(b * block, block)
-        total = jnp.zeros(done.shape[1:], F32)
-        begin = 0
+        total = own_part[:, at].astype(F32)
+        begin = rights[0].shape[0]
         for right in rights:
             depth = right.shape[0]
             total += jnp.dot(left_ref[:, pl.ds(begin, depth)], right[:, at], preferred_element_type=F32)
@@ -358,38 +347,39 @@
         [pltpu.VMEM((3, 2 * HEAD, channels), F32)],
     )(rims, heads, taps_here, rate, states)
     states = lax.all_to_all(states, ("y", "core"), 0, 0, tiled=True)
-    shared = (queries, gated, begin, late, top, rate, amplitude, skip)
+    shared = (queries, gated, begin, late, top, rate, amplitude, skip, own)
     scratch = [
         pltpu.VMEM(by_half, F32),
         pltpu.VMEM((rows, channels), BF16),
         pltpu.VMEM((2, modes, channels), F32),
         pltpu.SemaphoreType.DMA((channels // LANES, parts)),
     ]
-    before, totals, hyena = call(
+    before, totals, hyena, own_part = call(
         lambda *refs: plane_body(taps, rows, *refs),
         [VMEM] * (1 + len(shared)),
         (
             shape((modes, channels), F32),
             shape((planes, modes, channels), BF16),
             shape((parts, rows, channels), BF16),
+            shape((rows, width), BF16),
         ),
         "plane",
         scratch,
-        out_spec=(VMEM, VMEM, ANY),
+        out_spec=(VMEM, VMEM, ANY, VMEM),
         us=4,
     )(states, *shared)
     totals = lax.all_to_all(totals, "z", 0, 0, tiled=True)
     swapped = [lax.ppermute(x, "core", [(0, 1), (1, 0)]) for x in (side, half)]
-    hyena = call(
+    hyena, own_part = call(
         lambda *refs: mix_body(taps, rows * plane, *refs),
-        [VMEM] * 2 + [ANY] + [VMEM] * len(shared),
-        shape((parts, rows, channels), BF16),
+        [VMEM] * 2 + [ANY] + [VMEM] * (1 + len(shared)),
+        (shape((parts, rows, channels), BF16), shape((rows, width), BF16)),
         "mix",
         scratch,
-        out_spec=ANY,
-        aliases={2: 0},
+        out_spec=(ANY, VMEM),
+        aliases={2: 0, 3: 1},
         us=2,
-    )(before, totals, hyena, *shared)
+    )(before, totals, hyena, own_part, *shared)
     hyena = lax.all_to_all(hyena, "tp", 0, 0, tiled=True)
     hyena = call(order_body, [VMEM], shape((rows, parts * channels), BF16), "order", us=0)(hyena)
     block = 256
@@ -400,7 +390,7 @@
         "project",
         [pltpu.VMEM((width // block, rows, block), BF16), pltpu.SemaphoreType.DMA((width // block,))],
         out_spec=HBM,
-    )(hyena, own, side, swapped[0], half, swapped[1])
+    )(hyena, own_part, side, swapped[0], half, swapped[1])
 
 
 def solution(mesh):

time: 55.3 us -> 55.3 us (level)
  no operation moved by 1% of the time
where the time goes in v16:
time: 55.3 us; the launch traced here: 54.5 us
  starting transfers between devices  31.2 us (56%)
  blocking collectives  9.35 us (17%)
  waiting for transfers between devices  7.99 us (14%)
  Pallas kernels  5.91 us (11%)
    all_to_all x1, blocking collectives, local(): hyena = lax.all_to_all(hyena, 'tp', 0, 0, tiled=True)  9.35 us
    all_to_all x1, starting transfers between devices, local(): totals = lax.all_to_all(totals, 'z', 0, 0, tiled=True)  9.3 us
    all_to_all x1, starting transfers between devices, local(): states = lax.all_to_all(states, ('y', 'core'), 0, 0, tiled=True)  6.13 us
    ppermute x1, starting transfers between devices, local(): rims = lax.ppermute(rims, order, [(i, i + 1) for i in range(devices - 1)])  4.59 us
    ppermute x1, starting transfers between devices, local(): lax.ppermute(side, ('core', 'tp'), [(c * parts + t, c * parts + (t + 1 -...  4.37 us
    ppermute x2, starting transfers between devices, local(): swapped = [lax.ppermute(x, 'core', [(0, 1), (1, 0)]) for x in (side, half)]  4.33 us
    all_to_all x1, waiting for transfers between devices, local(): totals = lax.all_to_all(totals, 'z', 0, 0, tiled=True)  3.07 us
    ppermute x1, waiting for transfers between devices, local(): rims = lax.ppermute(rims, order, [(i, i + 1) for i in range(devices - 1)])  2.56 us
  transfers between devices with their start and end apart: 7, of which 3 were waited for; matrix products, arithmetic and copies ran while one was open for 0% of the time, Pallas kernels for 6%

profile of v16, /device:TPU:1, one launch (start us, length us, event | category | flops | bytes accessed | tf_op | source)
XLA Modules:
  0.0 54.5 jit_solution(9290659256001446013)
XLA Ops:
  0.0 0.8 %rims.1 = bf16[48,256]{1,0:T(8,128)(2,1)S(1)} custom-call(bf16[128,256]{1,0:T(8,128)(2,1)} %q_hbm.1, bf16[128,256]{1,0:T(8,128)(2,1)} %k_hbm.1, bf16[128,256]{1,0:T(8,128)(2,1)} %v_hbm.1), custom_call_target="tpu_custom_call" | custom-call | tf_op jit(solution)/shard_map/rims/pallas_call | solution.py:302
  0.8 4.6 %collective-permute-start = (bf16[48,256]{1,0:T(8,128)(2,1)S(1)}, bf16[48,256]{1,0:T(8,128)(2,1)S(1)}, u32[]{:S(2)}, u32[]{:S(2)}) collective-permute-start(bf16[48,256]{1,0:T(8,128)(2,1)S(1)} %rims.1), channel_id=1, source_target_pairs={{0,4},{4,8},{8,12},{12,16},{16,20},{20,24},{24,28},{28,32},{32,36}... | collective-permute-start | bytes 73736 | tf_op jit(solution)/shard_map/ppermute | solution.py:305
  5.4 1.7 %gate.1 = (f32[2,128,128]{2,1,0:T(8,128)S(1)}, f32[2,128,128]{2,1,0:T(8,128)S(1)}, f32[16,8,256]{2,1,0:T(8,128)S(1)}, f32[16,256]{1,0:T(8,128)S(1)}, f32[3,8,256...) custom-call(bf16[128,256]{1,0:T(8,128)(2,1)} %q_hbm.1, ...), custom_call_target="tpu_custom_call" | custom-call | tf_op jit(solution)/shard_map/gate/pallas_call | solution.py:306
  7.0 2.6 %collective-permute-done.refs_0_ = bf16[48,256]{1,0:T(8,128)(2,1)S(1)} collective-permute-done((bf16[48,256]{1,0:T(8,128)(2,1)S(1)}, bf16[48,256]{1,0:T(8,128)(2,1)S(1)}, u32[]{:S(2)}, u32[]{:S(2)}) %collective-permute-start) | collective-permute-done | bytes 24608 | tf_op jit(solution)/shard_map/ppermute | solution.py:305
  9.6 0.7 %join.1 = (bf16[16,16,256]{2,1,0:T(8,128)(2,1)}, f32[16,256]{1,0:T(8,128)S(1)}, f32[2,8,256]{2,1,0:T(8,128)S(1)}) custom-call(bf16[48,256]{1,0:T(8,128)(2,1)S(1)} %collective-permute-done.refs_0_, f32[3,8,256]{2,1,0:T(8,128)S(1)} %get-tuple-element.26.refs_1_, f32[3,7,256]{2,1,0:T(8,128)S(1)} %get-tuple-element.27.refs_2_, ...), custom_call_target="tpu_custom_call" | custom-call | tf_op jit(solution)/shard_map/join/pallas_call | solution.py:338
  10.3 6.1 %all-to-all-start = ((bf16[16,16,256]{2,1,0:T(8,128)(2,1)}), bf16[16,16,256]{2,1,0:T(8,128)(2,1)S(1)}, u32[]{:S(2)}, u32[]{:S(2)}) async-start(bf16[16,16,256]{2,1,0:T(8,128)(2,1)} %get-tuple-element.30), calls=%async_computation | async-start | bytes 262144 | tf_op jit(solution)/shard_map/all_to_all | solution.py:349
  16.5 4.4 %collective-permute-start.1 = (bf16[256,1024]{1,0:T(8,128)(2,1)S(1)}, bf16[256,1024]{1,0:T(8,128)(2,1)S(1)}, u32[]{:S(2)}, u32[]{:S(2)}) collective-permute-start(bf16[256,1024]{1,0:T(8,128)(2,1)S(1)} %get-tuple-element.45), channel_id=1, source_target_pairs={{0,1},{1,2},{2,3},{3,0},{4,7},{5,4},{6,5},{7,6},{8,9},{9,10},{10,1... | collective-permute-start | bytes 1572872 | tf_op jit(solution)/shard_map/ppermute | solution.py:332
  20.8 2.4 %collective-permute-start.3 = (bf16[128,1024]{1,0:T(8,128)(2,1)S(1)}, bf16[128,1024]{1,0:T(8,128)(2,1)S(1)}, u32[]{:S(2)}, u32[]{:S(2)}) collective-permute-start(bf16[128,1024]{1,0:T(8,128)(2,1)S(1)} %get-tuple-element.46), channel_id=1, source_target_pairs={{0,2},{1,3},{2,0},{3,1},{4,6},{5,7},{6,4},{7,5},{8,10},{9,11},{10,... | collective-permute-start | bytes 786440 | tf_op jit(solution)/shard_map/ppermute | solution.py:337
  23.3 2.3 %all-to-all-done.refs_0_ = bf16[16,16,256]{2,1,0:T(8,128)(2,1)S(1)} async-done(((bf16[16,16,256]{2,1,0:T(8,128)(2,1)}), bf16[16,16,256]{2,1,0:T(8,128)(2,1)S(1)}, u32[]{:S(2)}, u32[]{:S(2)}) %all-to-all-start) | async-done | bytes 131104 | tf_op jit(solution)/shard_map/all_to_all | solution.py:349
  25.6 1.5 %plane.1 = (f32[16,256]{1,0:T(8,128)S(1)}, bf16[8,16,256]{2,1,0:T(8,128)(2,1)}, bf16[4,128,256]{2,1,0:T(8,128)(2,1)S(1)}, bf16[128,1024]{1,0:T(8,128)(2,1)S(1)}) custom-call(bf16[16,16,256]{2,1,0:T(8,128)(2,1)S(1)} %all-to-all-done.refs_0_, f32[2,128,128]{2,1,0:T(8,128)S(1)} %get-tuple-element.31.refs_1_.refs_4_, ...), custom_call_target="tpu_custom_call" | custom-call | flops 4600000000 | tf_op jit(solution)/shard_map/plane/pallas_call | solution.py:357
  27.2 9.3 %all-to-all-start.1 = ((bf16[8,16,256]{2,1,0:T(8,128)(2,1)}), bf16[8,16,256]{2,1,0:T(8,128)(2,1)S(1)}, u32[]{:S(2)}, u32[]{:S(2)}) async-start(bf16[8,16,256]{2,1,0:T(8,128)(2,1)} %get-tuple-element.40), calls=%async_computation.1 | async-start | bytes 131072 | tf_op jit(solution)/shard_map/all_to_all | solution.py:371
  36.5 0.0 collective-permute-done.1.rest_0_
  36.5 1.9 %collective-permute-start.2 = (bf16[256,1024]{1,0:T(8,128)(2,1)S(1)}, bf16[256,1024]{1,0:T(8,128)(2,1)S(1)}, u32[]{:S(2)}, u32[]{:S(2)}) collective-permute-start(bf16[256,1024]{1,0:T(8,128)(2,1)S(1)} %collective-permute-done.1.rest_0_), channel_id=1, source_target_pairs={{0,4},{4,0},{1,5},{5,1},{2,6},{6,2},{3,7},{7,3},{8,12},{12,8},{9,1... | collective-permute-start | bytes 1572872 | tf_op jit(solution)/shard_map/ppermute | solution.py:372
  38.4 0.0 collective-permute-done.3.rest_2_
  38.4 2.4 %collective-permute-start.4 = (bf16[128,1024]{1,0:T(8,128)(2,1)S(1)}, bf16[128,1024]{1,0:T(8,128)(2,1)S(1)}, u32[]{:S(2)}, u32[]{:S(2)}) collective-permute-start(bf16[128,1024]{1,0:T(8,128)(2,1)S(1)} %collective-permute-done.3.rest_2_), channel_id=1, source_target_pairs={{0,4},{4,0},{1,5},{5,1},{2,6},{6,2},{3,7},{7,3},{8,12},{12,8},{9,1... | collective-permute-start | bytes 786440 | tf_op jit(solution)/shard_map/ppermute | solution.py:372
  40.8 3.1 %all-to-all-done.1.refs_1_ = bf16[8,16,256]{2,1,0:T(8,128)(2,1)S(1)} async-done(((bf16[8,16,256]{2,1,0:T(8,128)(2,1)}), bf16[8,16,256]{2,1,0:T(8,128)(2,1)S(1)}, u32[]{:S(2)}, u32[]{:S(2)}) %all-to-all-start.1) | async-done | bytes 65568 | tf_op jit(solution)/shard_map/all_to_all | solution.py:371
  43.9 0.1 mix.1
  44.0 9.3 %all_to_all.15.left_ref = bf16[4,128,256]{2,1,0:T(8,128)(2,1)S(1)} all-to-all(bf16[4,128,256]{2,1,0:T(8,128)(2,1)S(1)} %get-tuple-element.43), channel_id=1, replica_groups=mesh['z'=8,'y'=8,'core'=2,'tp'=4] {'tp'}, dimensions={0} | all-to-all | bytes 524288 | tf_op jit(solution)/shard_map/all_to_all | solution.py:383
  53.4 0.0 collective-permute-done.4.rest_3_
  53.4 0.0 collective-permute-done.2.rest_1_
  53.4 1.1 %project.1 = bf16[128,1024]{1,0:T(8,128)(2,1)} custom-call(bf16[128,1024]{1,0:T(8,128)(2,1)S(1)} %order.1.left_ref, bf16[128,1024]{1,0:T(8,128)(2,1)S(1)} %get-tuple-element.44.own_part, bf16[256,1024]{1,0:T(8,128)(2,1)S(1)} %collective-permute-done.1.rest_0_, bf16[256,1024]{1,0:T(8,128)(2,1)S(1)} %collective-permute-done.2.rest_1_, ...), custom_call_target="tpu_custom_call" | custom-call | tf_op jit(solution)/shard_map/project/pallas_call | solution.py:386
  (1 shorter events, 0.0 us)
Async XLA Ops:
  0.8 8.8 %collective-permute-start = (bf16[48,256]{1,0:T(8,128)(2,1)S(1)}, bf16[48,256]{1,0:T(8,128)(2,1)S(1)}, u32[]{:S(2)}, u32[]{:S(2)}) collective-permute-start(bf16[48,256]{1,0:T(8,128)(2,1)S(1)} %rims.1), channel_id=1, source_target_pairs={{0,4},{4,8},{8,12},{12,16},{16,20},{20,24},{24,28},{28,32},{32,36}... | collective-permute-start | bytes 73736 | tf_op jit(solution)/shard_map/ppermute | solution.py:305
  10.3 15.3 %all-to-all-start = ((bf16[16,16,256]{2,1,0:T(8,128)(2,1)}), bf16[16,16,256]{2,1,0:T(8,128)(2,1)S(1)}, u32[]{:S(2)}, u32[]{:S(2)}) async-start(bf16[16,16,256]{2,1,0:T(8,128)(2,1)} %get-tuple-element.30), calls=%async_computation | async-start | bytes 262144 | tf_op jit(solution)/shard_map/all_to_all | solution.py:349
  16.5 20.0 %collective-permute-start.1 = (bf16[256,1024]{1,0:T(8,128)(2,1)S(1)}, bf16[256,1024]{1,0:T(8,128)(2,1)S(1)}, u32[]{:S(2)}, u32[]{:S(2)}) collective-permute-start(bf16[256,1024]{1,0:T(8,128)(2,1)S(1)} %get-tuple-element.45), channel_id=1, source_target_pairs={{0,1},{1,2},{2,3},{3,0},{4,7},{5,4},{6,5},{7,6},{8,9},{9,10},{10,1... | collective-permute-start | bytes 1572872 | tf_op jit(solution)/shard_map/ppermute | solution.py:332
  20.8 17.6 %collective-permute-start.3 = (bf16[128,1024]{1,0:T(8,128)(2,1)S(1)}, bf16[128,1024]{1,0:T(8,128)(2,1)S(1)}, u32[]{:S(2)}, u32[]{:S(2)}) collective-permute-start(bf16[128,1024]{1,0:T(8,128)(2,1)S(1)} %get-tuple-element.46), channel_id=1, source_target_pairs={{0,2},{1,3},{2,0},{3,1},{4,6},{5,7},{6,4},{7,5},{8,10},{9,11},{10,... | collective-permute-start | bytes 786440 | tf_op jit(solution)/shard_map/ppermute | solution.py:337
  27.2 16.7 %all-to-all-start.1 = ((bf16[8,16,256]{2,1,0:T(8,128)(2,1)}), bf16[8,16,256]{2,1,0:T(8,128)(2,1)S(1)}, u32[]{:S(2)}, u32[]{:S(2)}) async-start(bf16[8,16,256]{2,1,0:T(8,128)(2,1)} %get-tuple-element.40), calls=%async_computation.1 | async-start | bytes 131072 | tf_op jit(solution)/shard_map/all_to_all | solution.py:371
  36.5 16.9 %collective-permute-start.2 = (bf16[256,1024]{1,0:T(8,128)(2,1)S(1)}, bf16[256,1024]{1,0:T(8,128)(2,1)S(1)}, u32[]{:S(2)}, u32[]{:S(2)}) collective-permute-start(bf16[256,1024]{1,0:T(8,128)(2,1)S(1)} %collective-permute-done.1.rest_0_), channel_id=1, source_target_pairs={{0,4},{4,0},{1,5},{5,1},{2,6},{6,2},{3,7},{7,3},{8,12},{12,8},{9,1... | collective-permute-start | bytes 1572872 | tf_op jit(solution)/shard_map/ppermute | solution.py:372
  38.4 15.0 %collective-permute-start.4 = (bf16[128,1024]{1,0:T(8,128)(2,1)S(1)}, bf16[128,1024]{1,0:T(8,128)(2,1)S(1)}, u32[]{:S(2)}, u32[]{:S(2)}) collective-permute-start(bf16[128,1024]{1,0:T(8,128)(2,1)S(1)} %collective-permute-done.3.rest_2_), channel_id=1, source_target_pairs={{0,4},{4,0},{1,5},{5,1},{2,6},{6,2},{3,7},{7,3},{8,12},{12,8},{9,1... | collective-permute-start | bytes 786440 | tf_op jit(solution)/shard_map/ppermute | solution.py:372
